TPU v7x, 32 devices: a whole 2x2x4 slice. The times are simulated.
32 devices in a mesh: img: 2 (over x), row: 4 (over z), col: 4 (over y, core).
Axes of the slice: x: 2, y: 2, z: 4, core: 2. Of those that a mesh axis runs over, the one named last changes fastest.
Arguments:
- tokens: bfloat16 [8, 32, 32, 1152], P('img', 'row', 'col'), may hold values from -6 to 6
- condition: bfloat16 [8, 1152], P('img'), may hold values from -6 to 6
- valid: int32 [8], P('img'), may hold values from 0 to 1, as said below
- positions: int32 [2, 8, 32, 32], P(None, 'img', 'row', 'col'), may hold values from 0 to 93, as said below
- w_qkv: bfloat16 [1152, 3456], P('img'), may hold values from -0.1875 to 0.1875
- w_out: bfloat16 [1152, 1152], P('img'), may hold values from -1.5 to 1.5
- w_up: bfloat16 [1152, 6144], P('img'), may hold values from -0.1875 to 0.1875
- w_down: bfloat16 [3072, 1152], P('img'), may hold values from -0.109375 to 0.109375
- w_ada: bfloat16 [1152, 6912], P(None, ('row', 'col')), may hold values from -0.25 to 0.25
- qk_gain: float32 [2, 72], replicated, may hold values from 0.1 to 1.9
- cotangent: bfloat16 [8, 32, 32, 1152], P('img', 'row', 'col'), may hold values from -6 to 6
Outputs:
- output: bfloat16 [8, 32, 32, 1152], P('img', 'row', 'col')
- grad_tokens: float32 [8, 32, 32, 1152], P('img', 'row', 'col')
- grad_condition: float32 [8, 1152], P('img')
- grad_w_qkv: float32 [1152, 3456], P('img')
- grad_w_out: float32 [1152, 1152], P('img')
- grad_w_up: float32 [1152, 6144], P('img')
- grad_w_down: float32 [3072, 1152], P('img')
- grad_w_ada: float32 [1152, 6912], P(None, ('row', 'col'))
- grad_qk_gain: float32 [2, 72], replicated
Inputs may be any that keep to these rules, and one draw needn't show every extreme that they name: Of the 4 images that one index of img holds, 1 to 4 are valid; some group has all 4 valid. `positions`: each image has a stride of 1 to 3 for rows and one for columns; a patch's row position is its row index times the row stride, its column position its column index times the column stride. Some image has stride 3 along each.
All inputs are finite; a program needn't handle non-finite values.
Results may differ from a plain program's by a relative error of at most 0.018.
Values may be sent and summed in bfloat16 or wider, within the bound.
No kernel may reach another device: no remote copies, remote signals or barrier semaphores. Data moves between devices by JAX's collectives and lax.ppermute only.
A program may use at most 256 MiB of HBM per device.

v0:
```python
import math

import jax
import jax.numpy as jnp
from jax import lax
from jax.sharding import PartitionSpec as P

epsilon = 1e-06


def rms_norm(values):
    return values * lax.rsqrt(jnp.mean(values * values, axis=-1, keepdims=True) + epsilon)


def modulate(values, offset, stretch):
    return rms_norm(values) * (1.0 + stretch[:, None, :]) + offset[:, None, :]


def swiglu(gate_up):
    half_width = gate_up.shape[-1] // 2
    return jax.nn.silu(gate_up[..., :half_width]) * gate_up[..., half_width:]


def tables(positions, pair_count):
    frequency = jnp.exp(-math.log(10000.0) * jnp.arange(pair_count, dtype=jnp.float32) / pair_count)
    angles = jnp.moveaxis(positions.astype(jnp.float32)[..., None] * frequency, 0, -2)
    return (jnp.cos(angles), jnp.sin(angles))


def rotate(vectors, cos_table, sin_table):
    pair_count = vectors.shape[-1] // 4
    shaped = vectors.reshape(vectors.shape[:-1] + (2, 2, pair_count))
    leading = shaped[..., 0, :]
    trailing = shaped[..., 1, :]
    turned = jnp.stack(
        [leading * cos_table - trailing * sin_table, leading * sin_table + trailing * cos_table],
        axis=-2,
    )
    return turned.reshape(vectors.shape)


def prepare(joined_pair, qk_gain, cos_table, sin_table):
    normed = rms_norm(joined_pair) * qk_gain[:, None, :]
    return rotate(normed, cos_table, sin_table)


def attend_image(query_rows, key_rows, value_rows):
    factor = query_rows.shape[-1] ** (-0.5)
    scores = (
        jnp.einsum("qhe,khe->hqk", query_rows, key_rows, preferred_element_type=jnp.float32)
        * factor
    )
    row_peak = jnp.max(scores, axis=-1, keepdims=True)
    exp_scores = jnp.exp(scores - row_peak)
    row_total = jnp.sum(exp_scores, axis=-1, keepdims=True)
    probability = (exp_scores / row_total).astype(jnp.bfloat16)
    mixed_rows = jnp.einsum(
        "hqk,khe->qhe", probability, value_rows, preferred_element_type=jnp.float32
    )
    return (mixed_rows, row_peak + jnp.log(row_total))


def attend(query_rows, key_rows, value_rows):

    def one_image(parts):
        return attend_image(parts[0], parts[1], parts[2])

    return lax.map(one_image, (query_rows, key_rows, value_rows))


def attend_back_image(query_rows, key_rows, value_rows, log_total, grad_rows):
    factor = query_rows.shape[-1] ** (-0.5)
    scores = (
        jnp.einsum("qhe,khe->hqk", query_rows, key_rows, preferred_element_type=jnp.float32)
        * factor
    )
    probability = jnp.exp(scores - log_total)
    grad_probs = jnp.einsum(
        "qhe,khe->hqk", grad_rows, value_rows, preferred_element_type=jnp.float32
    )
    inner_sum = jnp.sum(probability * grad_probs, axis=-1, keepdims=True)
    grad_scores = (probability * (grad_probs - inner_sum)).astype(jnp.bfloat16)
    grad_query = (
        jnp.einsum("hqk,khe->qhe", grad_scores, key_rows, preferred_element_type=jnp.float32)
        * factor
    )
    grad_key = (
        jnp.einsum("hqk,qhe->khe", grad_scores, query_rows, preferred_element_type=jnp.float32)
        * factor
    )
    grad_value = jnp.einsum(
        "hqk,qhe->khe",
        probability.astype(jnp.bfloat16),
        grad_rows,
        preferred_element_type=jnp.float32,
    )
    return (grad_query, grad_key, grad_value)


def attend_back(query_rows, key_rows, value_rows, log_total, grad_rows):

    def one_image(parts):
        return attend_back_image(parts[0], parts[1], parts[2], parts[3], parts[4])

    return lax.map(one_image, (query_rows, key_rows, value_rows, log_total, grad_rows))


def shards(
    tokens, condition, valid, positions, w_qkv, w_out, w_up, w_down, w_ada, qk_gain, cotangent
):
    image_count, tile_rows, tile_cols, model_width = tokens.shape
    tile_count = tile_rows * tile_cols
    flat_rows = image_count * tile_count
    head_dim = qk_gain.shape[1]
    head_count = model_width // head_dim
    residual = tokens.reshape(image_count, tile_count, model_width).astype(jnp.float32)
    cos_table, sin_table = tables(positions.reshape(2, image_count, tile_count), head_dim // 4)
    cos_qk = cos_table[:, :, None, None]
    sin_qk = sin_table[:, :, None, None]
    full_qkv, full_out, full_up, full_down = (
        lax.all_gather(w_qkv, "img", axis=0, tiled=True),
        lax.all_gather(w_out, "img", axis=0, tiled=True),
        lax.all_gather(w_up, "img", axis=0, tiled=True),
        lax.all_gather(w_down, "img", axis=0, tiled=True),
    )
    cond_float = condition.astype(jnp.float32)
    silu_cond = jax.nn.silu(cond_float).astype(jnp.bfloat16)
    mod_columns = jnp.dot(silu_cond, w_ada, preferred_element_type=jnp.float32)
    modulation = lax.all_gather(mod_columns, ("row", "col"), axis=1, tiled=True)
    offset_one, stretch_one, gate_one, offset_two, stretch_two, gate_two = jnp.split(
        modulation, 6, axis=1
    )
    valid_float = valid.astype(jnp.float32)[:, None]
    gate_attn = gate_one * valid_float
    gate_mlp = gate_two * valid_float
    attn_in, attn_back = jax.vjp(modulate, residual, offset_one, stretch_one)
    attn_rows = attn_in.astype(jnp.bfloat16).reshape(flat_rows, model_width)
    joined = jnp.dot(attn_rows, full_qkv, preferred_element_type=jnp.float32)
    joined = joined.reshape(image_count, tile_count, 3, head_count, head_dim)

    def qk_local(joined_pair, gains):
        return prepare(joined_pair, gains, cos_qk, sin_qk)

    rotated, rotate_back = jax.vjp(qk_local, joined[:, :, :2], qk_gain)
    query_rows = rotated[:, :, 0].astype(jnp.bfloat16).reshape(image_count, tile_count, model_width)
    key_rows = rotated[:, :, 1].astype(jnp.bfloat16).reshape(image_count, tile_count, model_width)
    value_rows = joined[:, :, 2].astype(jnp.bfloat16).reshape(image_count, tile_count, model_width)
    all_keys, all_values = (
        lax.all_gather(key_rows, ("row", "col"), axis=1, tiled=True),
        lax.all_gather(value_rows, ("row", "col"), axis=1, tiled=True),
    )
    kept_query = query_rows.reshape(image_count, tile_count, head_count, head_dim)
    kept_key = all_keys.reshape(image_count, -1, head_count, head_dim)
    kept_value = all_values.reshape(image_count, -1, head_count, head_dim)
    mixed_rows, log_total = attend(kept_query, kept_key, kept_value)
    mixed_low = mixed_rows.astype(jnp.bfloat16).reshape(image_count, tile_count, model_width)
    mixed_flat = mixed_low.reshape(flat_rows, model_width)
    branch = jnp.dot(mixed_flat, full_out, preferred_element_type=jnp.float32).reshape(
        image_count, tile_count, model_width
    )
    hidden_res = residual + gate_attn[:, None, :] * branch
    mlp_in, mlp_back = jax.vjp(modulate, hidden_res, offset_two, stretch_two)
    mlp_rows = mlp_in.astype(jnp.bfloat16).reshape(flat_rows, model_width)
    gate_up = jnp.dot(mlp_rows, full_up, preferred_element_type=jnp.float32)
    activated, swiglu_back = jax.vjp(swiglu, gate_up)
    act_rows = activated.astype(jnp.bfloat16)
    mlp_out = jnp.dot(act_rows, full_down, preferred_element_type=jnp.float32).reshape(
        image_count, tile_count, model_width
    )
    output = (hidden_res + gate_mlp[:, None, :] * mlp_out).astype(jnp.bfloat16)
    output = output.reshape(image_count, tile_rows, tile_cols, model_width)
    grad_out = cotangent.reshape(image_count, tile_count, model_width).astype(jnp.float32)
    grad_mlp = (
        (gate_mlp[:, None, :] * grad_out).astype(jnp.bfloat16).reshape(flat_rows, model_width)
    )
    grad_gate_mlp = valid_float * jnp.sum(grad_out * mlp_out, axis=1)
    grad_down = jnp.einsum("nf,nd->fd", act_rows, grad_mlp, preferred_element_type=jnp.float32)
    grad_act = jnp.einsum("nd,fd->nf", grad_mlp, full_down, preferred_element_type=jnp.float32)
    grad_gate_up = swiglu_back(grad_act)[0].astype(jnp.bfloat16)
    grad_up = jnp.einsum("nd,nf->df", mlp_rows, grad_gate_up, preferred_element_type=jnp.float32)
    grad_mlp_in = jnp.einsum("nf,df->nd", grad_gate_up, full_up, preferred_element_type=jnp.float32)
    grad_hidden_part, grad_offset_two, grad_stretch_two = mlp_back(
        grad_mlp_in.reshape(image_count, tile_count, model_width)
    )
    grad_hidden = grad_out + grad_hidden_part
    grad_branch = (
        (gate_attn[:, None, :] * grad_hidden).astype(jnp.bfloat16).reshape(flat_rows, model_width)
    )
    grad_gate_attn = valid_float * jnp.sum(grad_hidden * branch, axis=1)
    grad_wout = jnp.einsum("nd,ne->de", mixed_flat, grad_branch, preferred_element_type=jnp.float32)
    grad_mixed = jnp.einsum("ne,de->nd", grad_branch, full_out, preferred_element_type=jnp.float32)
    grad_mixed = grad_mixed.astype(jnp.bfloat16).reshape(image_count, tile_count, model_width)
    grad_heads = grad_mixed.reshape(image_count, tile_count, head_count, head_dim)
    grad_query, grad_key, grad_value = attend_back(
        kept_query, kept_key, kept_value, log_total, grad_heads
    )
    key_flat = grad_key.reshape(image_count, -1, model_width)
    value_flat = grad_value.reshape(image_count, -1, model_width)
    grad_key, grad_value = (
        lax.psum_scatter(
            key_flat.astype(jnp.bfloat16), ("row", "col"), scatter_dimension=1, tiled=True
        ).astype(jnp.float32),
        lax.psum_scatter(
            value_flat.astype(jnp.bfloat16), ("row", "col"), scatter_dimension=1, tiled=True
        ).astype(jnp.float32),
    )
    grad_rotated = jnp.stack(
        [grad_query, grad_key.reshape(image_count, tile_count, head_count, head_dim)], axis=2
    )
    grad_pair, grad_gain = rotate_back(grad_rotated)
    grad_joined = jnp.concatenate(
        [grad_pair, grad_value.reshape(image_count, tile_count, 1, head_count, head_dim)], axis=2
    )
    grad_joined = grad_joined.astype(jnp.bfloat16).reshape(flat_rows, 3 * model_width)
    grad_wqkv = jnp.einsum("nd,ne->de", attn_rows, grad_joined, preferred_element_type=jnp.float32)
    grad_attn_in = jnp.einsum(
        "ne,de->nd", grad_joined, full_qkv, preferred_element_type=jnp.float32
    )
    grad_resid_part, grad_offset_one, grad_stretch_one = attn_back(
        grad_attn_in.reshape(image_count, tile_count, model_width)
    )
    grad_tokens = (grad_hidden + grad_resid_part).reshape(
        image_count, tile_rows, tile_cols, model_width
    )
    grad_mod = jnp.concatenate(
        [
            grad_offset_one,
            grad_stretch_one,
            grad_gate_attn,
            grad_offset_two,
            grad_stretch_two,
            grad_gate_mlp,
        ],
        axis=1,
    )
    mod_share = lax.psum_scatter(
        grad_mod.astype(jnp.bfloat16), ("row", "col"), scatter_dimension=1, tiled=True
    )
    grad_ada_part = jnp.einsum(
        "bd,be->de", silu_cond, mod_share, preferred_element_type=jnp.float32
    )
    grad_silu_part = jnp.einsum("be,de->bd", mod_share, w_ada, preferred_element_type=jnp.float32)
    grad_silu, gain_partial = lax.psum((grad_silu_part, grad_gain), ("row", "col"))
    grad_condition = jax.vjp(jax.nn.silu, cond_float)[1](grad_silu)[0]
    shard_qkv, shard_out, shard_up, shard_down = (
        lax.psum_scatter(
            grad_wqkv.astype(jnp.bfloat16), "img", scatter_dimension=0, tiled=True
        ).astype(jnp.float32),
        lax.psum_scatter(
            grad_wout.astype(jnp.bfloat16), "img", scatter_dimension=0, tiled=True
        ).astype(jnp.float32),
        lax.psum_scatter(
            grad_up.astype(jnp.bfloat16), "img", scatter_dimension=0, tiled=True
        ).astype(jnp.float32),
        lax.psum_scatter(
            grad_down.astype(jnp.bfloat16), "img", scatter_dimension=0, tiled=True
        ).astype(jnp.float32),
    )
    sum_qkv, sum_out, sum_up, sum_down = (
        lax.psum(shard_qkv.astype(jnp.bfloat16), ("row", "col")).astype(jnp.float32),
        lax.psum(shard_out.astype(jnp.bfloat16), ("row", "col")).astype(jnp.float32),
        lax.psum(shard_up.astype(jnp.bfloat16), ("row", "col")).astype(jnp.float32),
        lax.psum(shard_down.astype(jnp.bfloat16), ("row", "col")).astype(jnp.float32),
    )
    grad_ada, grad_gains = (
        lax.psum(grad_ada_part.astype(jnp.bfloat16), "img").astype(jnp.float32),
        lax.psum(gain_partial.astype(jnp.bfloat16), "img").astype(jnp.float32),
    )
    return (
        output,
        grad_tokens,
        grad_condition,
        sum_qkv,
        sum_out,
        sum_up,
        sum_down,
        grad_ada,
        grad_gains,
    )


def solution(mesh):
    placed = (
        P("img", "row", "col", None),
        P("img", None),
        P("img"),
        P(None, "img", "row", "col"),
        P("img", None),
        P("img", None),
        P("img", None),
        P("img", None),
        P(None, ("row", "col")),
        P(),
        P("img", "row", "col", None),
    )
    return jax.shard_map(
        shards,
        mesh=mesh,
        in_specs=placed,
        out_specs=(
            P("img", "row", "col", None),
            P("img", "row", "col", None),
            P("img", None),
            P("img", None),
            P("img", None),
            P("img", None),
            P("img", None),
            P(None, ("row", "col")),
            P(),
        ),
        check_vma=False,
    )
```

profile of v0, /device:TPU:0, one launch (start us, length us, event | category | flops | bytes accessed | tf_op | source)
XLA Modules:
  0.0 1865.0 jit_solution(16265726678782862753)
XLA Ops:
  8.8 23.4 %all-gather = f32[16,432,4]{1,2,0:T(4,128)S(1)} all-gather(f32[1,432,4]{1,2,0:T(4,128)S(1)} %convolution_bitcast_fusion), channel_id=1, replica_groups=mesh['img'=2,'row'=4,'col'=4] {'row','col'}, dimensions={0}, use_global_device_ids=true | all-gather | bytes 117504 | tf_op jit(solution)/shard_map/all_gather | solution.py:129
  33.3 78.2 %all-gather.8.cloned.1.call-done = bf16[1152,3456]{1,0:T(8,128)(2,1)} async-done(((bf16[576,3456]{1,0:T(8,128)(2,1)}), bf16[1152,3456]{1,0:T(8,128)(2,1)}) %all-gather.8.cloned.1.call-update) | async-done | bytes 7962640 | tf_op jit(solution)/shard_map/all_gather | solution.py:121
  111.5 11.5 copy.122
  123.0 6.8 fusion.79
  165.7 51.5 %all-gather.10.cloned.1.call-done = bf16[4,1024,1152]{2,1,0:T(8,128)(2,1)} async-done(((bf16[4,64,1152]{2,1,0:T(8,128)(2,1)}), bf16[4,1024,1152]{2,1,0:T(8,128)(2,1)}) %all-gather.10.cloned.1.call-update) | async-done | bytes 9437200 | tf_op jit(solution)/shard_map/all_gather | solution.py:150
  217.2 12.6 copy.124
  229.9 69.9 %all-gather.12.cloned.1.call-done = bf16[4,1024,1152]{2,1,0:T(8,128)(2,1)} async-done(((bf16[4,64,1152]{2,1,0:T(8,128)(2,1)}), bf16[4,1024,1152]{2,1,0:T(8,128)(2,1)}) %all-gather.12.cloned.1.call-update) | async-done | bytes 9437200 | tf_op jit(solution)/shard_map/all_gather | solution.py:149
  299.7 12.7 copy.128
  312.5 25.8 %while.28 = (s32[]{:T(128)}, bf16[4,64,16,72]{3,1,2,0:T(8,128)(2,1)S(1)}, f32[4,16,64,1]{2,1,3,0:T(8,128)S(1)}, bf16[4,1024,16,72]{1,3,2,0:T(8,128)(2,1)}, bf16[...) while((s32[]{:T(128)}, bf16[4,64,16,72]{3,1,2,0:T(8,128)(2,1)S(1)}, ...), condition=%wide.region_5.6_spmd.clone, body=%wide.region_2.5_spmd.sunk.clone | while | flops 311426048 | bytes 18143312 | solution.py:68
  348.5 161.4 %all-gather.16.cloned.1.call-done = bf16[1152,6144]{1,0:T(8,128)(2,1)} async-done(((bf16[576,6144]{1,0:T(8,128)(2,1)}), bf16[1152,6144]{1,0:T(8,128)(2,1)}) %all-gather.16.cloned.1.call-update) | async-done | bytes 14155792 | tf_op jit(solution)/shard_map/all_gather | solution.py:123
  509.9 12.7 fusion.105
  522.6 78.0 %all-gather.18.cloned.1.call-done = bf16[3072,1152]{1,0:T(8,128)(2,1)} async-done(((bf16[1536,1152]{1,0:T(8,128)(2,1)}), bf16[3072,1152]{1,0:T(8,128)(2,1)}) %all-gather.18.cloned.1.call-update) | async-done | bytes 7077904 | tf_op jit(solution)/shard_map/all_gather | solution.py:124
  600.6 11.1 fusion.85
  611.6 12.3 fusion.84
  640.1 74.1 %while.29 = (s32[]{:T(128)}, f32[4,64,16,72]{3,1,2,0:T(8,128)}, bf16[4,1024,16,72]{1,3,2,0:T(8,128)(2,1)}, bf16[4,1024,16,72]{1,3,2,0:T(8,128)(2,1)}, bf16[4,102...) while((s32[]{:T(128)}, f32[4,64,16,72]{3,1,2,0:T(8,128)}, ...), condition=%wide.region_10.11_spmd.clone, body=%wide.region_8.10_spmd.sunk.clone | while | flops 768809984 | bytes 181882160 | solution.py:105
  714.2 15.4 copy.134
  729.7 12.7 copy.140
  749.8 164.8 %all-reduce.13.cloned.1.call-done = bf16[4,1024,1152]{2,0,1:T(4,128)(2,1)} async-done(((bf16[4,1024,1152]{2,0,1:T(4,128)(2,1)}), bf16[4,1024,1152]{2,0,1:T(4,128)(2,1)}) %all-reduce.13.cloned.1.call-update) | async-done | bytes 9437200
  941.4 89.9 %reduce-scatter.9.cloned.1.call-done = bf16[4,64,1152]{2,1,0:T(8,128)(2,1)} async-done(((bf16[4,1024,1152]{2,1,0:T(8,128)(2,1)}), bf16[4,64,1152]{2,1,0:T(8,128)(2,1)}) %reduce-scatter.9.cloned.1.call-update) | async-done | bytes 589840 | tf_op jit(solution)/shard_map/reduce_scatter | solution.py:203
  1040.9 6.6 convert_element_type.231
  1047.5 7.5 fusion.63
  1059.6 6.6 convolution_convert_fusion.2
  1067.3 12.2 convolution_convert_fusion
  1094.8 22.3 %reduce-scatter.19.cloned.1.call-done = bf16[432,4]{1,0:T(8,128)(2,1)} async-done(((bf16[6912,4]{1,0:T(8,128)(2,1)}), bf16[432,4]{1,0:T(8,128)(2,1)}) %reduce-scatter.19.cloned.1.call-update) | async-done | bytes 3472
  1119.4 37.2 %reduce-scatter.13.cloned.1.call-done = bf16[576,1152]{1,0:T(8,128)(2,1)} async-done(((bf16[1152,1152]{1,0:T(8,128)(2,1)}), bf16[576,1152]{1,0:T(8,128)(2,1)}) %reduce-scatter.13.cloned.1.call-update) | async-done | bytes 1327120 | tf_op jit(solution)/shard_map/reduce_scatter | solution.py:249
  1156.6 88.5 %reduce-scatter.17.cloned.1.call-done = bf16[1536,1152]{1,0:T(8,128)(2,1)} async-done(((bf16[3072,1152]{1,0:T(8,128)(2,1)}), bf16[1536,1152]{1,0:T(8,128)(2,1)}) %reduce-scatter.17.cloned.1.call-update) | async-done | bytes 3538960 | tf_op jit(solution)/shard_map/reduce_scatter | solution.py:255
  1245.2 164.3 %reduce-scatter.15.cloned.1.call-done = bf16[576,6144]{1,0:T(8,128)(2,1)} async-done(((bf16[1152,6144]{1,0:T(8,128)(2,1)}), bf16[576,6144]{1,0:T(8,128)(2,1)}) %reduce-scatter.15.cloned.1.call-update) | async-done | bytes 7077904 | tf_op jit(solution)/shard_map/reduce_scatter | solution.py:252
  1409.4 97.7 %reduce-scatter.11.cloned.1.call-done = bf16[576,3456]{1,0:T(8,128)(2,1)} async-done(((bf16[1152,3456]{1,0:T(8,128)(2,1)}), bf16[576,3456]{1,0:T(8,128)(2,1)}) %reduce-scatter.11.cloned.1.call-update) | async-done | bytes 3981328 | tf_op jit(solution)/shard_map/reduce_scatter | solution.py:246
  1508.3 61.5 %all-reduce.5 = (f32[4,1152]{1,0:T(4,128)S(1)}, bf16[2,72]{1,0:T(2,128)(2,1)S(1)}) all-reduce(f32[4,1152]{1,0:T(4,128)S(1)} %fusion.86, f32[2,72]{1,0:T(2,128)S(1)} %get-tuple-element.180), channel_id=1, replica_groups=mesh['img'=2,'row'=4,'col'=4] {'row','col'}, use_global_device_ids=true, to_apply=%region_22.23 | all-reduce | flops 4752 | bytes 37728 | tf_op jit(solution)/shard_map/psum | solution.py:243
  1578.6 260.9 %all-reduce.15.cloned.1.call-done = (bf16[576,3456]{1,0:T(8,128)(2,1)}, bf16[576,1152]{1,0:T(8,128)(2,1)}, bf16[576,6144]{1,0:T(8,128)(2,1)}, bf16[1536,1152]{1,0:T(8,128)(2,1)}) async-done(((bf16[576,3456]{1,0:T(8,128)(2,1)}, bf16[576,1152]{1,0:T(8,128)(2,1)}, bf16[576,6144]{1,0:T(8,128)(2,1)}, bf16[1536,1152]{1,0:T(8,128)(2,1)}), (bf16[576,3456]{1,0:T(8,128)(2,1)}, bf16[576,1152]{1,0:T(8,128)(2,1)}, ...) | async-done | bytes 15925264 | tf_op jit(solution)/shard_map/psum | solution.py:260
  1839.5 6.5 convert_element_type.236
  1847.6 7.2 convert_element_type.240
  (337 shorter events, 244.9 us)
Async XLA Ops:
  7.2 25.2 %copy-start.49 = (s32[4]{0:T(128)S(1)}, s32[4]{0:T(128)}, u32[]{:S(2)}) copy-start(s32[4]{0:T(128)} %param.17) | copy-start | bytes 52
  7.2 25.2 %copy-start.12 = (bf16[4,8,8,1152]{3,2,1,0:T(8,128)(2,1)S(1)}, bf16[4,8,8,1152]{3,2,1,0:T(8,128)(2,1)}, u32[]{:S(2)}) copy-start(bf16[4,8,8,1152]{3,2,1,0:T(8,128)(2,1)} %param.15) | copy-start | bytes 1769476
  7.2 104.3 %all-gather.8.cloned.1.call-start = ((), (), s32[]{:S(2)}) async-start(), calls=%async_computation.6 | async-start | bytes 11943936 | tf_op jit(solution)/shard_map/all_gather | solution.py:121
  8.0 209.3 %all-gather.10.cloned.1.call-start = ((), (), s32[]{:S(2)}) async-start(), calls=%async_computation.7 | async-start | bytes 10027008 | tf_op jit(solution)/shard_map/all_gather | solution.py:150
  32.4 90.6 %copy-start.47 = (f32[4]{0:T(128)}, f32[4]{0:T(128)S(1)}, u32[]{:S(2)}) copy-start(f32[4]{0:T(128)S(1)} %convert_element_type.205) | copy-start | bytes 52
  33.3 89.7 %copy-start.39 = (f32[4,1152]{1,0:T(4,128)}, f32[4,1152]{1,0:T(4,128)S(1)}, u32[]{:S(2)}) copy-start(f32[4,1152]{1,0:T(4,128)S(1)} %get-tuple-element.249) | copy-start | bytes 55300
  33.3 89.7 %copy-start.41 = (f32[4,1152]{1,0:T(4,128)}, f32[4,1152]{1,0:T(4,128)S(1)}, u32[]{:S(2)}) copy-start(f32[4,1152]{1,0:T(4,128)S(1)} %get-tuple-element.250) | copy-start | bytes 55300
  135.6 164.1 %all-gather.12.cloned.1.call-start = ((), (), s32[]{:S(2)}) async-start(), calls=%async_computation.8 | async-start | bytes 10027008 | tf_op jit(solution)/shard_map/all_gather | solution.py:149
  136.2 14.0 copy-start.30
  136.2 14.0 copy-start.32
  160.1 183.2 %all-gather.14.cloned.1.call-start = ((), (), s32[]{:S(2)}) async-start(), calls=%async_computation.9 | async-start | bytes 3981312 | tf_op jit(solution)/shard_map/all_gather | solution.py:122
  160.7 349.2 %all-gather.16.cloned.1.call-start = ((), (), s32[]{:S(2)}) async-start(), calls=%async_computation.10 | async-start | bytes 21233664 | tf_op jit(solution)/shard_map/all_gather | solution.py:123
  161.3 439.3 %all-gather.18.cloned.1.call-start = ((), (), s32[]{:S(2)}) async-start(), calls=%async_computation.11 | async-start | bytes 10616832 | tf_op jit(solution)/shard_map/all_gather | solution.py:124
  161.9 752.8 %all-reduce.13.cloned.1.call-start = ((), (), s32[]{:S(2)}) async-start(), calls=%async_computation.19 | async-start | bytes 18874368
  229.9 82.6 %copy-start.16 = (bf16[4,64,16,72]{3,1,2,0:T(8,128)(2,1)S(1)}, bf16[4,64,16,72]{3,1,2,0:T(8,128)(2,1)}, u32[]{:S(2)}) copy-start(bf16[4,64,16,72]{3,1,2,0:T(8,128)(2,1)} %broadcast_convert_fusion) | copy-start | bytes 1769476
  642.6 8.1 slice-start
  642.6 8.1 slice-start.1
  661.1 8.1 slice-start
  661.1 8.1 slice-start.1
  679.6 8.1 slice-start
  698.2 8.1 slice-start
  729.7 301.7 %reduce-scatter.9.cloned.1.call-start = ((), (), s32[]{:S(2)}) async-start(), calls=%async_computation.12 | async-start | bytes 10027008 | tf_op jit(solution)/shard_map/reduce_scatter | solution.py:203
  742.4 374.7 %reduce-scatter.19.cloned.1.call-start = ((), (), s32[]{:S(2)}) async-start(), calls=%async_computation.18 | async-start | bytes 1880064
  1057.0 99.7 %reduce-scatter.13.cloned.1.call-start = ((), (), s32[]{:S(2)}) async-start(), calls=%async_computation.14 | async-start | bytes 3981312 | tf_op jit(solution)/shard_map/reduce_scatter | solution.py:249
  1059.5 185.6 %reduce-scatter.17.cloned.1.call-start = ((), (), s32[]{:S(2)}) async-start(), calls=%async_computation.16 | async-start | bytes 10616832 | tf_op jit(solution)/shard_map/reduce_scatter | solution.py:255
  1066.3 343.2 %reduce-scatter.15.cloned.1.call-start = ((), (), s32[]{:S(2)}) async-start(), calls=%async_computation.15 | async-start | bytes 21233664 | tf_op jit(solution)/shard_map/reduce_scatter | solution.py:252
  1079.6 427.6 %reduce-scatter.11.cloned.1.call-start = ((), (), s32[]{:S(2)}) async-start(), calls=%async_computation.13 | async-start | bytes 11943936 | tf_op jit(solution)/shard_map/reduce_scatter | solution.py:246
  1094.7 22.4 %copy-start.38 = (bf16[4,1152]{1,0:T(4,128)(2,1)S(1)}, bf16[4,1152]{1,0:T(4,128)(2,1)}, u32[]{:S(2)}) copy-start(bf16[4,1152]{1,0:T(4,128)(2,1)} %param.16) | copy-start | bytes 27652
  1094.7 481.2 %all-reduce.11.cloned.1.call-start = ((), (), s32[]{:S(2)}) async-start(), calls=%async_computation.17 | async-start | bytes 1990656 | tf_op jit(solution)/shard_map/psum | solution.py:266
  1119.4 720.1 %all-reduce.15.cloned.1.call-start = ((), (), s32[]{:S(2)}) async-start(), calls=%async_computation.20 | async-start | bytes 31850496 | tf_op jit(solution)/shard_map/psum | solution.py:260
  1839.4 8.2 slice-start.6
  1839.5 8.2 slice-start.7
  (66 other events, 269.8 us)
Sparse Core Ops, SparseCore 0:
  9.6 101.8 all-gather.7
  135.7 81.4 all-gather.9
  220.1 79.5 all-gather.11
  301.1 37.5 all-gather.13
  340.1 169.7 all-gather.15
  511.3 89.2 all-gather.17
  729.8 184.7 all-reduce.12
  919.9 111.4 reduce-scatter.8
  1057.1 59.9 reduce-scatter.18
  1119.8 36.8 reduce-scatter.12
  1159.5 85.5 reduce-scatter.16
  1248.0 161.3 reduce-scatter.14
  1412.4 94.6 reduce-scatter.10
  1509.8 38.8 all-reduce.10
  1553.2 286.2 all-reduce.14
where the time goes:
time: 1880 us; the launch traced here: 1860 us
  waiting for transfers between devices  1370 us (73%)
  local copies, waits for them, and re-layouts  163 us (9%)
  matrix products  158 us (8%)
  blocking collectives  89.9 us (5%)
  other arithmetic  69.4 us (4%)
    psum x1, waiting for transfers between devices, shards(): lax.psum(shard_qkv.astype(jnp.bfloat16), ('row', 'col')).astype(jnp.float32)  261 us
    unnamed x17, waiting for transfers between devices  190 us
    reduce_scatter x1, waiting for transfers between devices, shards(): lax.psum_scatter(grad_up.astype(jnp.bfloat16), 'img', scatter_dimension=0...  164 us
    all_gather x1, waiting for transfers between devices, shards(): lax.all_gather(w_up, 'img', axis=0, tiled=True)  161 us
    reduce_scatter x1, waiting for transfers between devices, shards(): lax.psum_scatter(grad_wqkv.astype(jnp.bfloat16), 'img', scatter_dimension...  97.7 us
    reduce_scatter x1, waiting for transfers between devices, shards(): lax.psum_scatter(value_flat.astype(jnp.bfloat16), ('row', 'col'), scatter...  89.9 us
    reduce_scatter x1, waiting for transfers between devices, shards(): lax.psum_scatter(grad_down.astype(jnp.bfloat16), 'img', scatter_dimension...  88.5 us
    all_gather x1, waiting for transfers between devices, shards(): lax.all_gather(w_qkv, 'img', axis=0, tiled=True)  78.2 us
  transfers between devices with their start and end apart: 15, of which 13 were waited for; matrix products, arithmetic and copies ran while one was open for 10% of the time, Pallas kernels for 0%

commit v1 on v0

v1 whole, which is shorter than its diff:
```python
import functools
import math

import jax
import jax.numpy as jnp
from jax import lax
from jax.experimental import pallas as pl
from jax.experimental.pallas import tpu as pltpu
from jax.sharding import PartitionSpec as P

LANES=128
epsilon=1e-6

def lane_iota(shape):
    return lax.broadcasted_iota(jnp.int32, shape, len(shape)-1)

def turn(x, cos, sin_a, sin_b, shift):
    return x*cos + pltpu.roll(x, LANES-shift, 1)*sin_a + pltpu.roll(x, shift, 1)*sin_b

def attn_fwd_kernel(head_dim, pairs, scale, q_ref, k_ref, v_ref, cos_ref, sa_ref, sb_ref, gain_ref, o_ref, qa_ref, ka_ref, va_ref):
    tokens = q_ref.shape[0]
    cos, sa, sb = cos_ref[...], sa_ref[...], sb_ref[...]
    def normed(x):
        return x*lax.rsqrt(jnp.sum(x*x, axis=-1, keepdims=True)*(1.0/head_dim)+epsilon)
    q = turn(normed(q_ref[...])*gain_ref[0:1,:], cos, sa, sb, pairs)*scale
    k = turn(normed(k_ref[...])*gain_ref[1:2,:], cos, sa, sb, pairs)
    lane = lane_iota((tokens, LANES))
    extra = (lane==head_dim)|(lane==head_dim+1)
    ka_ref[...] = jnp.where(extra, 1.0, k).astype(jnp.bfloat16)
    va_ref[...] = jnp.where(extra, -1.0, v_ref[...]).astype(jnp.bfloat16)
    q_low = q.astype(jnp.bfloat16)
    rows = 256
    kk = ka_ref[...]
    vv = va_ref[...]
    for s in range(tokens//rows):
        qs = q_low[s*rows:(s+1)*rows]
        scores = lax.dot_general(qs, kk, (((1,),(1,)),((),())), preferred_element_type=jnp.float32)
        weights = jnp.exp2(scores).astype(jnp.bfloat16)
        out = jnp.dot(weights, vv, preferred_element_type=jnp.float32)
        total = -out[:, head_dim:head_dim+1]
        lane_s = lane[s*rows:(s+1)*rows]
        o_ref[s*rows:(s+1)*rows, :] = jnp.where(lane_s<head_dim, out*(1.0/total), 0.0).astype(jnp.bfloat16)
        lse = -jnp.log2(total)
        hi = lse.astype(jnp.bfloat16).astype(jnp.float32)
        lo = lse-hi
        qf = q[s*rows:(s+1)*rows]
        qf = jnp.where(lane_s==head_dim, hi, jnp.where(lane_s==head_dim+1, lo, qf))
        qa_ref[s*rows:(s+1)*rows, :] = qf.astype(jnp.bfloat16)

def attn_fwd(joined, cos, sa, sb, gain, head_dim):
    tokens, width = joined.shape
    heads = width//(3*LANES)
    scale = head_dim**-0.5*math.log2(math.e)
    blk = lambda off: pl.BlockSpec((tokens, LANES), lambda h: (0, off+h))
    full = pl.BlockSpec((tokens, LANES), lambda h: (0,0))
    outs = tuple(jax.ShapeDtypeStruct((tokens, heads*LANES), jnp.bfloat16) for _ in range(4))
    return pl.pallas_call(functools.partial(attn_fwd_kernel, head_dim, head_dim//4, scale),
        grid=(heads,), in_specs=[blk(0), blk(heads), blk(2*heads), full, full, full, pl.BlockSpec((2,LANES), lambda h:(0,0))],
        out_specs=tuple(blk(0) for _ in range(4)), out_shape=outs,
        compiler_params=pltpu.CompilerParams(vmem_limit_bytes=40*1024*1024),
        cost_estimate=pl.CostEstimate(flops=4*heads*tokens*tokens*LANES, bytes_accessed=10*1024*1024, transcendentals=heads*tokens*tokens),
        name="attn_fwd")(joined, joined, joined, cos, sa, sb, gain)

def attn_bwd_kernel(head_dim, pairs, scale, q_ref, k_ref, qa_ref, ka_ref, va_ref, o_ref, do_ref, cos_ref, sa_ref, sb_ref, gain_ref, gq_ref, gk_ref, gv_ref, gg_ref, dk_acc, dv_acc, dq_acc):
    tokens = q_ref.shape[0]
    h = pl.program_id(0)
    lane = lane_iota((tokens, LANES))
    do_f = do_ref[...].astype(jnp.float32)
    delta = jnp.sum(do_f*o_ref[...].astype(jnp.float32), axis=-1, keepdims=True)
    hi = delta.astype(jnp.bfloat16).astype(jnp.float32)
    lo = delta-hi
    do_a = jnp.where(lane==head_dim, hi, jnp.where(lane==head_dim+1, lo, do_f)).astype(jnp.bfloat16)
    qa = qa_ref[...]; ka = ka_ref[...]; va = va_ref[...]
    ka_t = ka.T
    cols = 256
    for s in range(tokens//cols):
        qs = qa[s*cols:(s+1)*cols]
        ds = do_a[s*cols:(s+1)*cols]
        st = lax.dot_general(ka, qs, (((1,),(1,)),((),())), preferred_element_type=jnp.float32)
        pt = jnp.exp2(st)
        dpt = lax.dot_general(va, ds, (((1,),(1,)),((),())), preferred_element_type=jnp.float32)
        dst = (pt*dpt).astype(jnp.bfloat16)
        ptl = pt.astype(jnp.bfloat16)
        dv = jnp.dot(ptl, ds, preferred_element_type=jnp.float32)
        dk = jnp.dot(dst, qs, preferred_element_type=jnp.float32)
        if s == 0:
            dv_acc[...] = dv; dk_acc[...] = dk
        else:
            dv_acc[...] += dv; dk_acc[...] += dk
        dq_acc[:, s*cols:(s+1)*cols] = jnp.dot(ka_t, dst, preferred_element_type=jnp.float32)
    inside = lane < head_dim
    cos, sa, sb = cos_ref[...], sa_ref[...], sb_ref[...]
    def back(g, x, gain):
        g = jnp.where(inside, g, 0.0)
        g = g*cos - pltpu.roll(g, LANES-pairs, 1)*sa - pltpu.roll(g, pairs, 1)*sb
        inv = lax.rsqrt(jnp.sum(x*x, axis=-1, keepdims=True)*(1.0/head_dim)+epsilon)
        n = x*inv
        gg = jnp.sum(g*n, axis=0, keepdims=True)
        g = g*gain
        return (g - n*(jnp.sum(g*n, axis=-1, keepdims=True)*(1.0/head_dim)))*inv, gg
    gq, ggq = back(dq_acc[...].T*(head_dim**-0.5), q_ref[...], gain_ref[0:1,:])
    gk, ggk = back(dk_acc[...]*math.log(2.0), k_ref[...], gain_ref[1:2,:])
    gq_ref[...] = gq.astype(jnp.bfloat16)
    gk_ref[...] = gk.astype(jnp.bfloat16)
    gv_ref[...] = jnp.where(inside, dv_acc[...], 0.0).astype(jnp.bfloat16)
    gg = jnp.concatenate([ggq, ggk], axis=0)
    @pl.when(h==0)
    def _(): gg_ref[...] = gg
    @pl.when(h>0)
    def _(): gg_ref[...] += gg

def attn_bwd(joined, qa, ka, va, o, do, cos, sa, sb, gain, head_dim):
    tokens, width = joined.shape
    heads = width//(3*LANES)
    blk = lambda off: pl.BlockSpec((tokens, LANES), lambda h: (0, off+h))
    full = pl.BlockSpec((tokens, LANES), lambda h: (0,0))
    small = pl.BlockSpec((2,LANES), lambda h:(0,0))
    o1 = jax.ShapeDtypeStruct((tokens, heads*LANES), jnp.bfloat16)
    return pl.pallas_call(functools.partial(attn_bwd_kernel, head_dim, head_dim//4, 0.0),
        grid=(heads,), in_specs=[blk(0), blk(heads), blk(0), blk(0), blk(0), blk(0), blk(0), full, full, full, small],
        out_specs=(blk(0), blk(0), blk(0), small), out_shape=(o1, o1, o1, jax.ShapeDtypeStruct((2,LANES), jnp.float32)),
        scratch_shapes=[pltpu.VMEM((tokens,LANES),jnp.float32), pltpu.VMEM((tokens,LANES),jnp.float32), pltpu.VMEM((LANES,tokens),jnp.float32)],
        compiler_params=pltpu.CompilerParams(vmem_limit_bytes=48*1024*1024),
        cost_estimate=pl.CostEstimate(flops=10*heads*tokens*tokens*LANES, bytes_accessed=14*1024*1024, transcendentals=heads*tokens*tokens),
        name="attn_bwd")(joined, joined, qa, ka, va, o, do, cos, sa, sb, gain)


def bits_of(size):
    return [1 << b for b in reversed(range(size.bit_length() - 1))]


def swap(value, axis, size, bit):
    return lax.ppermute(value, axis, [(a, a ^ bit) for a in range(size)])


def spread(value, axis, size):
    for bit in bits_of(size):
        value = jnp.concatenate([value, swap(value, axis, size, bit)], axis=0)
    return value


def gather_sum(value, axis, size):
    for bit in reversed(bits_of(size)):
        half = value.shape[0] // 2
        other = swap(value[half:].astype(jnp.bfloat16), axis, size, bit)
        value = value[:half].astype(jnp.float32) + other.astype(jnp.float32)
    return value


def block_order(size):
    order = [0]
    for bit in bits_of(size):
        order = order + [o ^ bit for o in order]
    return order


def scatter_rows(value, axis, size, me):
    pieces = [lax.dynamic_index_in_dim(value, me ^ k, 0, keepdims=True) for k in range(size)]
    return [pieces[0]] + [swap(pieces[k], axis, size, k) for k in range(1, size)]


def total(value, axis, size):
    for bit in reversed(bits_of(size)):
        value = value + swap(value, axis, size, bit)
    return value


def assemble_columns_kernel(parts, order_ref, x_ref, o_ref):
    count, _, rows, width = x_ref.shape
    piece = width // parts
    for dest in range(count):
        block = x_ref[order_ref[dest], 0].astype(jnp.float32)
        for p in range(parts):
            start = (p * count + dest) * piece
            o_ref[:, start : start + piece] = block[:, p * piece : (p + 1) * piece]


def assemble_columns(stacked, order, parts):
    count, tiles, rows, width = stacked.shape
    return pl.pallas_call(
        functools.partial(assemble_columns_kernel, parts),
        grid_spec=pltpu.PrefetchScalarGridSpec(
            num_scalar_prefetch=1,
            grid=(tiles,),
            in_specs=[pl.BlockSpec((count, 1, rows, width), lambda z, o: (0, o[count + z], 0, 0))],
            out_specs=pl.BlockSpec((rows, count * width), lambda z, o: (z, 0)),
        ),
        out_shape=jax.ShapeDtypeStruct((tiles * rows, count * width), jnp.float32),
        compiler_params=pltpu.CompilerParams(vmem_limit_bytes=40 * 1024 * 1024),
        cost_estimate=pl.CostEstimate(flops=0, bytes_accessed=6 * stacked.size, transcendentals=0),
        name="assemble_columns",
    )(order, stacked)


def assemble_rows_kernel(order_ref, x_ref, o_ref):
    _, tiles, rows, width = x_ref.shape
    length = o_ref.shape[0]
    for z in range(tiles):
        start = z * rows
        n = min(rows, length - start)
        o_ref[start : start + n] = x_ref[0, order_ref[z], :n].astype(jnp.float32)


def assemble_rows(stacked, order, length):
    count, tiles, rows, width = stacked.shape
    return pl.pallas_call(
        lambda o, x, y: assemble_rows_kernel(o.at[pl.ds(count, tiles)], x, y),
        grid_spec=pltpu.PrefetchScalarGridSpec(
            num_scalar_prefetch=1,
            grid=(count,),
            in_specs=[pl.BlockSpec((1, tiles, rows, width), lambda c, o: (o[c], 0, 0, 0))],
            out_specs=pl.BlockSpec((length, width), lambda c, o: (c, 0)),
        ),
        out_shape=jax.ShapeDtypeStruct((count * length, width), jnp.float32),
        compiler_params=pltpu.CompilerParams(vmem_limit_bytes=40 * 1024 * 1024),
        cost_estimate=pl.CostEstimate(flops=0, bytes_accessed=6 * stacked.size, transcendentals=0),
        name="assemble_rows",
    )(order, stacked)


def program(sizes, tokens, condition, valid, positions, w_qkv, w_out, w_up, w_down, w_ada, qk_gain, cotangent):
    n_img, n_row, n_col = sizes
    images, tile_rows, tile_cols, width = tokens.shape
    assert images == n_row
    tile = tile_rows * tile_cols
    head_dim = qk_gain.shape[1]
    pairs = head_dim // 4
    heads = width // head_dim
    my_heads = heads // n_col
    hidden = w_up.shape[1] // 2
    me_img, me_row, me_col = lax.axis_index("img"), lax.axis_index("row"), lax.axis_index("col")
    order_col, order_row = block_order(n_col), list(range(n_row))
    halves = 2
    low, wide = jnp.bfloat16, jnp.float32

    def dot(a, b, dims=((1,), (0,))):
        return lax.dot_general(a, b, (dims, ((), ())), preferred_element_type=jnp.float32)

    def to_image(array):
        flat = array.reshape(images, tile, width)
        own = jnp.concatenate([p[0] for p in scatter_rows(flat, "row", n_row, me_row)], axis=0)
        return spread(own, "col", n_col)

    def from_image(own):
        blocks = own.reshape(n_row, tile, width)
        got = [blocks[0]] + [swap(blocks[k], "row", n_row, k) for k in range(1, n_row)]
        stack = jnp.stack(got, axis=0)
        return jnp.concatenate(
            [lax.dynamic_index_in_dim(stack, me_row ^ b, 0, keepdims=True) for b in range(images)], axis=0
        ).reshape(images, tile_rows, tile_cols, width)

    def cut_columns(w, parts):
        piece = w.shape[1] // (parts * n_col)
        return jnp.concatenate(
            [
                lax.dynamic_slice_in_dim(w, (p * n_col + me_col) * piece, piece, axis=1)
                for p in range(parts)
            ],
            axis=1,
        )

    def whole_rows(part):
        if n_img == 2:
            other = swap(part, "img", 2, 1)
            return jnp.where(me_img == 0, jnp.concatenate([part, other], 0), jnp.concatenate([other, part], 0))
        return lax.all_gather(part, "img", axis=0, tiled=True)

    def cut_rows(w):
        if n_img == 2:
            length = w.shape[0] // n_col
            return whole_rows(lax.dynamic_slice_in_dim(w, me_col * length, length, axis=0))
        full = lax.all_gather(w, "img", axis=0, tiled=True)
        length = full.shape[0] // (halves * n_col)
        return jnp.concatenate(
            [
                lax.dynamic_slice_in_dim(full, (h * n_col + me_col) * length, length, axis=0)
                for h in range(halves)
            ],
            axis=0,
        )

    tok = to_image(tokens)
    my_qkv = whole_rows(cut_columns(w_qkv, 3 * halves))
    cond = condition.astype(wide)
    silu_cond = jax.nn.silu(cond).astype(low)
    mod_columns = dot(silu_cond, w_ada)
    my_out = cut_rows(w_out)
    my_up = whole_rows(cut_columns(w_up, 2 * halves))
    my_down = cut_rows(w_down)
    cot = to_image(cotangent)

    mod_span = mod_columns.shape[1]
    mod_rel = jnp.concatenate(scatter_rows(mod_columns, "row", n_row, me_row), axis=0)
    mod_rel = spread(mod_rel, "col", n_col)
    source = jnp.stack(
        [(me_row ^ k) * n_col + (me_col ^ j) for j in order_col for k in order_row]
    )
    pick = source[None, :] == jnp.arange(n_row * n_col)[:, None]
    modulation = jnp.sum(jnp.where(pick[:, :, None], mod_rel[None], 0.0), axis=1).reshape(6, width)
    offset_one, stretch_one, gate_one, offset_two, stretch_two, gate_two = [modulation[g : g + 1] for g in range(6)]
    live = lax.dynamic_index_in_dim(valid, me_row, 0, keepdims=False).astype(wide)
    gate_attn = gate_one * live
    gate_mlp = gate_two * live

    steps = lax.dynamic_index_in_dim(positions, me_row, 1, keepdims=False)
    step_row = (steps[0, 1, 0] - steps[0, 0, 0]).astype(wide)
    step_col = (steps[1, 0, 1] - steps[1, 0, 0]).astype(wide)
    frequency = jnp.exp(-math.log(10000.0) * jnp.arange(pairs, dtype=wide) / pairs)
    row_index = jnp.stack([(me_row ^ k) * tile_rows + jnp.arange(tile_rows) for k in order_row])
    col_index = jnp.stack([(me_col ^ j) * tile_cols + jnp.arange(tile_cols) for j in order_col])
    row_angle = (row_index.astype(wide) * step_row)[..., None] * frequency
    col_angle = (col_index.astype(wide) * step_col)[..., None] * frequency
    shape = (n_col, n_row, tile_rows, tile_cols, pairs)

    def over(rows_part, cols_part):
        none = jnp.zeros(shape[:-1] + (LANES - head_dim,), wide)
        rows_part = [jnp.broadcast_to(a[None, :, :, None, :], shape) for a in rows_part]
        cols_part = [jnp.broadcast_to(a[:, None, None, :, :], shape) for a in cols_part]
        return jnp.concatenate(rows_part + cols_part + [none], axis=-1).reshape(-1, LANES)

    cos_r, sin_r, cos_c, sin_c = jnp.cos(row_angle), jnp.sin(row_angle), jnp.cos(col_angle), jnp.sin(col_angle)
    cos_all = over([cos_r, cos_r], [cos_c, cos_c])
    sin_a = over([-sin_r, jnp.zeros_like(sin_r)], [-sin_c, jnp.zeros_like(sin_c)])
    sin_b = over([jnp.zeros_like(sin_r), sin_r], [jnp.zeros_like(sin_c), sin_c])
    gain = jnp.pad(qk_gain, ((0, 0), (0, LANES - head_dim)))

    qkv_wide = jnp.pad(
        my_qkv.reshape(width, 3 * my_heads, head_dim), ((0, 0), (0, 0), (0, LANES - head_dim))
    ).reshape(width, 3 * my_heads * LANES)
    out_wide = jnp.pad(
        my_out.reshape(my_heads, head_dim, width), ((0, 0), (0, LANES - head_dim), (0, 0))
    ).reshape(my_heads * LANES, width)

    def inverse(v):
        return lax.rsqrt(jnp.mean(v * v, axis=-1, keepdims=True) + epsilon)

    residual = tok.astype(wide)
    attn_in = (residual * inverse(residual) * (1.0 + stretch_one) + offset_one).astype(low)
    joined = dot(attn_in, qkv_wide)
    mixed, q_aug, k_aug, v_aug = attn_fwd(joined, cos_all, sin_a, sin_b, gain, head_dim)
    branch = gather_sum(dot(mixed, out_wide), "col", n_col)
    own = branch.shape[0]
    own_tok = residual[:own]
    hidden_res = own_tok + gate_attn * branch
    inv_two = inverse(hidden_res)
    mlp_own = (hidden_res * inv_two * (1.0 + stretch_two) + offset_two).astype(low)
    mlp_in = spread(mlp_own, "col", n_col)
    gate_up = dot(mlp_in, my_up)
    half = gate_up.shape[1] // 2
    gate, up = gate_up[:, :half], gate_up[:, half:]
    sig = 1.0 / (1.0 + jnp.exp(-gate))
    act = (gate * sig * up).astype(low)
    mlp_out = gather_sum(dot(act, my_down), "col", n_col)
    output = from_image((hidden_res + gate_mlp * mlp_out).astype(low))

    grad_mlp = (gate_mlp * cot.astype(wide)).astype(low)
    cot_own = cot[:own].astype(wide)
    sums = [None] * 6
    sums[5] = live * jnp.sum(cot_own * mlp_out, axis=0, keepdims=True)
    grad_act = dot(grad_mlp, my_down, ((1,), (1,)))
    grad_gu = jnp.concatenate(
        [grad_act * up * sig * (1.0 + gate * (1.0 - sig)), grad_act * (gate * sig)], axis=1
    ).astype(low)
    grad_mlp_in = gather_sum(dot(grad_gu, my_up, ((1,), (1,))), "col", n_col)
    g_down = dot(act, grad_mlp, ((0,), (0,)))
    g_up = dot(mlp_in, grad_gu, ((0,), (0,)))

    def norm_back(v, inv, stretch, g_y):
        normed = v * inv
        g = g_y * (1.0 + stretch)
        g_v = (g - normed * jnp.mean(g * normed, axis=-1, keepdims=True)) * inv
        return g_v, jnp.sum(g_y, axis=0, keepdims=True), jnp.sum(g_y * normed, axis=0, keepdims=True)

    g_v, sums[3], sums[4] = norm_back(hidden_res, inv_two, stretch_two, grad_mlp_in)
    grad_hidden = cot_own + g_v
    sums[2] = live * jnp.sum(grad_hidden * branch, axis=0, keepdims=True)
    grad_branch = spread((gate_attn * grad_hidden).astype(low), "col", n_col)
    grad_mixed = dot(grad_branch, out_wide, ((1,), (1,))).astype(low)
    g_out = dot(mixed, grad_branch, ((0,), (0,)))
    g_out = g_out.reshape(my_heads, LANES, width)[:, :head_dim].reshape(my_heads * head_dim, width)
    gq, gk, gv, g_gain = attn_bwd(joined, q_aug, k_aug, v_aug, mixed, grad_mixed, cos_all, sin_a, sin_b, gain, head_dim)
    grad_joined = jnp.concatenate([gq, gk, gv], axis=1)
    grad_attn_in = gather_sum(dot(grad_joined, qkv_wide, ((1,), (1,))), "col", n_col)
    g_qkv = dot(attn_in, grad_joined, ((0,), (0,)))
    g_qkv = g_qkv.reshape(width, 3 * my_heads, LANES)[:, :, :head_dim].reshape(width, 3 * my_heads * head_dim)
    g_v, sums[0], sums[1] = norm_back(own_tok, inverse(own_tok), stretch_one, grad_attn_in)
    grad_tokens = from_image((grad_hidden + g_v).astype(low)).astype(wide)

    order = jnp.stack(
        [sum(jnp.where((me_col ^ d) == j, p, 0) for p, j in enumerate(order_col)) for d in range(n_col)]
        + [me_row ^ z for z in range(n_row)]
    ).astype(jnp.int32)

    def reduce_parts(partial):
        rows = partial.shape[0] // 2
        low_part = partial.astype(low)
        mine = lax.dynamic_slice_in_dim(low_part, me_img * rows, rows, axis=0)
        theirs = lax.dynamic_slice_in_dim(low_part, (1 - me_img) * rows, rows, axis=0)
        other = swap(theirs, "img", 2, 1)
        summed = (mine.astype(wide) + other.astype(wide)).astype(low)
        block = -(-rows // (8 * n_row)) * 8
        summed = jnp.pad(summed, ((0, block * n_row - rows), (0, 0))).reshape(n_row, block, -1)
        got = scatter_rows(summed, "row", n_row, me_row)
        shard = sum(g.astype(wide) for g in got).astype(low)
        around = jnp.concatenate([shard] + [swap(shard, "row", n_row, k) for k in range(1, n_row)], axis=0)
        return spread(around[None], "col", n_col), rows

    if n_img == 2:
        stack_down, rows_down = reduce_parts(g_down)
        stack_up, _ = reduce_parts(g_up)
        stack_out, rows_out = reduce_parts(g_out)
        stack_qkv, _ = reduce_parts(g_qkv)
        sum_down = assemble_rows(stack_down, order, rows_down)
        sum_up = assemble_columns(stack_up, order, 2 * halves)
        sum_out = assemble_rows(stack_out, order, rows_out)
        sum_qkv = assemble_columns(stack_qkv, order, 3 * halves)
    else:

        def reduce_columns(partial, parts):
            summed = lax.psum_scatter(
                lax.psum(partial.astype(low), "row"), "img", scatter_dimension=0, tiled=True
            )
            wholes = lax.all_gather(summed, "col", axis=0)
            rows = wholes.shape[1]
            wholes = wholes.reshape(n_col, rows, parts, -1)
            return jnp.transpose(wholes, (1, 2, 0, 3)).reshape(rows, -1).astype(wide)

        def reduce_rows(partial):
            wholes = lax.all_gather(lax.psum(partial.astype(low), "row"), "col", axis=0)
            columns = wholes.shape[2]
            wholes = jnp.transpose(wholes.reshape(n_col, halves, -1, columns), (1, 0, 2, 3)).reshape(-1, columns)
            return lax.psum_scatter(wholes, "img", scatter_dimension=0, tiled=True).astype(wide)

        sum_down, sum_up = reduce_rows(g_down), reduce_columns(g_up, 2 * halves)
        sum_out, sum_qkv = reduce_rows(g_out), reduce_columns(g_qkv, 3 * halves)

    grad_mod = total(jnp.concatenate(sums, axis=0), "col", n_col).astype(low)
    blocks = grad_mod.reshape(n_row, n_col, mod_span)
    mine = lax.dynamic_index_in_dim(blocks, me_col, 1, keepdims=False)
    share_rel = jnp.concatenate(scatter_rows(mine, "row", n_row, me_row), axis=0)
    share = jnp.concatenate(
        [lax.dynamic_index_in_dim(share_rel, me_row ^ b, 0, keepdims=True) for b in range(images)], axis=0
    )
    if n_img == 2:
        pairs_of = [(silu_cond, share), (swap(silu_cond, "img", 2, 1), swap(share, "img", 2, 1))]
    else:
        pairs_of = [
            (lax.all_gather(silu_cond, "img", axis=0, tiled=True), lax.all_gather(share, "img", axis=0, tiled=True))
        ]
    grad_ada = sum(dot(a, b, ((0,), (0,))) for a, b in pairs_of)
    back = dot(share, w_ada, ((1,), (1,)))
    flat = jnp.concatenate([back.reshape(-1), g_gain[:, :head_dim].reshape(-1)]).reshape(1, -1)
    flat = total(total(flat, "row", n_row), "col", n_col)[0]
    grad_silu = flat[: images * width].reshape(images, width)
    gains = flat[images * width :].reshape(2, head_dim)
    if n_img == 2:
        gains = gains + swap(gains, "img", 2, 1)
    else:
        gains = lax.psum(gains, "img")
    s = 1.0 / (1.0 + jnp.exp(-cond))
    grad_condition = grad_silu * (s * (1.0 + cond * (1.0 - s)))
    return output, grad_tokens, grad_condition, sum_qkv, sum_out, sum_up, sum_down, grad_ada, gains


def solution(mesh):
    sizes = tuple(mesh.shape[name] for name in ("img", "row", "col"))
    placed = (
        P("img", "row", "col", None),
        P("img", None),
        P("img"),
        P(None, "img", "row", "col"),
        P("img", None),
        P("img", None),
        P("img", None),
        P("img", None),
        P(None, ("row", "col")),
        P(),
        P("img", "row", "col", None),
    )
    return jax.shard_map(
        functools.partial(program, sizes),
        mesh=mesh,
        in_specs=placed,
        out_specs=(
            P("img", "row", "col", None),
            P("img", "row", "col", None),
            P("img", None),
            P("img", None),
            P("img", None),
            P("img", None),
            P("img", None),
            P(None, ("row", "col")),
            P(),
        ),
        check_vma=False,
    )
```

time: 1880 us -> 666 us (0.35)
  waiting for transfers between devices: 1370 us -> 246 us
  starting transfers between devices: 1.29 us -> 116 us
  matrix products: 158 us -> 56.3 us
  blocking collectives: 89.9 us -> 0 us
  Pallas kernels: 0 us -> 49.4 us
  local copies, waits for them, and re-layouts: 163 us -> 122 us
    reduce_scatter x5 -> x0, waiting for transfers between devices: 478 us -> none  [the longest x1 164 us: shards(): lax.psum_scatter(grad_up.astype(jnp.bfloat16), 'img', scatter_dimension=0...]
    all_gather x6 -> x0, waiting for transfers between devices: 439 us -> none  [the longest x1 161 us: shards(): lax.all_gather(w_up, 'img', axis=0, tiled=True)]
    psum x2 -> x0, waiting for transfers between devices: 261 us -> none  [the longest x1 261 us: shards(): lax.psum(shard_qkv.astype(jnp.bfloat16), ('row', 'col')).astype(jnp.float32)]
    ppermute x0 -> x85, waiting for transfers between devices: none -> 246 us  [swap(): return lax.ppermute(value, axis, [(a, a ^ bit) for a in range(size)])]
    unnamed x17 -> x0, waiting for transfers between devices: 190 us -> none
    ppermute x0 -> x85, starting transfers between devices: none -> 116 us  [swap(): return lax.ppermute(value, axis, [(a, a ^ bit) for a in range(size)])]
    dot_general x43 -> x16, matrix products: 158 us -> 56.3 us  [dot(): lax.dot_general(a, b, (dims, ((), ())), preferred_element_type=jnp.float32)]
    psum x2 -> x0, blocking collectives: 66.4 us -> none  [the longest x1 61.5 us: shards(): lax.psum((grad_silu_part, grad_gain), ('row', 'col'))]
  transfers between devices with their start and end apart: 15 -> 85, of which waited for: 13 -> 29; matrix products, arithmetic and copies ran while one was open for 10% -> 32% of each run, Pallas kernels for 0% -> 5%
where the time goes in v1:
time: 666 us; the launch traced here: 660 us
  waiting for transfers between devices  246 us (37%)
  local copies, waits for them, and re-layouts  122 us (18%)
  starting transfers between devices  116 us (17%)
  other arithmetic  64.5 us (10%)
  matrix products  56.3 us (8%)
  Pallas kernels  49.4 us (7%)
    ppermute x85, waiting for transfers between devices, swap(): return lax.ppermute(value, axis, [(a, a ^ bit) for a in range(size)])  246 us
    ppermute x85, starting transfers between devices, swap(): return lax.ppermute(value, axis, [(a, a ^ bit) for a in range(size)])  116 us
    dot_general x16, matrix products, dot(): lax.dot_general(a, b, (dims, ((), ())), preferred_element_type=jnp.float32)  56.3 us
    unnamed x238, local copies, waits for them, and re-layouts  44.1 us
    pallas_call x1, Pallas kernels, attn_bwd(): pl.pallas_call(functools.partial(attn_bwd_kernel, head_dim, head_dim // 4...  19.6 us
    concatenate x10, other arithmetic, spread(): value = jnp.concatenate([value, swap(value, axis, size, bit)], axis=0)  17.5 us
  transfers between devices with their start and end apart: 85, of which 29 were waited for; matrix products, arithmetic and copies ran while one was open for 32% of the time, Pallas kernels for 5%

profile of v1, /device:TPU:0, one launch (start us, length us, event | category | flops | bytes accessed | tf_op | source)
XLA Modules:
  0.0 660.2 jit_solution(11295576456044570021)
XLA Ops:
  68.8 6.6 collective-permute-done.3
  127.6 12.1 %attn_fwd.1 = (bf16[1024,512]{1,0:T(8,128)(2,1)S(1)}, bf16[1024,512]{1,0:T(8,128)(2,1)S(1)}, bf16[1024,512]{1,0:T(8,128)(2,1)S(1)}, bf16[1024,512]{1,0:T(8,128)(2,1)S(1)}) custom-call(f32[1024,1536]{1,0:T(8,128)S(1)} %fusion.6.q_ref.k_ref.v_ref, f32[1024,1536]{1,0:T(8,128)S(1)} %fusion.6.q_ref.k_ref.v_ref, f32[1024,1536]{1,0:T(8,128)S(1)} %fusion.6.q_ref.k_ref.v_ref, ...), custom_call_target="tpu_custom_call" | custom-call | flops 2147483648 | bytes 10485760 | tf_op jit(solution)/shard_map/attn_fwd/pallas_call | solution.py:57
  168.0 19.8 %collective-permute-done.13 = bf16[256,1152]{1,0:T(8,128)(2,1)S(1)} collective-permute-done((bf16[256,1152]{1,0:T(8,128)(2,1)S(1)}, bf16[256,1152]{1,0:T(8,128)(2,1)S(1)}, u32[]{:S(2)}, u32[]{:S(2)}) %collective-permute-start.13) | collective-permute-done | bytes 589856 | tf_op jit(solution)/shard_map/ppermute | solution.py:133
  192.2 10.6 %collective-permute-done.14 = bf16[256,1152]{1,0:T(8,128)(2,1)S(1)} collective-permute-done((bf16[256,1152]{1,0:T(8,128)(2,1)S(1)}, bf16[256,1152]{1,0:T(8,128)(2,1)S(1)}, u32[]{:S(2)}, u32[]{:S(2)}) %collective-permute-start.14) | collective-permute-done | bytes 589856 | tf_op jit(solution)/shard_map/ppermute | solution.py:133
  210.3 6.9 %fusion.4 = f32[1024,1536]{1,0:T(8,128)S(1)} fusion(bf16[512,1152]{1,0:T(8,128)(2,1)} %collective-permute-done.15, bf16[256,1152]{1,0:T(8,128)(2,1)} %copy-done.59, bf16[256,1152]{1,0:T(8,128)(2,1)S(1)} %copy-done.45, bf16[576,1536]{1,0:T(8,128)(2,1)} %collective-permute-done.16, bf16[576,384]{1,0:T(8,128)(2,1)S(1)} %copy-done.53, ...), kind=kOutput, calls=%fused_computation.69 | convolution fusion | flops 3668115456 | bytes 12189697 | tf_op jit(solution)/shard_map/dot_general | solution.py:237
  217.3 10.1 %collective-permute-done.17 = bf16[384,1152]{1,0:T(8,128)(2,1)S(1)} collective-permute-done((bf16[384,1152]{1,0:T(8,128)(2,1)}, bf16[384,1152]{1,0:T(8,128)(2,1)S(1)}, u32[]{:S(2)}, u32[]{:S(2)}) %collective-permute-start.17) | collective-permute-done | bytes 884768 | tf_op jit(solution)/shard_map/ppermute | solution.py:133
  227.4 5.2 multiply_convert_fusion.2
  234.3 6.6 %fusion.2 = f32[1024,1152]{1,0:T(8,128)S(1)} fusion(bf16[1024,768]{1,0:T(8,128)(2,1)S(1)} %get-tuple-element.46, bf16[1024,768]{1,0:T(8,128)(2,1)S(1)} %get-tuple-element.45, bf16[576,1536]{1,0:T(8,128)(2,1)} %collective-permute-done.16, bf16[576,384]{1,0:T(8,128)(2,1)S(1)} %copy-done.53, bf16[576,384]{1,0:T(8,128)(2,1)S(1)} %copy-done.55, ...), kind=kOutput, calls=%fused_computation.33 | convolution fusion | flops 3667329024 | bytes 11403265 | tf_op jit(solution)/shard_map/dot_general | solution.py:237
  249.6 5.8 convolution_convert_fusion
  255.4 10.2 %collective-permute-done.73 = bf16[384,1152]{1,0:T(8,128)(2,1)S(1)} collective-permute-done((bf16[384,1152]{1,0:T(8,128)(2,1)S(1)}, bf16[384,1152]{1,0:T(8,128)(2,1)S(1)}, u32[]{:S(2)}, u32[]{:S(2)}) %collective-permute-start.73) | collective-permute-done | bytes 884768 | tf_op jit(solution)/shard_map/ppermute | solution.py:133
  279.5 9.6 %collective-permute-done.75 = bf16[1,96,1152]{2,1,0:T(8,128)(2,1)S(1)} collective-permute-done((bf16[1,96,1152]{2,1,0:T(8,128)(2,1)S(1)}, bf16[1,96,1152]{2,1,0:T(8,128)(2,1)S(1)}, u32[]{:S(2)}, u32[]{:S(2)}) %collective-permute-start.75) | collective-permute-done | bytes 221216 | tf_op jit(solution)/shard_map/ppermute | solution.py:133
  295.6 4.6 collective-permute-done.77
  301.6 9.8 %collective-permute-done.78 = bf16[1,96,1152]{2,1,0:T(8,128)(2,1)S(1)} collective-permute-done((bf16[1,96,1152]{2,1,0:T(8,128)(2,1)S(1)}, bf16[1,96,1152]{2,1,0:T(8,128)(2,1)S(1)}, u32[]{:S(2)}, u32[]{:S(2)}) %collective-permute-start.78) | collective-permute-done | bytes 221216 | tf_op jit(solution)/shard_map/ppermute | solution.py:133
  317.5 20.2 %collective-permute-done.64 = bf16[576,1536]{1,0:T(8,128)(2,1)S(1)} collective-permute-done((bf16[576,1536]{1,0:T(8,128)(2,1)S(1)}, bf16[576,1536]{1,0:T(8,128)(2,1)S(1)}, u32[]{:S(2)}, u32[]{:S(2)}) %collective-permute-start.64) | collective-permute-done | bytes 1769504 | tf_op jit(solution)/shard_map/ppermute | solution.py:133
  353.3 10.9 %collective-permute-done.65 = bf16[1,144,1536]{2,1,0:T(8,128)(2,1)S(1)} collective-permute-done((bf16[1,144,1536]{2,1,0:T(8,128)(2,1)S(1)}, bf16[1,144,1536]{2,1,0:T(8,128)(2,1)S(1)}, u32[]{:S(2)}, u32[]{:S(2)}) %collective-permute-start.65) | collective-permute-done | bytes 442400 | tf_op jit(solution)/shard_map/ppermute | solution.py:133
  364.2 16.7 %collective-permute-done.66 = bf16[1,144,1536]{2,1,0:T(8,128)(2,1)S(1)} collective-permute-done((bf16[1,144,1536]{2,1,0:T(8,128)(2,1)S(1)}, bf16[1,144,1536]{2,1,0:T(8,128)(2,1)S(1)}, u32[]{:S(2)}, u32[]{:S(2)}) %collective-permute-start.66) | collective-permute-done | bytes 442400 | tf_op jit(solution)/shard_map/ppermute | solution.py:133
  381.1 8.4 %collective-permute-start.68 = (bf16[1,144,1536]{2,1,0:T(8,128)(2,1)S(1)}, bf16[1,144,1536]{2,1,0:T(8,128)(2,1)S(1)}, u32[]{:S(2)}, u32[]{:S(2)}) collective-permute-start(bf16[1,144,1536]{2,1,0:T(8,128)(2,1)S(1)} %add_convert_fusion.7), channel_id=1, source_target_pairs={{0,4},{4,0},{8,12},{12,8},{1,5},{5,1},{9,13},{13,9},{2,6},{6,2},{1... | collective-permute-start | bytes 1327112 | tf_op jit(solution)/shard_map/ppermute | solution.py:133
  394.4 11.3 %collective-permute-done.68 = bf16[1,144,1536]{2,1,0:T(8,128)(2,1)S(1)} collective-permute-done((bf16[1,144,1536]{2,1,0:T(8,128)(2,1)S(1)}, bf16[1,144,1536]{2,1,0:T(8,128)(2,1)S(1)}, u32[]{:S(2)}, u32[]{:S(2)}) %collective-permute-start.68) | collective-permute-done | bytes 442400 | tf_op jit(solution)/shard_map/ppermute | solution.py:133
  405.6 16.8 %collective-permute-done.69 = bf16[1,144,1536]{2,1,0:T(8,128)(2,1)S(1)} collective-permute-done((bf16[1,144,1536]{2,1,0:T(8,128)(2,1)S(1)}, bf16[1,144,1536]{2,1,0:T(8,128)(2,1)S(1)}, u32[]{:S(2)}, u32[]{:S(2)}) %collective-permute-start.69) | collective-permute-done | bytes 442400 | tf_op jit(solution)/shard_map/ppermute | solution.py:133
  425.4 19.6 %attn_bwd.1 = (bf16[1024,512]{1,0:T(8,128)(2,1)S(1)}, bf16[1024,512]{1,0:T(8,128)(2,1)S(1)}, bf16[1024,512]{1,0:T(8,128)(2,1)S(1)}, f32[2,128]{1,0:T(2,128)S(1)}) custom-call(f32[1024,1536]{1,0:T(8,128)} %copy-done.2, f32[1024,1536]{1,0:T(8,128)} %copy-done.2, bf16[1024,512]{1,0:T(8,128)(2,1)S(1)} %copy-done.12, bf16[1024,512]{1,0:T(8,128)(2,1)} %copy-done.13, ...), custom_call_target="tpu_custom_call" | custom-call | flops 5368709120 | bytes 14680064 | tf_op jit(solution)/shard_map/attn_bwd/pallas_call | solution.py:119
  454.8 5.9 convolution_convert_fusion.1
  461.8 5.8 copy.75
  470.2 7.2 %collective-permute-start.56 = (bf16[1,40,1152]{2,1,0:T(8,128)(2,1)}, bf16[1,40,1152]{2,1,0:T(8,128)(2,1)}, u32[]{:S(2)}, u32[]{:S(2)}) collective-permute-start(bf16[1,40,1152]{2,1,0:T(8,128)(2,1)} %get-tuple-element.101), channel_id=1, source_target_pairs={{0,4},{4,0},{8,12},{12,8},{1,5},{5,1},{9,13},{13,9},{2,6},{6,2},{1... | collective-permute-start | bytes 276488 | tf_op jit(solution)/shard_map/ppermute | solution.py:133
  505.1 32.1 %collective-permute-done.62 = bf16[1,4,40,1152]{3,2,1,0:T(8,128)(2,1)S(1)} collective-permute-done((bf16[1,4,40,1152]{3,2,1,0:T(8,128)(2,1)S(1)}, bf16[1,4,40,1152]{3,2,1,0:T(8,128)(2,1)S(1)}, u32[]{:S(2)}, u32[]{:S(2)}) %collective-permute-start.62) | collective-permute-done | bytes 368672 | tf_op jit(solution)/shard_map/ppermute | solution.py:133
  541.3 7.5 %collective-permute-done.33 = bf16[256,1152]{1,0:T(8,128)(2,1)S(1)} collective-permute-done((bf16[256,1152]{1,0:T(8,128)(2,1)S(1)}, bf16[256,1152]{1,0:T(8,128)(2,1)S(1)}, u32[]{:S(2)}, u32[]{:S(2)}) %collective-permute-start.33) | collective-permute-done | bytes 589856 | tf_op jit(solution)/shard_map/ppermute | solution.py:133
  563.8 5.4 collective-permute-start.50
  571.7 7.7 %collective-permute-done.50 = bf16[1,144,864]{2,1,0:T(8,128)(2,1)S(1)} collective-permute-done((bf16[1,144,864]{2,1,0:T(8,128)(2,1)}, bf16[1,144,864]{2,1,0:T(8,128)(2,1)S(1)}, u32[]{:S(2)}, u32[]{:S(2)}) %collective-permute-start.50) | collective-permute-done | bytes 248864 | tf_op jit(solution)/shard_map/ppermute | solution.py:133
  579.4 11.2 %collective-permute-done.51 = bf16[1,144,864]{2,1,0:T(8,128)(2,1)S(1)} collective-permute-done((bf16[1,144,864]{2,1,0:T(8,128)(2,1)}, bf16[1,144,864]{2,1,0:T(8,128)(2,1)S(1)}, u32[]{:S(2)}, u32[]{:S(2)}) %collective-permute-start.51) | collective-permute-done | bytes 248864 | tf_op jit(solution)/shard_map/ppermute | solution.py:133
  621.5 6.3 collective-permute-start.34
  633.4 8.8 %collective-permute-done.35 = bf16[64,1152]{1,0:T(8,128)(2,1)S(1)} collective-permute-done((bf16[64,1152]{1,0:T(8,128)(2,1)S(1)}, bf16[64,1152]{1,0:T(8,128)(2,1)S(1)}, u32[]{:S(2)}, u32[]{:S(2)}) %collective-permute-start.35) | collective-permute-done | bytes 147488 | tf_op jit(solution)/shard_map/ppermute | solution.py:133
  647.0 6.2 assemble_columns.3
  655.0 5.0 assemble_columns.2
  (555 shorter events, 323.4 us)
Async XLA Ops:
  2.7 57.9 %collective-permute-start = (bf16[1,64,1152]{2,1,0:T(8,128)(2,1)}, bf16[1,64,1152]{2,1,0:T(8,128)(2,1)}, u32[]{:S(2)}, u32[]{:S(2)}) collective-permute-start(bf16[1,64,1152]{2,1,0:T(8,128)(2,1)} %get-tuple-element.100), channel_id=1, source_target_pairs={{0,4},{4,0},{8,12},{12,8},{1,5},{5,1},{9,13},{13,9},{2,6},{6,2},{1... | collective-permute-start | bytes 442376 | tf_op jit(solution)/shard_map/ppermute | solution.py:133
  5.7 56.5 %collective-permute-start.1 = (bf16[1,64,1152]{2,1,0:T(8,128)(2,1)}, bf16[1,64,1152]{2,1,0:T(8,128)(2,1)}, u32[]{:S(2)}, u32[]{:S(2)}) collective-permute-start(bf16[1,64,1152]{2,1,0:T(8,128)(2,1)} %get-tuple-element.99), channel_id=1, source_target_pairs={{0,8},{4,12},{8,0},{12,4},{1,9},{5,13},{9,1},{13,5},{2,10},{6,14},... | collective-permute-start | bytes 442376 | tf_op jit(solution)/shard_map/ppermute | solution.py:133
  8.3 53.9 %collective-permute-start.2 = (bf16[1,64,1152]{2,1,0:T(8,128)(2,1)}, bf16[1,64,1152]{2,1,0:T(8,128)(2,1)}, u32[]{:S(2)}, u32[]{:S(2)}) collective-permute-start(bf16[1,64,1152]{2,1,0:T(8,128)(2,1)} %get-tuple-element.98), channel_id=1, source_target_pairs={{0,12},{4,8},{8,4},{12,0},{1,13},{5,9},{9,5},{13,1},{2,14},{6,10},... | collective-permute-start | bytes 442376 | tf_op jit(solution)/shard_map/ppermute | solution.py:133
  10.5 42.4 %collective-permute-start.5 = (f32[1,432]{1,0:T(1,128)S(1)}, f32[1,432]{1,0:T(1,128)S(1)}, u32[]{:S(2)}, u32[]{:S(2)}) collective-permute-start(f32[1,432]{1,0:T(1,128)S(1)} %get-tuple-element.128), channel_id=1, source_target_pairs={{0,4},{4,0},{8,12},{12,8},{1,5},{5,1},{9,13},{13,9},{2,6},{6,2},{1... | collective-permute-start | bytes 5192 | tf_op jit(solution)/shard_map/ppermute | solution.py:133
  11.4 44.6 %collective-permute-start.6 = (f32[1,432]{1,0:T(1,128)}, f32[1,432]{1,0:T(1,128)S(1)}, u32[]{:S(2)}, u32[]{:S(2)}) collective-permute-start(f32[1,432]{1,0:T(1,128)} %get-tuple-element.127), channel_id=1, source_target_pairs={{0,8},{4,12},{8,0},{12,4},{1,9},{5,13},{9,1},{13,5},{2,10},{6,14},... | collective-permute-start | bytes 5192 | tf_op jit(solution)/shard_map/ppermute | solution.py:133
  56.0 56.9 %collective-permute-start.10 = (bf16[576,864]{1,0:T(8,128)(2,1)}, bf16[576,864]{1,0:T(8,128)(2,1)}, u32[]{:S(2)}, u32[]{:S(2)}) collective-permute-start(bf16[576,864]{1,0:T(8,128)(2,1)} %copy.70), channel_id=1, source_target_pairs={{0,16},{16,0},{1,17},{17,1},{2,18},{18,2},{3,19},{19,3},{4,20},{20... | collective-permute-start | bytes 2985992 | tf_op jit(solution)/shard_map/ppermute | solution.py:133
  58.4 51.7 %collective-permute-start.11 = (bf16[144,1152]{1,0:T(8,128)(2,1)}, bf16[144,1152]{1,0:T(8,128)(2,1)}, u32[]{:S(2)}, u32[]{:S(2)}) collective-permute-start(bf16[144,1152]{1,0:T(8,128)(2,1)} %constant_dynamic-slice_fusion.41), channel_id=1, source_target_pairs={{0,16},{16,0},{1,17},{17,1},{2,18},{18,2},{3,19},{19,3},{4,20},{20... | collective-permute-start | bytes 995336 | tf_op jit(solution)/shard_map/ppermute | solution.py:133
  76.5 42.9 %collective-permute-start.4 = (bf16[512,1152]{1,0:T(8,128)(2,1)}, bf16[512,1152]{1,0:T(8,128)(2,1)}, u32[]{:S(2)}, u32[]{:S(2)}) collective-permute-start(bf16[512,1152]{1,0:T(8,128)(2,1)} %get-tuple-element.96), channel_id=1, source_target_pairs={{0,1},{1,0},{2,3},{3,2},{4,5},{5,4},{6,7},{7,6},{8,9},{9,8},{10,11... | collective-permute-start | bytes 3538952 | tf_op jit(solution)/shard_map/ppermute | solution.py:133
  152.5 57.8 %collective-permute-start.16 = (bf16[576,1536]{1,0:T(8,128)(2,1)}, bf16[576,1536]{1,0:T(8,128)(2,1)}, u32[]{:S(2)}, u32[]{:S(2)}) collective-permute-start(bf16[576,1536]{1,0:T(8,128)(2,1)} %pad_maximum_fusion.10), channel_id=1, source_target_pairs={{0,16},{16,0},{1,17},{17,1},{2,18},{18,2},{3,19},{19,3},{4,20},{20... | collective-permute-start | bytes 5308424 | tf_op jit(solution)/shard_map/ppermute | solution.py:133
  160.6 30.6 %collective-permute-start.26 = (bf16[256,1152]{1,0:T(8,128)(2,1)S(1)}, bf16[256,1152]{1,0:T(8,128)(2,1)S(1)}, u32[]{:S(2)}, u32[]{:S(2)}) collective-permute-start(bf16[256,1152]{1,0:T(8,128)(2,1)S(1)} %pad_maximum_fusion.22), channel_id=1, source_target_pairs={{0,2},{1,3},{2,0},{3,1},{4,6},{5,7},{6,4},{7,5},{8,10},{9,11},{10,... | collective-permute-start | bytes 1769480 | tf_op jit(solution)/shard_map/ppermute | solution.py:133
  163.0 24.9 %collective-permute-start.13 = (bf16[256,1152]{1,0:T(8,128)(2,1)S(1)}, bf16[256,1152]{1,0:T(8,128)(2,1)S(1)}, u32[]{:S(2)}, u32[]{:S(2)}) collective-permute-start(bf16[256,1152]{1,0:T(8,128)(2,1)S(1)} %slice.317), channel_id=1, source_target_pairs={{0,2},{1,3},{2,0},{3,1},{4,6},{5,7},{6,4},{7,5},{8,10},{9,11},{10,... | collective-permute-start | bytes 1769480 | tf_op jit(solution)/shard_map/ppermute | solution.py:133
  241.0 31.7 %collective-permute-start.28 = (bf16[512,1152]{1,0:T(8,128)(2,1)S(1)}, bf16[512,1152]{1,0:T(8,128)(2,1)S(1)}, u32[]{:S(2)}, u32[]{:S(2)}) collective-permute-start(bf16[512,1152]{1,0:T(8,128)(2,1)S(1)} %slice.311), channel_id=1, source_target_pairs={{0,1},{1,0},{2,3},{3,2},{4,5},{5,4},{6,7},{7,6},{8,9},{9,8},{10,11... | collective-permute-start | bytes 3538952 | tf_op jit(solution)/shard_map/ppermute | solution.py:133
  273.0 39.1 %collective-permute-start.29 = (bf16[256,1152]{1,0:T(8,128)(2,1)S(1)}, bf16[256,1152]{1,0:T(8,128)(2,1)S(1)}, u32[]{:S(2)}, u32[]{:S(2)}) collective-permute-start(bf16[256,1152]{1,0:T(8,128)(2,1)S(1)} %slice.315), channel_id=1, source_target_pairs={{0,2},{1,3},{2,0},{3,1},{4,6},{5,7},{6,4},{7,5},{8,10},{9,11},{10,... | collective-permute-start | bytes 1769480 | tf_op jit(solution)/shard_map/ppermute | solution.py:133
  273.9 38.3 %collective-permute-start.19 = (bf16[256,1152]{1,0:T(8,128)(2,1)S(1)}, bf16[256,1152]{1,0:T(8,128)(2,1)S(1)}, u32[]{:S(2)}, u32[]{:S(2)}) collective-permute-start(bf16[256,1152]{1,0:T(8,128)(2,1)S(1)} %slice.316), channel_id=1, source_target_pairs={{0,2},{1,3},{2,0},{3,1},{4,6},{5,7},{6,4},{7,5},{8,10},{9,11},{10,... | collective-permute-start | bytes 1769480 | tf_op jit(solution)/shard_map/ppermute | solution.py:133
  300.2 37.5 %collective-permute-start.64 = (bf16[576,1536]{1,0:T(8,128)(2,1)S(1)}, bf16[576,1536]{1,0:T(8,128)(2,1)S(1)}, u32[]{:S(2)}, u32[]{:S(2)}) collective-permute-start(bf16[576,1536]{1,0:T(8,128)(2,1)S(1)} %constant_dynamic-slice_fusion.7), channel_id=1, source_target_pairs={{0,16},{16,0},{1,17},{17,1},{2,18},{18,2},{3,19},{19,3},{4,20},{20... | collective-permute-start | bytes 5308424 | tf_op jit(solution)/shard_map/ppermute | solution.py:133
  311.6 81.3 %collective-permute-start.80 = (bf16[1,4,96,1152]{3,2,1,0:T(8,128)(2,1)S(1)}, bf16[1,4,96,1152]{3,2,1,0:T(8,128)(2,1)S(1)}, u32[]{:S(2)}, u32[]{:S(2)}) collective-permute-start(bf16[1,4,96,1152]{3,2,1,0:T(8,128)(2,1)S(1)} %maximum_bitcast_fusion.2), channel_id=1, source_target_pairs={{0,2},{1,3},{2,0},{3,1},{4,6},{5,7},{6,4},{7,5},{8,10},{9,11},{10,... | collective-permute-start | bytes 2654216 | tf_op jit(solution)/shard_map/ppermute | solution.py:133
  316.5 36.6 %collective-permute-start.30 = (bf16[256,1152]{1,0:T(8,128)(2,1)S(1)}, bf16[256,1152]{1,0:T(8,128)(2,1)S(1)}, u32[]{:S(2)}, u32[]{:S(2)}) collective-permute-start(bf16[256,1152]{1,0:T(8,128)(2,1)S(1)} %multiply_convert_fusion.6), channel_id=1, source_target_pairs={{0,2},{1,3},{2,0},{3,1},{4,6},{5,7},{6,4},{7,5},{8,10},{9,11},{10,... | collective-permute-start | bytes 1769480 | tf_op jit(solution)/shard_map/ppermute | solution.py:133
  347.6 33.3 %collective-permute-start.66 = (bf16[1,144,1536]{2,1,0:T(8,128)(2,1)S(1)}, bf16[1,144,1536]{2,1,0:T(8,128)(2,1)S(1)}, u32[]{:S(2)}, u32[]{:S(2)}) collective-permute-start(bf16[1,144,1536]{2,1,0:T(8,128)(2,1)S(1)} %get-tuple-element.65), channel_id=1, source_target_pairs={{0,8},{4,12},{8,0},{12,4},{1,9},{5,13},{9,1},{13,5},{2,10},{6,14},... | collective-permute-start | bytes 1327112 | tf_op jit(solution)/shard_map/ppermute | solution.py:133
  351.3 29.6 %collective-permute-start.67 = (bf16[1,144,1536]{2,1,0:T(8,128)(2,1)S(1)}, bf16[1,144,1536]{2,1,0:T(8,128)(2,1)S(1)}, u32[]{:S(2)}, u32[]{:S(2)}) collective-permute-start(bf16[1,144,1536]{2,1,0:T(8,128)(2,1)S(1)} %get-tuple-element.64), channel_id=1, source_target_pairs={{0,12},{4,8},{8,4},{12,0},{1,13},{5,9},{9,5},{13,1},{2,14},{6,10},... | collective-permute-start | bytes 1327112 | tf_op jit(solution)/shard_map/ppermute | solution.py:133
  353.2 69.6 %collective-permute-start.31 = (bf16[512,1152]{1,0:T(8,128)(2,1)S(1)}, bf16[512,1152]{1,0:T(8,128)(2,1)S(1)}, u32[]{:S(2)}, u32[]{:S(2)}) collective-permute-start(bf16[512,1152]{1,0:T(8,128)(2,1)S(1)} %pad_maximum_fusion.14), channel_id=1, source_target_pairs={{0,1},{1,0},{2,3},{3,2},{4,5},{5,4},{6,7},{7,6},{8,9},{9,8},{10,11... | collective-permute-start | bytes 3538952 | tf_op jit(solution)/shard_map/ppermute | solution.py:133
  389.5 33.0 %collective-permute-start.69 = (bf16[1,144,1536]{2,1,0:T(8,128)(2,1)S(1)}, bf16[1,144,1536]{2,1,0:T(8,128)(2,1)S(1)}, u32[]{:S(2)}, u32[]{:S(2)}) collective-permute-start(bf16[1,144,1536]{2,1,0:T(8,128)(2,1)S(1)} %add_convert_fusion.7), channel_id=1, source_target_pairs={{0,8},{4,12},{8,0},{12,4},{1,9},{5,13},{9,1},{13,5},{2,10},{6,14},... | collective-permute-start | bytes 1327112 | tf_op jit(solution)/shard_map/ppermute | solution.py:133
  389.5 33.0 %collective-permute-start.70 = (bf16[1,144,1536]{2,1,0:T(8,128)(2,1)S(1)}, bf16[1,144,1536]{2,1,0:T(8,128)(2,1)S(1)}, u32[]{:S(2)}, u32[]{:S(2)}) collective-permute-start(bf16[1,144,1536]{2,1,0:T(8,128)(2,1)S(1)} %add_convert_fusion.7), channel_id=1, source_target_pairs={{0,12},{4,8},{8,4},{12,0},{1,13},{5,9},{9,5},{13,1},{2,14},{6,10},... | collective-permute-start | bytes 1327112 | tf_op jit(solution)/shard_map/ppermute | solution.py:133
  394.4 97.1 %collective-permute-start.81 = (bf16[2,4,96,1152]{3,2,1,0:T(8,128)(2,1)}, bf16[2,4,96,1152]{3,2,1,0:T(8,128)(2,1)}, u32[]{:S(2)}, u32[]{:S(2)}) collective-permute-start(bf16[2,4,96,1152]{3,2,1,0:T(8,128)(2,1)} %pad_maximum_fusion.11), channel_id=1, source_target_pairs={{0,1},{1,0},{2,3},{3,2},{4,5},{5,4},{6,7},{7,6},{8,9},{9,8},{10,11... | collective-permute-start | bytes 5308424 | tf_op jit(solution)/shard_map/ppermute | solution.py:133
  461.8 41.0 %collective-permute-start.32 = (bf16[512,1152]{1,0:T(8,128)(2,1)}, bf16[512,1152]{1,0:T(8,128)(2,1)}, u32[]{:S(2)}, u32[]{:S(2)}) collective-permute-start(bf16[512,1152]{1,0:T(8,128)(2,1)} %slice.310), channel_id=1, source_target_pairs={{0,1},{1,0},{2,3},{3,2},{4,5},{5,4},{6,7},{7,6},{8,9},{9,8},{10,11... | collective-permute-start | bytes 3538952 | tf_op jit(solution)/shard_map/ppermute | solution.py:133
  487.8 67.5 %collective-permute-start.71 = (bf16[1,4,144,1536]{3,2,1,0:T(8,128)(2,1)S(1)}, bf16[1,4,144,1536]{3,2,1,0:T(8,128)(2,1)}, u32[]{:S(2)}, u32[]{:S(2)}) collective-permute-start(bf16[1,4,144,1536]{3,2,1,0:T(8,128)(2,1)S(1)} %maximum_bitcast_fusion), channel_id=1, source_target_pairs={{0,2},{1,3},{2,0},{3,1},{4,6},{5,7},{6,4},{7,5},{8,10},{9,11},{10,... | collective-permute-start | bytes 5308424 | tf_op jit(solution)/shard_map/ppermute | solution.py:133
  499.7 38.4 %collective-permute-start.46 = (bf16[576,864]{1,0:T(8,128)(2,1)S(1)}, bf16[576,864]{1,0:T(8,128)(2,1)S(1)}, u32[]{:S(2)}, u32[]{:S(2)}) collective-permute-start(bf16[576,864]{1,0:T(8,128)(2,1)S(1)} %copy-done.57), channel_id=1, source_target_pairs={{0,16},{16,0},{1,17},{17,1},{2,18},{18,2},{3,19},{19,3},{4,20},{20... | collective-permute-start | bytes 2985992 | tf_op jit(solution)/shard_map/ppermute | solution.py:133
  501.3 35.8 %collective-permute-start.62 = (bf16[1,4,40,1152]{3,2,1,0:T(8,128)(2,1)S(1)}, bf16[1,4,40,1152]{3,2,1,0:T(8,128)(2,1)S(1)}, u32[]{:S(2)}, u32[]{:S(2)}) collective-permute-start(bf16[1,4,40,1152]{3,2,1,0:T(8,128)(2,1)S(1)} %maximum_bitcast_fusion.5), channel_id=1, source_target_pairs={{0,2},{1,3},{2,0},{3,1},{4,6},{5,7},{6,4},{7,5},{8,10},{9,11},{10,... | collective-permute-start | bytes 1105928 | tf_op jit(solution)/shard_map/ppermute | solution.py:133
  504.4 44.4 %collective-permute-start.33 = (bf16[256,1152]{1,0:T(8,128)(2,1)S(1)}, bf16[256,1152]{1,0:T(8,128)(2,1)S(1)}, u32[]{:S(2)}, u32[]{:S(2)}) collective-permute-start(bf16[256,1152]{1,0:T(8,128)(2,1)S(1)} %slice.314), channel_id=1, source_target_pairs={{0,2},{1,3},{2,0},{3,1},{4,6},{5,7},{6,4},{7,5},{8,10},{9,11},{10,... | collective-permute-start | bytes 1769480 | tf_op jit(solution)/shard_map/ppermute | solution.py:133
  538.1 62.6 %collective-permute-start.63 = (bf16[2,4,40,1152]{3,2,1,0:T(8,128)(2,1)}, bf16[2,4,40,1152]{3,2,1,0:T(8,128)(2,1)}, u32[]{:S(2)}, u32[]{:S(2)}) collective-permute-start(bf16[2,4,40,1152]{3,2,1,0:T(8,128)(2,1)} %pad_maximum_fusion.19), channel_id=1, source_target_pairs={{0,1},{1,0},{2,3},{3,2},{4,5},{5,4},{6,7},{7,6},{8,9},{9,8},{10,11... | collective-permute-start | bytes 2211848 | tf_op jit(solution)/shard_map/ppermute | solution.py:133
  558.9 84.7 %collective-permute-start.72 = (bf16[2,4,144,1536]{3,2,1,0:T(8,128)(2,1)}, bf16[2,4,144,1536]{3,2,1,0:T(8,128)(2,1)}, u32[]{:S(2)}, u32[]{:S(2)}) collective-permute-start(bf16[2,4,144,1536]{3,2,1,0:T(8,128)(2,1)} %pad_maximum_fusion.2), channel_id=1, source_target_pairs={{0,1},{1,0},{2,3},{3,2},{4,5},{5,4},{6,7},{7,6},{8,9},{9,8},{10,11... | collective-permute-start | bytes 10616840 | tf_op jit(solution)/shard_map/ppermute | solution.py:133
  593.8 25.3 %collective-permute-start.53 = (bf16[1,4,144,864]{3,2,1,0:T(8,128)(2,1)}, bf16[1,4,144,864]{3,2,1,0:T(8,128)(2,1)}, u32[]{:S(2)}, u32[]{:S(2)}) collective-permute-start(bf16[1,4,144,864]{3,2,1,0:T(8,128)(2,1)} %maximum_bitcast_fusion.1), channel_id=1, source_target_pairs={{0,2},{1,3},{2,0},{3,1},{4,6},{5,7},{6,4},{7,5},{8,10},{9,11},{10,... | collective-permute-start | bytes 2985992 | tf_op jit(solution)/shard_map/ppermute | solution.py:133
  620.9 32.3 %collective-permute-start.54 = (bf16[2,4,144,864]{3,2,1,0:T(8,128)(2,1)S(1)}, bf16[2,4,144,864]{3,2,1,0:T(8,128)(2,1)S(1)}, u32[]{:S(2)}, u32[]{:S(2)}) collective-permute-start(bf16[2,4,144,864]{3,2,1,0:T(8,128)(2,1)S(1)} %pad_maximum_fusion.7), channel_id=1, source_target_pairs={{0,1},{1,0},{2,3},{3,2},{4,5},{5,4},{6,7},{7,6},{8,9},{9,8},{10,11... | collective-permute-start | bytes 5971976 | tf_op jit(solution)/shard_map/ppermute | solution.py:133
  (160 other events, 2015.9 us)

commit v2 on v0

v2 whole, which is shorter than its diff:
```python
import functools
import math

import jax
import jax.numpy as jnp
from jax import lax
from jax.experimental import pallas as pl
from jax.experimental.pallas import tpu as pltpu
from jax.sharding import PartitionSpec as P

LANES = 128
epsilon = 1e-06
low, wide = jnp.bfloat16, jnp.float32


def bits_of(size):
    return [1 << b for b in reversed(range(size.bit_length() - 1))]


def block_order(size):
    order = [0]
    for bit in bits_of(size):
        order = order + [o ^ bit for o in order]
    return order


def swap(value, axis, size, bit):
    return lax.ppermute(value, axis, [(a, a ^ bit) for a in range(size)])


def after(value, *earlier):
    return lax.optimization_barrier((value,) + earlier)[0]


def cat(*parts):
    return jnp.concatenate(parts, axis=0)


def dot(a, b):
    return jnp.dot(a, b, preferred_element_type=wide)


def dot_t(a, b):
    return lax.dot_general(a, b, (((1,), (1,)), ((), ())), preferred_element_type=wide)


def whole(shape):
    return pl.BlockSpec(shape, lambda *_: (0,) * len(shape))


def shape_of(shape, dtype):
    return jax.ShapeDtypeStruct(shape, dtype)


def kernel(body, name, scalars, args, grid, in_specs, out_specs, out_shape, scratch=(), megabytes=32):
    none = scalars is None
    return pl.pallas_call(
        functools.partial(body, None) if none else body,
        grid_spec=pltpu.PrefetchScalarGridSpec(
            num_scalar_prefetch=0 if none else 1, grid=grid, in_specs=in_specs, out_specs=out_specs, scratch_shapes=scratch
        ),
        out_shape=out_shape,
        compiler_params=pltpu.CompilerParams(vmem_limit_bytes=megabytes * 1024 * 1024),
        cost_estimate=pl.CostEstimate(flops=1, bytes_accessed=1, transcendentals=0),
        name=name,
    )(*([] if none else [scalars]), *args)


def pick(step, refs):
    value = refs[0][...]
    for n in range(1, len(refs)):
        value = jnp.where(step == n, refs[n][...], value)
    return value


def cut_qkv_kernel(parts, count, at, w_ref, o_ref):
    piece = o_ref.shape[1] // parts
    for c in range(count):

        @pl.when(at[0] == c)
        def _():
            for p in range(parts):
                start = (p * count + c) * piece
                o_ref[:, p * piece : (p + 1) * piece] = w_ref[:, start : start + piece]


def cut_qkv(w, at, parts, count):
    rows, width = w.shape
    step = 144
    return kernel(
        functools.partial(cut_qkv_kernel, parts, count),
        "cut_qkv",
        at,
        [w],
        (rows // step,),
        [pl.BlockSpec((step, width), lambda s, o=None: (s, 0))],
        pl.BlockSpec((step, width // count), lambda s, o=None: (s, 0)),
        shape_of((rows, width // count), w.dtype),
    )


def copy_kernel(at, *refs):
    n = len(refs) // 2
    for a, b in zip(refs[:n], refs[n:]):
        b[...] = a[...]


def cut_rest(w_up, w_out, w_down, at, parts, count):
    rows, width = w_up.shape
    piece = width // (parts * count)
    shapes = [(w.shape[0] // count, w.shape[1]) for w in (w_out, w_down)]
    return kernel(
        copy_kernel,
        "cut_rest",
        at,
        [w_up, w_out, w_down],
        (parts,),
        [pl.BlockSpec((rows, piece), lambda p, o=None: (0, p * count + o[0]))]
        + [pl.BlockSpec(s, lambda p, o=None: (o[0], 0)) for s in shapes],
        [pl.BlockSpec((rows, piece), lambda p, o=None: (0, p))] + [whole(s) for s in shapes],
        [shape_of((rows, piece * parts), w_up.dtype)] + [shape_of(s, w_up.dtype) for s in shapes],
    )


def widen_kernel(head_dim, heads, at, mine_ref, other_ref, o_ref):
    src = jnp.where(at[0] == pl.program_id(0), mine_ref[...], other_ref[...])
    none = jnp.zeros((src.shape[0], LANES - head_dim), src.dtype)
    for t in range(3):
        for n in range(heads):
            start, end = (t * heads + n) * head_dim, (n * 3 + t) * LANES
            o_ref[:, end : end + LANES] = jnp.concatenate([src[:, start : start + head_dim], none], axis=1)


def widen(mine, other, at, head_dim):
    rows, width = mine.shape
    out = width // head_dim * LANES
    return kernel(
        functools.partial(widen_kernel, head_dim, width // (3 * head_dim)),
        "widen",
        at,
        [mine, other],
        (2,),
        [whole((rows, width))] * 2,
        pl.BlockSpec((rows, out), lambda h, o=None: (h, 0)),
        shape_of((2 * rows, out), mine.dtype),
    )


def widen_rows_kernel(head_dim, at, mine_ref, other_ref, o_ref):
    src = jnp.where(at[0] == pl.program_id(0), mine_ref[...], other_ref[...]).astype(wide)
    none = jnp.zeros((LANES - head_dim, src.shape[1]), wide)
    for n in range(src.shape[0] // head_dim):
        part = jnp.concatenate([src[n * head_dim : (n + 1) * head_dim], none], axis=0)
        o_ref[n * LANES : (n + 1) * LANES] = part.astype(low)


def widen_rows(mine, other, at, head_dim):
    rows, width = mine.shape
    out = rows // head_dim * LANES
    return kernel(
        functools.partial(widen_rows_kernel, head_dim),
        "widen_rows",
        at,
        [mine, other],
        (2,),
        [whole((rows, width))] * 2,
        pl.BlockSpec((out, width), lambda h, o=None: (h, 0)),
        shape_of((2 * out, width), mine.dtype),
    )


def join_kernel(at, a_ref, b_ref, c_ref, d_ref, x_ref, y_ref):
    mine = at[0] == pl.program_id(0)
    x_ref[...] = jnp.where(mine, a_ref[...], b_ref[...])
    y_ref[...] = jnp.where(mine, c_ref[...], d_ref[...])


def join(mine_up, other_up, mine_down, other_down, at):
    specs = [whole(a.shape) for a in (mine_up, other_up, mine_down, other_down)]
    return kernel(
        join_kernel,
        "join",
        at,
        [mine_up, other_up, mine_down, other_down],
        (2,),
        specs,
        [pl.BlockSpec(a.shape, lambda h, o=None: (h, 0)) for a in (mine_up, mine_down)],
        [shape_of((2 * a.shape[0], a.shape[1]), low) for a in (mine_up, mine_down)],
    )


def tables_kernel(n_row, tile, tile_cols, head_dim, at, cos_ref, a_ref, b_ref):
    shape = cos_ref.shape
    pairs = head_dim // 4
    pos = lax.broadcasted_iota(jnp.int32, shape, 0)
    lane = lax.broadcasted_iota(jnp.int32, shape, 1)
    block = pos // tile
    row_block, col_block = block % n_row, block // n_row
    row_at = jnp.zeros(shape, jnp.int32)
    for k in range(n_row):
        row_at = jnp.where(row_block == k, at[2 + k], row_at)
    col_at = jnp.zeros(shape, jnp.int32)
    for j in range(shape[0] // (tile * n_row)):
        col_at = jnp.where(col_block == j, at[2 + n_row + j], col_at)
    inside = pos % tile
    row = (row_at * (tile // tile_cols) + inside // tile_cols) * at[0]
    col = (col_at * tile_cols + inside % tile_cols) * at[1]
    half = 2 * pairs
    within = jnp.where(lane < half, lane, lane - half)
    first = within < pairs
    step = jnp.where(first, within, within - pairs).astype(wide)
    frequency = jnp.exp(step * (-math.log(10000.0) / pairs))
    angle = jnp.where(lane < half, row, col).astype(wide) * frequency
    live = lane < head_dim
    cos, sin = jnp.cos(angle), jnp.sin(angle)
    cos_ref[...] = jnp.where(live, cos, 0.0)
    a_ref[...] = jnp.where(live & first, -sin, 0.0)
    b_ref[...] = jnp.where(live & jnp.logical_not(first), sin, 0.0)


def tables(at, n_row, n_col, tile, tile_cols, head_dim):
    shape = (n_row * n_col * tile, LANES)
    return kernel(
        functools.partial(tables_kernel, n_row, tile, tile_cols, head_dim),
        "tables",
        at,
        [],
        (1,),
        [],
        [whole(shape)] * 3,
        [shape_of(shape, wide)] * 3,
    )


def place_modulation_kernel(at, *refs):
    o_ref = refs[-1]
    rows = refs[0].shape[0]
    for j, ref in enumerate(refs[:-1]):
        for k in range(rows):
            o_ref[pl.ds(at[j * rows + k], 1), :] = ref[k : k + 1, :]


def place_modulation(parts, at):
    rows, width = parts[0].shape
    shape = (rows * len(parts), width)
    return kernel(
        place_modulation_kernel,
        "place_modulation",
        at,
        parts,
        (1,),
        [whole(p.shape) for p in parts],
        whole(shape),
        shape_of(shape, wide),
    )


def inverse(v):
    return lax.rsqrt(jnp.mean(v * v, axis=-1, keepdims=True) + epsilon)


def norm_back(v, inv, stretch, g_y):
    normed = v * inv
    g = g_y * (1.0 + stretch)
    g_v = (g - normed * jnp.mean(g * normed, axis=-1, keepdims=True)) * inv
    return g_v, jnp.sum(g_y, axis=0, keepdims=True), jnp.sum(g_y * normed, axis=0, keepdims=True)


def put_rows(ref, **rows):
    ref[...] = jnp.zeros_like(ref)
    for name, row in rows.items():
        n = int(name[1:])
        ref[n : n + 1, :] = row


def turn(x, cos, sin_a, sin_b, shift):
    return x * cos + pltpu.roll(x, LANES - shift, 1) * sin_a + pltpu.roll(x, shift, 1) * sin_b


def project_qkv_kernel(at, *refs):
    toks, (mod_ref, w_ref, in_ref, joined_ref) = refs[:-4], refs[-4:]
    x = pick(pl.program_id(0), toks).astype(wide)
    attn_in = (x * inverse(x) * (1.0 + mod_ref[1:2, :]) + mod_ref[0:1, :]).astype(low)
    in_ref[...] = attn_in
    joined_ref[...] = dot(attn_in, w_ref[...])


def project_qkv(toks, modulation, w):
    rows, width = toks[0].shape
    n, columns = len(toks), w.shape[1]
    return kernel(
        project_qkv_kernel,
        "project_qkv",
        None,
        [*toks, modulation, w],
        (n,),
        [whole(t.shape) for t in toks] + [whole(modulation.shape), whole(w.shape)],
        [pl.BlockSpec((rows, width), lambda s, o=None: (s, 0)), pl.BlockSpec((rows, columns), lambda s, o=None: (s, 0))],
        [shape_of((n * rows, width), low), shape_of((n * rows, columns), wide)],
    )


def attn_fwd_kernel(head_dim, at, x_ref, cos_ref, a_ref, b_ref, gain_ref, o_ref, aug_ref):
    tokens = x_ref.shape[0]
    pairs, scale = head_dim // 4, head_dim**-0.5 * math.log2(math.e)
    cos, sa, sb = cos_ref[...], a_ref[...], b_ref[...]

    def normed(x):
        return x * lax.rsqrt(jnp.sum(x * x, axis=-1, keepdims=True) * (1.0 / head_dim) + epsilon)

    q = turn(normed(x_ref[:, :LANES]) * gain_ref[0:1, :], cos, sa, sb, pairs) * scale
    k = turn(normed(x_ref[:, LANES : 2 * LANES]) * gain_ref[1:2, :], cos, sa, sb, pairs)
    lane = lax.broadcasted_iota(jnp.int32, (tokens, LANES), 1)
    extra = (lane == head_dim) | (lane == head_dim + 1)
    kk = jnp.where(extra, 1.0, k).astype(low)
    vv = jnp.where(extra, -1.0, x_ref[:, 2 * LANES :]).astype(low)
    aug_ref[:, LANES : 2 * LANES] = kk
    aug_ref[:, 2 * LANES :] = vv
    q_low = q.astype(low)
    rows = 256
    for s in range(tokens // rows):
        span = slice(s * rows, (s + 1) * rows)
        out = dot(jnp.exp2(dot_t(q_low[span], kk)).astype(low), vv)
        total = -out[:, head_dim : head_dim + 1]
        lane_s = lane[span]
        o_ref[span, :] = jnp.where(lane_s < head_dim, out * (1.0 / total), 0.0).astype(low)
        lse = -jnp.log2(total)
        high = lse.astype(low).astype(wide)
        aug = jnp.where(lane_s == head_dim, high, jnp.where(lane_s == head_dim + 1, lse - high, q[span]))
        aug_ref[span, :LANES] = aug.astype(low)


def attn_fwd(joined, cos, sa, sb, gain, head_dim):
    tokens, columns = joined.shape
    heads = columns // (3 * LANES)
    block = pl.BlockSpec((tokens, 3 * LANES), lambda h, o=None: (0, h))
    return kernel(
        functools.partial(attn_fwd_kernel, head_dim),
        "attn_fwd",
        None,
        [joined, cos, sa, sb, gain],
        (heads,),
        [block, whole(cos.shape), whole(cos.shape), whole(cos.shape), whole(gain.shape)],
        [pl.BlockSpec((tokens, LANES), lambda h, o=None: (0, h)), block],
        [shape_of((tokens, heads * LANES), low), shape_of((tokens, columns), low)],
        megabytes=60,
    )


def attn_bwd_kernel(head_dim, at, *refs):
    n = len(refs) - 14
    gbs = refs[:n]
    x_ref, aug_ref, o_ref, w_ref, cos_ref, a_ref, b_ref, gain_ref, g_ref, gg_ref = refs[n : n + 10]
    dk_acc, dv_acc, dq_acc, do_acc = refs[n + 10 :]
    tokens = x_ref.shape[0]
    pairs = head_dim // 4
    h = pl.program_id(0)
    rows = tokens // n
    for j in range(n):
        do_acc[j * rows : (j + 1) * rows, :] = dot_t(gbs[j][...], w_ref[...]).astype(low)
    lane = lax.broadcasted_iota(jnp.int32, (tokens, LANES), 1)
    do_f = do_acc[...].astype(wide)
    delta = jnp.sum(do_f * o_ref[...].astype(wide), axis=-1, keepdims=True)
    high = delta.astype(low).astype(wide)
    do_a = jnp.where(lane == head_dim, high, jnp.where(lane == head_dim + 1, delta - high, do_f)).astype(low)
    qa, ka, va = aug_ref[:, :LANES], aug_ref[:, LANES : 2 * LANES], aug_ref[:, 2 * LANES :]
    ka_t = ka.T
    cols = 256
    for s in range(tokens // cols):
        qs = qa[s * cols : (s + 1) * cols]
        ds = do_a[s * cols : (s + 1) * cols]
        p = jnp.exp2(dot_t(ka, qs))
        grad_s = (p * dot_t(va, ds)).astype(low)
        dv, dk = dot(p.astype(low), ds), dot(grad_s, qs)
        if s == 0:
            dv_acc[...] = dv
            dk_acc[...] = dk
        else:
            dv_acc[...] += dv
            dk_acc[...] += dk
        dq_acc[:, s * cols : (s + 1) * cols] = dot(ka_t, grad_s)
    inside = lane < head_dim
    cos, sa, sb = cos_ref[...], a_ref[...], b_ref[...]

    def back(g, x, gain):
        g = jnp.where(inside, g, 0.0)
        g = g * cos - pltpu.roll(g, LANES - pairs, 1) * sa - pltpu.roll(g, pairs, 1) * sb
        inv = lax.rsqrt(jnp.sum(x * x, axis=-1, keepdims=True) * (1.0 / head_dim) + epsilon)
        normed = x * inv
        gain_part = jnp.sum(g * normed, axis=0, keepdims=True)
        g = g * gain
        return (g - normed * (jnp.sum(g * normed, axis=-1, keepdims=True) * (1.0 / head_dim))) * inv, gain_part

    gq, ggq = back(dq_acc[...].T * (head_dim**-0.5), x_ref[:, :LANES], gain_ref[0:1, :])
    gk, ggk = back(dk_acc[...] * math.log(2.0), x_ref[:, LANES : 2 * LANES], gain_ref[1:2, :])
    g_ref[:, :LANES] = gq.astype(low)
    g_ref[:, LANES : 2 * LANES] = gk.astype(low)
    g_ref[:, 2 * LANES :] = jnp.where(inside, dv_acc[...], 0.0).astype(low)
    gg = jnp.concatenate([ggq, ggk], axis=0)

    @pl.when(h == 0)
    def _():
        gg_ref[...] = gg

    @pl.when(h > 0)
    def _():
        gg_ref[...] += gg


def attn_bwd(grads, joined, aug, mixed, w_out, cos, sa, sb, gain, head_dim, first, heads):
    tokens = joined.shape[0]
    block = pl.BlockSpec((tokens, 3 * LANES), lambda h, o=None: (0, first + h))
    return kernel(
        functools.partial(attn_bwd_kernel, head_dim),
        "attn_bwd",
        None,
        [*grads, joined, aug, mixed, w_out, cos, sa, sb, gain],
        (heads,),
        [whole(g.shape) for g in grads]
        + [block, block, pl.BlockSpec((tokens, LANES), lambda h, o=None: (0, first + h))]
        + [pl.BlockSpec((LANES, w_out.shape[1]), lambda h, o=None: (first + h, 0))]
        + [whole(cos.shape), whole(cos.shape), whole(cos.shape), whole(gain.shape)],
        [pl.BlockSpec((tokens, 3 * LANES), lambda h, o=None: (0, h)), whole(gain.shape)],
        [shape_of((tokens, heads * 3 * LANES), low), shape_of(gain.shape, wide)],
        scratch=[
            pltpu.VMEM((tokens, LANES), wide),
            pltpu.VMEM((tokens, LANES), wide),
            pltpu.VMEM((LANES, tokens), wide),
            pltpu.VMEM((tokens, LANES), low),
        ],
        megabytes=60,
    )


def project_kernel(at, x_ref, w_ref, o_ref):
    o_ref[...] = dot(x_ref[...], w_ref[...]).astype(o_ref.dtype)


def project_back_kernel(at, *refs):
    xs, (w_ref, o_ref) = refs[:-2], refs[-2:]
    width = xs[0].shape[1]
    value = sum(dot_t(x[...], w_ref[:, n * width : (n + 1) * width]) for n, x in enumerate(xs))
    o_ref[...] = value.astype(o_ref.dtype)


def project(xs, w, first, count, rows, dtype):
    columns = w.shape[1] if len(xs) == 1 else w.shape[0]
    return kernel(
        project_kernel if len(xs) == 1 else project_back_kernel,
        "project",
        None,
        [*xs, w],
        (count,),
        [pl.BlockSpec((rows, x.shape[1]), lambda s, o=None: (first + s, 0)) for x in xs] + [whole(w.shape)],
        pl.BlockSpec((rows, columns), lambda s, o=None: (s, 0)),
        shape_of((count * rows, columns), dtype),
    )


def add_kernel(at, a_ref, b_ref, o_ref):
    o_ref[...] = (a_ref[...].astype(wide) + b_ref[...].astype(wide)).astype(low)


def add_second(a, b):
    rows, columns = a.shape[0] // 2, a.shape[1]
    return kernel(
        add_kernel,
        "add_second",
        None,
        [a, b],
        (1,),
        [pl.BlockSpec((rows, columns), lambda s, o=None: (1, 0))] * 2,
        whole((rows, columns)),
        shape_of((rows, columns), low),
    )


def middle_kernel(live, keep_ref, core_ref, y_ref, tok_ref, mod_ref, hidden_ref, branch_ref, mlp_ref):
    branch = keep_ref[...] + core_ref[...].astype(wide) + y_ref[...].astype(wide)
    gate = mod_ref[2:3, :] * live[0].astype(wide)
    hidden = tok_ref[...].astype(wide) + gate * branch
    hidden_ref[...] = hidden
    branch_ref[...] = branch
    mlp_ref[...] = (hidden * inverse(hidden) * (1.0 + mod_ref[4:5, :]) + mod_ref[3:4, :]).astype(low)


def middle(keep, core, y, tok, modulation, live):
    shape = y.shape
    first = pl.BlockSpec(shape, lambda s, o=None: (0, 0))
    return kernel(
        middle_kernel,
        "middle",
        live,
        [keep, core, y, tok, modulation],
        (1,),
        [first, first, first, first, whole(modulation.shape)],
        [first] * 3,
        [shape_of(shape, wide), shape_of(shape, wide), shape_of(shape, low)],
    )


def middle_back_kernel(live, keep_ref, core_ref, y_ref, hidden_ref, branch_ref, cot_ref, mod_ref, grad_ref, gb_ref, s_ref):
    g_y = keep_ref[...] + core_ref[...].astype(wide) + y_ref[...].astype(wide)
    hidden = hidden_ref[...]
    on = live[0].astype(wide)
    g_v, g_o, g_a = norm_back(hidden, inverse(hidden), mod_ref[4:5, :], g_y)
    grad = cot_ref[...].astype(wide) + g_v
    grad_ref[...] = grad
    gb_ref[...] = (mod_ref[2:3, :] * on * grad).astype(low)
    put_rows(s_ref, r2=on * jnp.sum(grad * branch_ref[...], axis=0, keepdims=True), r3=g_o, r4=g_a)


def middle_back(keep, core, y, hidden, branch, cot, modulation, live):
    shape = y.shape
    first = pl.BlockSpec(shape, lambda s, o=None: (0, 0))
    sums = (8, shape[1])
    return kernel(
        middle_back_kernel,
        "middle_back",
        live,
        [keep, core, y, hidden, branch, cot, modulation],
        (1,),
        [first] * 6 + [whole(modulation.shape)],
        [first, first, whole(sums)],
        [shape_of(shape, wide), shape_of(shape, low), shape_of(sums, wide)],
    )


def result_kernel(live, keep_ref, core_ref, y_ref, hidden_ref, cot_ref, mod_ref, *outs):
    mlp_out = keep_ref[...] + core_ref[...].astype(wide) + y_ref[...].astype(wide)
    on = live[0].astype(wide)
    result = (hidden_ref[...] + mod_ref[5:6, :] * on * mlp_out).astype(low)
    put_rows(outs[-1], r5=on * jnp.sum(cot_ref[...].astype(wide) * mlp_out, axis=0, keepdims=True))
    outs[0][...] = result


def result(keep, core, y, hidden, cot, modulation, live):
    shape = y.shape
    first = pl.BlockSpec(shape, lambda s, o=None: (0, 0))
    sums = (8, shape[1])
    return kernel(
        result_kernel,
        "result",
        live,
        [keep, core, y, hidden, cot, modulation],
        (1,),
        [first] * 5 + [whole(modulation.shape)],
        [first, whole(sums)],
        [shape_of(shape, low), shape_of(sums, wide)],
    )


def last_back_kernel(live, keep_ref, core_ref, y_ref, tok_ref, grad_ref, mod_ref, *outs):
    g_y = keep_ref[...] + core_ref[...].astype(wide) + y_ref[...].astype(wide)
    tok = tok_ref[...].astype(wide)
    g_v, g_o, g_a = norm_back(tok, inverse(tok), mod_ref[1:2, :], g_y)
    grad = (grad_ref[...] + g_v).astype(low)
    put_rows(outs[-1], r0=g_o, r1=g_a)
    outs[0][...] = grad


def last_back(keep, core, y, tok, grad, modulation, live):
    shape = y.shape
    first = pl.BlockSpec(shape, lambda s, o=None: (0, 0))
    sums = (8, shape[1])
    return kernel(
        last_back_kernel,
        "last_back",
        live,
        [keep, core, y, tok, grad, modulation],
        (1,),
        [first] * 5 + [whole(modulation.shape)],
        [first, whole(sums)],
        [shape_of(shape, low), shape_of(sums, wide)],
    )


def feed_forward_kernel(n, live, *refs):
    xs, cots = refs[:n], refs[n : 2 * n]
    mod_ref, up_ref, down_ref, act_ref, gu_ref, gm_ref, send_ref, keep_ref = refs[2 * n :]
    s = pl.program_id(0)
    block = (s + n // 2) % n
    x, cot = pick(block, xs), pick(block, cots)
    w_up = up_ref[...]
    gate_up = dot(x, w_up)
    half = gate_up.shape[1] // 2
    gate, up = gate_up[:, :half], gate_up[:, half:]
    sig = 1.0 / (1.0 + jnp.exp(-gate))
    silu = gate * sig
    act_ref[...] = (silu * up).astype(low)
    grad = (mod_ref[5:6, :] * live[0].astype(wide) * cot.astype(wide)).astype(low)
    gm_ref[...] = grad
    grad_act = dot_t(grad, down_ref[...])
    gu_ref[:, :half] = (grad_act * up * sig * (1.0 + gate * (1.0 - sig))).astype(low)
    gu_ref[:, half:] = (grad_act * silu).astype(low)
    grad_in = dot_t(gu_ref[...], w_up)

    @pl.when(s < n // 2)
    def _():
        send_ref[...] = grad_in.astype(low)

    @pl.when(s >= n // 2)
    def _():
        keep_ref[...] = grad_in


def feed_forward(xs, cots, modulation, w_up, w_down, live):
    n = len(xs)
    rows, width = xs[0].shape
    hidden = w_down.shape[0]
    half = n // 2

    def by_block(columns):
        return pl.BlockSpec((rows, columns), lambda s, o=None: ((s + half) % n, 0))

    return kernel(
        functools.partial(feed_forward_kernel, n),
        "feed_forward",
        live,
        [*xs, *cots, modulation, w_up, w_down],
        (n,),
        [whole(x.shape) for x in (*xs, *cots, modulation, w_up, w_down)],
        [
            by_block(hidden),
            by_block(2 * hidden),
            by_block(width),
            pl.BlockSpec((rows, width), lambda s, o=None: (jnp.minimum(s, half - 1), 0)),
            pl.BlockSpec((rows, width), lambda s, o=None: (jnp.maximum(s - half, 0), 0)),
        ],
        [
            shape_of((n * rows, hidden), low),
            shape_of((n * rows, 2 * hidden), low),
            shape_of((n * rows, width), low),
            shape_of((half * rows, width), low),
            shape_of((half * rows, width), wide),
        ],
        megabytes=48,
    )


def halves_of(acc_ref, at):
    rows = acc_ref.shape[0] // 2
    return [acc_ref[pl.ds(pl.multiple_of(i * rows, 8), rows), :] for i in (1 - at[0], at[0])]


def turned(xs, xt_ref):
    @pl.when(pl.program_id(0) == 0)
    def _():
        rows = xs[0].shape[0]
        for j, x in enumerate(xs):
            xt_ref[:, j * rows : (j + 1) * rows] = x[...].T


def turn_kernel(at, *refs):
    n = len(refs) // 2
    for a, b in zip(refs[:n], refs[n:]):
        b[...] = a[...].T


def turn_blocks(arrays, rows):
    tokens = arrays[0].shape[0]
    return kernel(
        turn_kernel,
        "turn_blocks",
        None,
        arrays,
        (tokens // rows,),
        [pl.BlockSpec((rows, a.shape[1]), lambda s, o=None: (s, 0)) for a in arrays],
        [pl.BlockSpec((a.shape[1], rows), lambda s, o=None: (0, s)) for a in arrays],
        [shape_of((a.shape[1], tokens), a.dtype) for a in arrays],
    )


def grad_part_kernel(n, at, *refs):
    xs, (b_ref, theirs, mine, xt_ref, acc_ref) = refs[:n], refs[n:]
    turned(xs, xt_ref)
    acc_ref[...] = dot(xt_ref[...], b_ref[...])
    for ref, value in zip((theirs, mine), halves_of(acc_ref, at)):
        ref[...] = value.astype(low)


def grad_part(xs, b, at, first, columns, chunk):
    tokens, width = len(xs) * xs[0].shape[0], xs[0].shape[1]
    out = pl.BlockSpec((width // 2, chunk), lambda s, o=None: (0, s))
    return kernel(
        functools.partial(grad_part_kernel, len(xs)),
        "grad_part",
        at,
        [*xs, b],
        (columns // chunk,),
        [whole(x.shape) for x in xs] + [pl.BlockSpec((tokens, chunk), lambda s, o=None: (0, first // chunk + s))],
        [out, out],
        [shape_of((width // 2, columns), low)] * 2,
        scratch=[pltpu.VMEM((width, tokens), low), pltpu.VMEM((width, chunk), wide)],
        megabytes=36,
    )


def grad_last_kernel(n, head_dim, cut, columns, at, *refs):
    xt_ref, mt_ref = refs[:2]
    parts, gbs = refs[2 : 2 + n], refs[2 + n : 2 + 2 * n]
    outs = refs[2 + 2 * n : 6 + 2 * n]
    acc_ref, out_ref = refs[6 + 2 * n :]
    s = pl.program_id(0)

    @pl.when(s == 0)
    def _():
        for ref in outs:
            ref[:, columns:] = jnp.zeros((ref.shape[0], ref.shape[1] - columns), low)

    acc_ref[...] = dot(xt_ref[...], pick(s, parts))
    for half, value in enumerate(halves_of(acc_ref, at)):
        joined = [value[:, h * LANES : h * LANES + head_dim] for h in range(value.shape[1] // LANES)]
        value = jnp.concatenate(joined, axis=1).astype(low)
        width, rows = value.shape[1], value.shape[0] - cut
        for c in range(n):

            @pl.when(s == c)
            def _():
                outs[half][:, c * width : (c + 1) * width] = value[:cut]
                outs[2 + half][:rows, c * width : (c + 1) * width] = value[cut:]

    @pl.when(s == n - 1)
    def _():
        rows = gbs[0].shape[0]
        out_ref[...] = sum(dot(mt_ref[:, j * rows : (j + 1) * rows], gbs[j][...]) for j in range(n))
        for half, value in enumerate(halves_of(out_ref, at)):
            ref = outs[2 + half]
            heads = [value[h * LANES : h * LANES + head_dim] for h in range(value.shape[0] // LANES)]
            value = jnp.concatenate(heads, axis=0)
            length, width = value.shape[0], columns
            start = xt_ref.shape[0] // 2 - cut
            side, third = value.shape[1] - width, length // 3
            ref[start : start + length, :width] = value[:, :width].astype(low)
            rest = [value[k * third : (k + 1) * third, width:] for k in range(3)]
            ref[start + length :, :width] = jnp.concatenate(rest, axis=1).astype(low)


def grad_last(xt, parts, mixed_t, gbs, at, head_dim, cut):
    n = len(parts)
    width = xt.shape[0]
    columns = n * parts[0].shape[1] // LANES * head_dim
    length = mixed_t.shape[0] // LANES * head_dim // 2
    assert gbs[0].shape[1] - columns == columns // 3 and length % 3 == 0
    padded = -(-columns // LANES) * LANES
    shapes = [(cut, padded), (width // 2 - cut + length + length // 3, padded)]
    return kernel(
        functools.partial(grad_last_kernel, n, head_dim, cut, columns),
        "grad_last",
        at,
        [xt, mixed_t, *parts, *gbs],
        (n,),
        [whole(a.shape) for a in (xt, mixed_t, *parts, *gbs)],
        [whole(a) for a in shapes for _ in range(2)],
        [shape_of(a, low) for a in shapes for _ in range(2)],
        scratch=[
            pltpu.VMEM((width, parts[0].shape[1]), wide),
            pltpu.VMEM((mixed_t.shape[0], gbs[0].shape[1]), wide),
        ],
        megabytes=52,
    )


def add_halves_kernel(at, a_ref, b_ref, send_ref, keep_ref):
    value = a_ref[...].astype(wide) + b_ref[...].astype(wide)

    @pl.when(pl.program_id(0) == 0)
    def _():
        send_ref[...] = value.astype(low)

    @pl.when(pl.program_id(0) == 1)
    def _():
        keep_ref[...] = value


def add_halves(a, b, at):
    rows, columns = a.shape[0] // 2, a.shape[1]
    block = pl.BlockSpec((rows, columns), lambda s, o=None: (o[s], 0))
    return kernel(
        add_halves_kernel,
        "add_halves",
        at,
        [a, b],
        (2,),
        [block, block],
        [whole((rows, columns))] * 2,
        [shape_of((rows, columns), low), shape_of((rows, columns), wide)],
    )


def join_halves_kernel(at, a_ref, b_ref, o_ref):
    o_ref[...] = jnp.where(pl.program_id(0) == at[1], a_ref[...], b_ref[...])


def join_halves(mine, other, at):
    rows, columns = mine.shape
    return kernel(
        join_halves_kernel,
        "join_halves",
        at,
        [mine, other],
        (2,),
        [whole(mine.shape)] * 2,
        pl.BlockSpec((rows, columns), lambda s, o=None: (s, 0)),
        shape_of((2 * rows, columns), low),
    )


def place_columns(srcs, at, start, step, parts, up_ref):
    width = srcs[0].shape[1]
    piece, count = width // parts, len(srcs)

    def put(d, block):
        for p in range(parts):
            end = (p * count + d) * piece
            up_ref[:, end : end + piece] = block[:, p * piece : (p + 1) * piece]

    for j in range(count):
        block = srcs[j][pl.ds(start, step), :].astype(wide)
        for d in range(count):
            pl.when(at[j] == d)(functools.partial(put, d, block))


def place_first_kernel(parts, at, *refs):
    srcs, up_ref = refs[:-1], refs[-1]
    step = up_ref.shape[0]
    place_columns(srcs, at, pl.multiple_of(pl.program_id(0) * step, 16), step, parts, up_ref)


def place_first(blocks, at, parts):
    count = len(blocks)
    rows, width = blocks[0].shape
    step = 144
    return kernel(
        functools.partial(place_first_kernel, parts),
        "place_first",
        at,
        blocks,
        (rows // step,),
        [whole(b.shape) for b in blocks],
        pl.BlockSpec((step, width * count), lambda s, o=None: (s, 0)),
        shape_of((rows, 2 * width * count), wide),
    )


def place_second_kernel(count, parts, at, *refs):
    srcs, up_ref = refs[:count], refs[-1]
    step = up_ref.shape[0]
    place_columns(srcs, at, pl.multiple_of(pl.program_id(0) * step, 16), step, parts, up_ref)


def place_second(blocks, first, at, parts):
    count = len(blocks)
    width = blocks[0].shape[1]
    rows = first.shape[0]
    step = 144
    return pl.pallas_call(
        functools.partial(place_second_kernel, count, parts),
        grid_spec=pltpu.PrefetchScalarGridSpec(
            num_scalar_prefetch=1,
            grid=(rows // step,),
            in_specs=[whole(b.shape) for b in blocks] + [pl.BlockSpec(memory_space=pl.ANY)],
            out_specs=pl.BlockSpec((step, width * count), lambda s, o: (s, 1)),
        ),
        out_shape=shape_of(first.shape, wide),
        input_output_aliases={count + 1: 0},
        compiler_params=pltpu.CompilerParams(vmem_limit_bytes=32 * 1024 * 1024),
        cost_estimate=pl.CostEstimate(flops=1, bytes_accessed=1, transcendentals=0),
        name="place_second",
    )(at, *blocks, first)


def place_rows_kernel(at, *refs):
    srcs, o_ref = refs[:-1], refs[-1]
    rows = srcs[0].shape[0]
    for j, ref in enumerate(srcs):
        o_ref[pl.ds(pl.multiple_of(at[j] * rows, 8), rows), :] = ref[...].astype(wide)


def place_rows(blocks, at, chunk):
    rows, width = blocks[0].shape
    n = len(blocks)
    return kernel(
        place_rows_kernel,
        "place_rows",
        at,
        blocks,
        (width // chunk,),
        [pl.BlockSpec((rows, chunk), lambda s, o=None: (0, s))] * n,
        pl.BlockSpec((n * rows, chunk), lambda s, o=None: (0, s)),
        shape_of((n * rows, width), wide),
    )


def place_last_kernel(count, halves, head_dim, steps, columns, at, *refs):
    firsts, seconds, lasts = refs[:count], refs[count : 2 * count], refs[2 * count : 3 * count]
    o_ref, out_ref = refs[3 * count :]
    heads = columns // (3 * head_dim) // halves
    s = pl.program_id(0)

    def put(d, block):
        for t in range(3):
            for h in range(halves):
                for u in range(heads):
                    end = ((t * halves + h) * count + d) * heads + u
                    start = (h * heads + u) * 3 + t
                    o_ref[:, end * head_dim : (end + 1) * head_dim] = block[
                        :, start * head_dim : (start + 1) * head_dim
                    ]

    for j in range(count):
        block = jnp.where(s < steps, firsts[j][...], seconds[j][...]).astype(wide)
        for d in range(count):
            pl.when(at[j] == d)(functools.partial(put, d, block))

    @pl.when(s == 0)
    def _():
        length = out_ref.shape[0] // count
        for j in range(count):
            value = lasts[j][...].astype(wide)
            width, side = columns, columns // 3
            at_row = pl.multiple_of(at[j] * length, 8)
            out_ref[pl.ds(at_row, length), :width] = value[:length, :width]
            rest = [value[length:, k * side : (k + 1) * side] for k in range(3)]
            out_ref[pl.ds(at_row, length), width:] = jnp.concatenate(rest, axis=0)


def place_last(firsts, seconds, at, halves, head_dim, rows, length, columns):
    count = len(firsts)
    cut, width = firsts[0].shape
    step = 96
    steps, total = cut // step, rows // step
    last = seconds[0].shape[0] - (rows - cut)
    assert last == rows - cut
    outs = [(rows, columns * count), (count * length, columns // 3 * 4)]
    return kernel(
        functools.partial(place_last_kernel, count, halves, head_dim, steps, columns),
        "place_last",
        at,
        [*firsts, *seconds, *seconds],
        (total,),
        [pl.BlockSpec((step, width), lambda s, o: (jnp.minimum(s, steps - 1), 0))] * count
        + [pl.BlockSpec((step, width), lambda s, o: (jnp.maximum(s - steps, 0), 0))] * count
        + [pl.BlockSpec((last, width), lambda s, o: (1, 0))] * count,
        [pl.BlockSpec((step, columns * count), lambda s, o: (s, 0)), whole(outs[1])],
        [shape_of(a, wide) for a in outs],
        megabytes=40,
    )


def program(sizes, tokens, condition, valid, positions, w_qkv, w_out, w_up, w_down, w_ada, qk_gain, cotangent):
    n_img, n_row, n_col = sizes
    images, tile_rows, tile_cols, width = tokens.shape
    assert images == n_row == 4 and n_col == 4
    tile = tile_rows * tile_cols
    own = n_row * tile
    head_dim = qk_gain.shape[1]
    my_heads = width // head_dim // n_col
    me_img, me_row, me_col = lax.axis_index("img"), lax.axis_index("row"), lax.axis_index("col")
    order_col, order_row = block_order(n_col), block_order(n_row)
    halves = 2
    paired = n_img == 2

    def integers(*values):
        return jnp.stack(values).astype(jnp.int32)

    steps = lax.dynamic_index_in_dim(positions, me_row, 1, keepdims=False)
    bit = me_row % 2
    at_col, at_img, at_columns, at_halves, live, at_tables, source = lax.optimization_barrier(
        (
            integers(me_col),
            integers(me_img if paired else jnp.zeros_like(me_img)),
            integers(*[me_col ^ j for j in order_col]),
            integers(1 - bit, bit),
            lax.dynamic_slice_in_dim(valid, me_row, 1, axis=0),
            jnp.concatenate(
                [
                    integers(steps[0, 1, 0] - steps[0, 0, 0], steps[1, 0, 1] - steps[1, 0, 0]),
                    jnp.arange(n_row, dtype=jnp.int32),
                    integers(*[me_col ^ j for j in order_col]),
                ]
            ),
            integers(*[(me_row ^ k) * n_col + (me_col ^ j) for j in order_col for k in order_row]),
        )
    )

    def x_swap(v):
        return swap(v, "img", 2, 1)

    def y_swap(v):
        return swap(v, "col", n_col, 2)

    def core_swap(v):
        return swap(v, "col", n_col, 1)

    def z_swaps(parts):
        return [parts[0]] + [swap(p, "row", n_row, k) for p, k in zip(parts[1:], order_row[1:])]

    def over_rows(v):
        return lax.all_to_all(v, "row", split_axis=0, concat_axis=0, tiled=True)

    if paired:
        part_qkv = cut_qkv(w_qkv, at_col, 3 * halves, n_col)
        other_qkv = x_swap(part_qkv)
    else:
        full = cut_qkv(lax.all_gather(w_qkv, "img", axis=0, tiled=True), at_col, 3 * halves, n_col)
        part_qkv, other_qkv = full[: width // 2], full[width // 2 :]
    tok_row = over_rows(after(tokens, part_qkv).reshape(images * tile, width))
    cond = condition.astype(wide)
    silu_cond = jax.nn.silu(cond).astype(low)
    mod_columns = jnp.dot(after(silu_cond, part_qkv), w_ada, preferred_element_type=wide)
    mod_span = mod_columns.shape[1]
    mod_z = z_swaps([lax.dynamic_slice_in_dim(mod_columns, me_row ^ k, 1, axis=0) for k in order_row])
    cos_all, sin_a, sin_b = tables(after(at_tables, mod_columns), n_row, n_col, tile, tile_cols, head_dim)
    gain = after(jnp.pad(qk_gain, ((0, 0), (0, LANES - head_dim))), at_col)
    t = cos_all
    if paired:
        part_up, part_out, part_down = cut_rest(w_up, w_out, w_down, after(at_col, mod_columns), 2 * halves, n_col)
        other_out, other_down = x_swap(part_out), x_swap(part_down)
        other_silu = x_swap(after(silu_cond, mod_columns))
        t = part_down
    mod_row = cat(*[after(m, cos_all, t) for m in mod_z])
    mod_y, mod_core = y_swap(mod_row), core_swap(mod_row)
    t = mod_row
    mod_y, mod_core = lax.optimization_barrier((mod_y, mod_core, t))[:2]
    mod_last = core_swap(mod_y)
    tok_row = after(tok_row, mod_y)
    tok_y, tok_core = y_swap(tok_row), core_swap(tok_row)
    cot_row = over_rows(after(cotangent, tok_row).reshape(images * tile, width))
    modulation = place_modulation([mod_row, mod_y, mod_core, after(mod_last, tok_row)], source).reshape(6, width)
    tok_core = after(tok_core, modulation)
    if paired:
        other_qkv = after(other_qkv, tok_core)
    w_qkv_mine = widen(part_qkv, other_qkv, at_img, head_dim)
    tok_y = after(tok_y, w_qkv_mine)
    if paired:
        other_out, other_down, tok_y, other_silu = lax.optimization_barrier((other_out, other_down, tok_y, other_silu))
        other_up = x_swap(after(part_up, other_down))
    tok_last = core_swap(tok_y)
    toks = [tok_row, tok_y, tok_core, tok_last]

    attn_in, joined = project_qkv(toks, modulation, w_qkv_mine)
    cot_row = after(cot_row, joined)
    cot_y, cot_core = y_swap(cot_row), core_swap(cot_row)
    mixed, aug = attn_fwd(after(joined, cot_row), cos_all, sin_a, sin_b, gain, head_dim)
    if paired:
        w_out_mine = widen_rows(part_out, after(other_out, joined), at_img, head_dim)
    else:

        def cut_rows(w):
            full = lax.all_gather(w, "img", axis=0, tiled=True)
            length = full.shape[0] // (halves * n_col)
            return [
                lax.dynamic_slice_in_dim(full, (h * n_col + me_col) * length, length, axis=0) for h in range(halves)
            ]

        w_out_mine = widen_rows(*cut_rows(w_out), at_img, head_dim)
        w_down_mine = cat(*cut_rows(w_down))
        full_up = lax.all_gather(w_up, "img", axis=0, tiled=True)
        piece = full_up.shape[1] // (2 * halves * n_col)
        w_up_mine = jnp.concatenate(
            [
                lax.dynamic_slice_in_dim(full_up, (p * n_col + me_col) * piece, piece, axis=1)
                for p in range(2 * halves)
            ],
            axis=1,
        )
    cot_y, cot_core, mixed = lax.optimization_barrier((cot_y, cot_core, mixed))
    if paired:
        mixed, other_up = lax.optimization_barrier((mixed, other_up))
    sent = project([mixed], w_out_mine, 2, 2, own, low)
    got = core_swap(sent)
    cot_last = core_swap(after(cot_y, sent))
    keep = project([after(mixed, sent)], w_out_mine, 0, 2, own, wide)
    got = after(got, keep)
    sent = add_second(keep, got)
    got_y = y_swap(sent)
    cots = [cot_row, cot_y, cot_core, after(cot_last, sent)]
    t = cots[3]
    if paired:
        w_up_mine, w_down_mine = join(part_up, after(other_up, t), part_down, after(other_down, t), at_img)
        t = w_up_mine
    attn_t, mixed_t = turn_blocks([after(attn_in, t), mixed], own)
    hidden, branch, mlp_own = middle(keep, got, after(got_y, attn_t), tok_row, modulation, live)
    mlp_y, mlp_core = y_swap(mlp_own), core_swap(mlp_own)
    mlp_y, mlp_core = lax.optimization_barrier((mlp_y, mlp_core))
    xs = [mlp_own, mlp_y, mlp_core, core_swap(mlp_y)]

    act, grad_gu, grad_mlp, sent, keep = feed_forward(xs, cots, modulation, w_up_mine, w_down_mine, live)
    got = core_swap(sent)

    class Piece:
        def __init__(self, theirs, mine):
            self.sent = theirs
            self.value, self.got = mine, x_swap(theirs)

        def z_one(self, *earlier):
            self.sent, self.keep = add_halves(self.value, after(self.got, *earlier), at_halves)
            self.got = swap(self.sent, "row", n_row, 1)
            return self.sent

        def z_two(self, *earlier):
            self.sent = (self.keep + after(self.got, *earlier).astype(wide)).astype(low)
            self.got = swap(self.sent, "row", n_row, 2)
            return self.sent

        def z_three(self, *earlier):
            other = after(self.got, *earlier)
            self.keep = (self.sent.astype(wide) + other.astype(wide)).astype(low)
            self.got = swap(self.keep, "row", n_row, 1)
            return self.keep

        def y(self, *earlier):
            self.value = join_halves(self.keep, after(self.got, *earlier), at_halves)
            self.got, self.core = y_swap(self.value), core_swap(self.value)
            return self.value

        def end(self, *earlier):
            self.got, self.core = lax.optimization_barrier((self.got, self.core) + earlier)[:2]
            self.last = core_swap(self.got)
            return self.got

        def blocks(self, *earlier):
            return [self.value, self.got, self.core, after(self.last, *earlier)]

    got = after(got, keep)
    sent = add_second(keep, got)
    got_y = y_swap(sent)
    t = sent
    if paired:
        d = Piece(*grad_part([after(act, t)], grad_mlp, at_img, 0, width, 384))
        half_up = grad_gu.shape[1] // 2
        u_one = Piece(*grad_part(xs, after(grad_gu, d.sent), at_img, 0, half_up, 384))
        u_two = Piece(*grad_part(xs, after(grad_gu, u_one.sent), at_img, half_up, half_up, 384))
        t = u_two.sent
    grad_hidden, gb_own, sums_two = middle_back(
        keep, got, after(got_y, t), hidden, branch, cot_row, modulation, live
    )
    gb_y, gb_core = y_swap(gb_own), core_swap(gb_own)
    mlp_sent = project([after(act, gb_own)], w_down_mine, 2, 2, own, low)
    mlp_got = core_swap(mlp_sent)
    mlp_keep = project([after(act, mlp_sent)], w_down_mine, 0, 2, own, wide)
    t = mlp_keep
    if paired:
        t = d.z_one(t)
    gb_y, gb_core = lax.optimization_barrier((gb_y, gb_core, t))[:2]
    gb_last = core_swap(gb_y)
    mlp_got = after(mlp_got, gb_y)
    mlp_next = add_second(mlp_keep, mlp_got)
    mlp_y = y_swap(mlp_next)
    gbs = [gb_own, gb_y, gb_core, after(gb_last, mlp_next)]
    heads_back = []

    def back_of(head, *earlier):
        heads_back.append(
            attn_bwd(
                gbs, after(joined, *earlier), aug, mixed, w_out_mine, cos_all, sin_a, sin_b, gain, head_dim, head, 1
            )
        )
        return heads_back[-1][0]

    t = back_of(0)
    if paired:
        t = d.z_two(t)
        t = u_one.z_one(t)
    t = back_of(1, t)
    out_own, sums_out = result(mlp_keep, mlp_got, after(mlp_y, t), hidden, cot_row, modulation, live)
    output = over_rows(out_own)
    t = out_own
    if paired:
        t = u_one.z_two(t)
        t = d.z_three(t)
        t = u_two.z_one(t)
    t = back_of(2, t)
    if paired:
        t = d.y(t)
    t = back_of(3, t)
    assert my_heads == 4
    if paired:
        t = u_one.z_three(t)
        t = u_two.z_two(t)
    grad_heads = [g for g, _ in heads_back]
    g_gain = sum(g for _, g in heads_back)
    if paired:
        rows = width // 2
        length = my_heads * head_dim // halves
        cut = (rows + length + length // 3) // 2
        g = grad_last(attn_t, grad_heads[:3] + [after(grad_heads[3], t)], mixed_t, gbs, at_img, head_dim, cut)
        q_one, q_two = Piece(g[0], g[1]), Piece(g[2], g[3])
        t = d.end(g[0])
    sent = project(grad_heads[:3] + [after(grad_heads[3], t)], w_qkv_mine, 2, 2, own, low)
    got = core_swap(sent)
    t = sent
    if paired:
        t = u_one.y(t)
    keep = project(grad_heads[:3] + [after(grad_heads[3], t)], w_qkv_mine, 0, 2, own, wide)
    got = after(got, keep)
    sent = add_second(keep, got)
    got_y = y_swap(sent)
    t = sent
    if paired:
        t = u_two.z_three(t)
        t = q_one.z_one(t)
    output = after(output, t)
    grad_own, sums_last = last_back(keep, got, after(got_y, output), tok_row, grad_hidden, modulation, live)
    t = grad_own
    if paired:
        t = u_two.y(t)
    grad_tokens = over_rows(after(grad_own, t))
    vector = (sums_two + sums_last + sums_out)[:6]
    got = core_swap(vector)
    t = vector
    if paired:
        t = q_one.z_two(t)
        t = q_two.z_one(t)
        t = u_one.end(t)
    vector = vector + after(got, t)
    got = y_swap(vector)
    t = vector
    if paired:
        sum_down = place_rows(d.blocks(t), at_columns, 384)
        t = sum_down
    grad_mod = (vector + after(got, t)).astype(low)
    blocks = grad_mod.reshape(n_row, n_col, mod_span)
    mine = lax.dynamic_slice_in_dim(blocks, at_col[0], 1, axis=1)[:, 0]
    share = over_rows(after(mine, grad_tokens))
    t = mine
    if paired:
        t = q_two.z_two(t)
        t = q_one.z_three(t)
        sum_up = place_first(u_one.blocks(t), at_columns, halves)
        t = sum_up
    share = after(share, t)
    back = lax.dot_general(share, w_ada, (((1,), (1,)), ((), ())), preferred_element_type=wide)
    flat = jnp.concatenate([back.reshape(-1), g_gain[:, :head_dim].reshape(-1)]).reshape(1, -1)
    got = swap(flat, "row", n_row, 1)
    t = flat
    if paired:
        other_share = x_swap(share)
        t = u_two.end(t)
        t = q_one.y(t)
    flat = flat + after(got, t)
    got = swap(flat, "row", n_row, 2)
    t = flat

    def outer_product(a, b):
        return lax.dot_general(a, b, (((0,), (0,)), ((), ())), preferred_element_type=wide)

    if paired:
        grad_ada = outer_product(silu_cond, share) + outer_product(other_silu, after(other_share, t))
        t = grad_ada
    else:
        grad_ada = outer_product(
            lax.all_gather(silu_cond, "img", axis=0, tiled=True), lax.all_gather(share, "img", axis=0, tiled=True)
        )
    flat = flat + after(got, t)
    got = core_swap(flat)
    t = flat
    if paired:
        t = q_two.z_three(t)
    flat = flat + after(got, t)
    got = y_swap(flat)
    t = flat
    grad_tokens = after(grad_tokens, t).astype(wide).reshape(tokens.shape)
    output = output.reshape(tokens.shape)
    t = grad_tokens
    if paired:
        sum_up = place_second(u_two.blocks(t), sum_up, at_columns, halves)
        t = sum_up
    flat = (flat + after(got, t))[0]
    grad_silu = flat[: images * width].reshape(images, width)
    gains = flat[images * width :].reshape(2, head_dim)
    s = 1.0 / (1.0 + jnp.exp(-cond))
    grad_condition = grad_silu * (s * (1.0 + cond * (1.0 - s)))
    if paired:
        gains_other = x_swap(gains)
        t = q_two.y(grad_condition)
        t = q_one.end(t)
        gains = gains + after(gains_other, t)
        t = q_two.end(gains)
        sum_qkv, sum_out = place_last(
            q_one.blocks(t),
            q_two.blocks(t),
            at_columns,
            halves,
            head_dim,
            rows,
            length,
            3 * my_heads * head_dim,
        )
    else:
        gains = lax.psum(gains, "img")

        def weight_grad(a, b):
            return lax.dot_general(a, b, (((0,), (0,)), ((), ())), preferred_element_type=wide).astype(low)

        def reduce_columns(partial, parts):
            summed = lax.psum_scatter(lax.psum(partial, "row"), "img", scatter_dimension=0, tiled=True)
            wholes = lax.all_gather(summed, "col", axis=0)
            rows = wholes.shape[1]
            wholes = wholes.reshape(n_col, rows, parts, -1)
            return jnp.transpose(wholes, (1, 2, 0, 3)).reshape(rows, -1).astype(wide)

        def reduce_rows(partial):
            wholes = lax.all_gather(lax.psum(partial, "row"), "col", axis=0)
            columns = wholes.shape[2]
            wholes = jnp.transpose(wholes.reshape(n_col, halves, -1, columns), (1, 0, 2, 3)).reshape(-1, columns)
            return lax.psum_scatter(wholes, "img", scatter_dimension=0, tiled=True).astype(wide)

        g_qkv = weight_grad(attn_in, jnp.concatenate(grad_heads, axis=1)).reshape(width, my_heads, 3, LANES)[..., :head_dim]
        g_qkv = jnp.swapaxes(g_qkv, 1, 2).reshape(width, -1)
        g_out = weight_grad(mixed, cat(*gbs)).reshape(my_heads, LANES, width)[:, :head_dim].reshape(-1, width)
        sum_up = reduce_columns(weight_grad(cat(*xs), grad_gu), 2 * halves)
        sum_down = reduce_rows(weight_grad(act, grad_mlp))
        sum_out = reduce_rows(g_out)
        sum_qkv = reduce_columns(g_qkv, 3 * halves)
    return output, grad_tokens, grad_condition, sum_qkv, sum_out, sum_up, sum_down, grad_ada, gains


def solution(mesh):
    sizes = tuple(mesh.shape[name] for name in ("img", "row", "col"))
    placed = (
        P("img", "row", "col", None),
        P("img", None),
        P("img"),
        P(None, "img", "row", "col"),
        P("img", None),
        P("img", None),
        P("img", None),
        P("img", None),
        P(None, ("row", "col")),
        P(),
        P("img", "row", "col", None),
    )
    return jax.shard_map(
        functools.partial(program, sizes),
        mesh=mesh,
        in_specs=placed,
        out_specs=(
            P("img", "row", "col", None),
            P("img", "row", "col", None),
            P("img", None),
            P("img", None),
            P("img", None),
            P("img", None),
            P("img", None),
            P(None, ("row", "col")),
            P(),
        ),
        check_vma=False,
    )
```

time: 1880 us -> 504 us (0.27)
  waiting for transfers between devices: 1370 us -> 144 us
  Pallas kernels: 0 us -> 182 us
  matrix products: 158 us -> 3.5 us
  local copies, waits for them, and re-layouts: 163 us -> 60.6 us
  blocking collectives: 89.9 us -> 0 us
  starting transfers between devices: 1.29 us -> 80.7 us
  other arithmetic: 69.4 us -> 22 us
    reduce_scatter x5 -> x0, waiting for transfers between devices: 478 us -> none  [the longest x1 164 us: shards(): lax.psum_scatter(grad_up.astype(jnp.bfloat16), 'img', scatter_dimension=0...]
    all_gather x6 -> x0, waiting for transfers between devices: 439 us -> none  [the longest x1 161 us: shards(): lax.all_gather(w_up, 'img', axis=0, tiled=True)]
    psum x2 -> x0, waiting for transfers between devices: 261 us -> none  [the longest x1 261 us: shards(): lax.psum(shard_qkv.astype(jnp.bfloat16), ('row', 'col')).astype(jnp.float32)]
    unnamed x17 -> x0, waiting for transfers between devices: 190 us -> none
    pallas_call x0 -> x47, Pallas kernels: none -> 182 us  [the longest x46 176 us: kernel(): pl.pallas_call(functools.partial(body, None) if none else body, grid_spec...]
    dot_general x43 -> x4, matrix products: 158 us -> 3.5 us  [the longest x2 2.9 us: outer_product(): lax.dot_general(a, b, (((0,), (0,)), ((), ())), preferred_element_type=wide)]
    ppermute x0 -> x74, waiting for transfers between devices: none -> 144 us  [swap(): return lax.ppermute(value, axis, [(a, a ^ bit) for a in range(size)])]
    psum x2 -> x0, blocking collectives: 66.4 us -> none  [the longest x1 61.5 us: shards(): lax.psum((grad_silu_part, grad_gain), ('row', 'col'))]
  transfers between devices with their start and end apart: 15 -> 79, of which waited for: 13 -> 27; matrix products, arithmetic and copies ran while one was open for 10% -> 6% of each run, Pallas kernels for 0% -> 29%
where the time goes in v2:
time: 504 us; the launch traced here: 497 us
  Pallas kernels  182 us (36%)
  waiting for transfers between devices  144 us (29%)
  starting transfers between devices  80.7 us (16%)
  local copies, waits for them, and re-layouts  60.6 us (12%)
  other arithmetic  22 us (4%)
    pallas_call x46, Pallas kernels, kernel(): pl.pallas_call(functools.partial(body, None) if none else body, grid_spec...  176 us
    ppermute x74, waiting for transfers between devices, swap(): return lax.ppermute(value, axis, [(a, a ^ bit) for a in range(size)])  144 us
    ppermute x74, starting transfers between devices, swap(): return lax.ppermute(value, axis, [(a, a ^ bit) for a in range(size)])  58.8 us
    unnamed x181, local copies, waits for them, and re-layouts  55.5 us
    all_to_all x5, starting transfers between devices, over_rows(): return lax.all_to_all(v, 'row', split_axis=0, concat_axis=0, tiled=True)  21.9 us
  transfers between devices with their start and end apart: 79, of which 27 were waited for; matrix products, arithmetic and copies ran while one was open for 6% of the time, Pallas kernels for 29%

profile of v2, /device:TPU:0, one launch (start us, length us, event | category | flops | bytes accessed | tf_op | source)
XLA Modules:
  0.0 497.0 jit_solution(3769085163908189296)
XLA Ops:
  12.1 4.9 all-to-all-start
  57.5 3.7 collective-permute-done.11
  63.0 5.2 %all-to-all-start.1 = ((bf16[4,64,1152]{2,1,0:T(8,128)(2,1)}), bf16[4,64,1152]{2,1,0:T(8,128)(2,1)S(1)}, u32[]{:S(2)}, u32[]{:S(2)}) async-start(bf16[4,64,1152]{2,1,0:T(8,128)(2,1)} %bitcast.67), calls=%async_computation.1 | async-start | bytes 1179648 | tf_op jit(solution)/shard_map/all_to_all | solution.py:1000
  73.6 6.9 %project_qkv.1 = (bf16[1024,1152]{1,0:T(8,128)(2,1)S(1)}, f32[1024,1536]{1,0:T(8,128)S(1)}) custom-call(bf16[256,1152]{1,0:T(8,128)(2,1)S(1)} %bitcast.63, bf16[256,1152]{1,0:T(8,128)(2,1)} %collective-permute-done.7.refs_1_, bf16[256,1152]{1,0:T(8,128)(2,1)S(1)} %copy-done.71, bf16[256,1152]{1,0:T(8,128)(2,1)S(1)} %collective-permute-done.12.refs_3_, ...), custom_call_target="tpu_custom_call" | custom-call | flops 1 | bytes 1 | tf_op jit(solution)/shard_map/project_qkv/pallas_call | solution.py:57
  88.9 13.2 %attn_fwd.1 = (bf16[1024,512]{1,0:T(8,128)(2,1)}, bf16[1024,1536]{1,0:T(8,128)(2,1)}) custom-call(f32[1024,1536]{1,0:T(8,128)} %copy-done.1, f32[1024,128]{1,0:T(8,128)} %copy-done.18, f32[1024,128]{1,0:T(8,128)} %copy-done.19, f32[1024,128]{1,0:T(8,128)} %copy-done.20, f32[2,128]{1,0:T(2,128)} %pad.4.gain_ref.refs_11_), custom_call_target="tpu_custom_call" | custom-call | flops 1 | bytes 1 | tf_op jit(solution)/shard_map/attn_fwd/pallas_call | solution.py:57
  117.7 6.3 %collective-permute-done.17.y_ref = bf16[256,1152]{1,0:T(8,128)(2,1)S(1)} collective-permute-done((bf16[256,1152]{1,0:T(8,128)(2,1)S(1)}, bf16[256,1152]{1,0:T(8,128)(2,1)S(1)}, u32[]{:S(2)}, u32[]{:S(2)}) %collective-permute-start.17) | collective-permute-done | bytes 589856 | tf_op jit(solution)/shard_map/ppermute | solution.py:28
  126.0 14.3 %collective-permute-done.19.refs_1_ = bf16[256,1152]{1,0:T(8,128)(2,1)S(1)} collective-permute-done((bf16[256,1152]{1,0:T(8,128)(2,1)S(1)}, bf16[256,1152]{1,0:T(8,128)(2,1)S(1)}, u32[]{:S(2)}, u32[]{:S(2)}) %collective-permute-start.19) | collective-permute-done | bytes 589856 | tf_op jit(solution)/shard_map/ppermute | solution.py:28
  142.4 18.4 %feed_forward.1 = (bf16[1024,768]{1,0:T(8,128)(2,1)}, bf16[1024,1536]{1,0:T(8,128)(2,1)}, bf16[1024,1152]{1,0:T(8,128)(2,1)}, bf16[512,1152]{1,0:T(8,128)(2,1)S(1)}, f32[512,1152]{1,0:T(8,128)}) custom-call(s32[1]{0:T(128)} %dynamic_slice.22.live, bf16[256,1152]{1,0:T(8,128)(2,1)S(1)} %get-tuple-element.237.refs_0_, ...), custom_call_target="tpu_custom_call" | custom-call | flops 1 | bytes 1 | tf_op jit(solution)/shard_map/feed_forward/pallas_call | solution.py:57
  167.5 4.1 grad_part.3
  171.9 5.1 %grad_part.4 = (bf16[576,768]{1,0:T(8,128)(2,1)}, bf16[576,768]{1,0:T(8,128)(2,1)S(1)}) custom-call(s32[1]{0:T(128)} %bitcast.1.at, bf16[256,1152]{1,0:T(8,128)(2,1)S(1)} %get-tuple-element.237.refs_0_, bf16[256,1152]{1,0:T(8,128)(2,1)S(1)} %collective-permute-done.19.refs_1_, bf16[256,1152]{1,0:T(8,128)(2,1)S(1)} %collective-permute-done.20.refs_2_, ...), custom_call_target="tpu_custom_call" | custom-call | flops 1 | bytes 1 | tf_op jit(solution)/shard_map/grad_part/pallas_call | solution.py:57
  178.0 4.7 grad_part.5
  195.2 4.7 collective-permute-done.25.refs_1_.refs_7_
  207.0 8.6 %attn_bwd.4 = (bf16[1024,384]{1,0:T(8,128)(2,1)}, f32[2,128]{1,0:T(2,128)}) custom-call(bf16[256,1152]{1,0:T(8,128)(2,1)} %copy-done.11, bf16[256,1152]{1,0:T(8,128)(2,1)} %copy-done.13, bf16[256,1152]{1,0:T(8,128)(2,1)} %copy-done.15, bf16[256,1152]{1,0:T(8,128)(2,1)} %copy-done.80, f32[1024,1536]{1,0:T(8,128)} %copy-done.1, ...), custom_call_target="tpu_custom_call" | custom-call | flops 1 | bytes 1 | tf_op jit(solution)/shard_map/attn_bwd/pallas_call | solution.py:57
  217.9 7.3 %collective-permute-done.30.b_ref = bf16[576,768]{1,0:T(8,128)(2,1)} collective-permute-done((bf16[576,768]{1,0:T(8,128)(2,1)}, bf16[576,768]{1,0:T(8,128)(2,1)}, u32[]{:S(2)}, u32[]{:S(2)}) %collective-permute-start.30) | collective-permute-done | bytes 884768 | tf_op jit(solution)/shard_map/ppermute | solution.py:28
  232.7 8.7 %attn_bwd.5 = (bf16[1024,384]{1,0:T(8,128)(2,1)}, f32[2,128]{1,0:T(2,128)}) custom-call(bf16[256,1152]{1,0:T(8,128)(2,1)} %copy-done.11, bf16[256,1152]{1,0:T(8,128)(2,1)} %copy-done.13, bf16[256,1152]{1,0:T(8,128)(2,1)} %copy-done.15, bf16[256,1152]{1,0:T(8,128)(2,1)} %copy-done.80, f32[1024,1536]{1,0:T(8,128)} %copy-done.1, ...), custom_call_target="tpu_custom_call" | custom-call | flops 1 | bytes 1 | tf_op jit(solution)/shard_map/attn_bwd/pallas_call | solution.py:57
  258.1 8.8 %attn_bwd.6 = (bf16[1024,384]{1,0:T(8,128)(2,1)}, f32[2,128]{1,0:T(2,128)}) custom-call(bf16[256,1152]{1,0:T(8,128)(2,1)} %copy-done.11, bf16[256,1152]{1,0:T(8,128)(2,1)} %copy-done.13, bf16[256,1152]{1,0:T(8,128)(2,1)} %copy-done.15, bf16[256,1152]{1,0:T(8,128)(2,1)} %copy-done.80, f32[1024,1536]{1,0:T(8,128)} %copy-done.1, ...), custom_call_target="tpu_custom_call" | custom-call | flops 1 | bytes 1 | tf_op jit(solution)/shard_map/attn_bwd/pallas_call | solution.py:57
  266.8 5.4 %collective-permute-done.35.b_ref = bf16[192,1152]{1,0:T(8,128)(2,1)S(1)} collective-permute-done((bf16[192,1152]{1,0:T(8,128)(2,1)S(1)}, bf16[192,1152]{1,0:T(8,128)(2,1)S(1)}, u32[]{:S(2)}, u32[]{:S(2)}) %collective-permute-start.35) | collective-permute-done | bytes 442400 | tf_op jit(solution)/shard_map/ppermute | solution.py:28
  274.1 8.6 %attn_bwd.7 = (bf16[1024,384]{1,0:T(8,128)(2,1)}, f32[2,128]{1,0:T(2,128)}) custom-call(bf16[256,1152]{1,0:T(8,128)(2,1)} %copy-done.11, bf16[256,1152]{1,0:T(8,128)(2,1)} %copy-done.13, bf16[256,1152]{1,0:T(8,128)(2,1)} %copy-done.15, bf16[256,1152]{1,0:T(8,128)(2,1)} %copy-done.80, f32[1024,1536]{1,0:T(8,128)} %copy-done.1, ...), custom_call_target="tpu_custom_call" | custom-call | flops 1 | bytes 1 | tf_op jit(solution)/shard_map/attn_bwd/pallas_call | solution.py:57
  287.8 14.3 %grad_last.1 = (bf16[384,896]{1,0:T(8,128)(2,1)}, bf16[384,896]{1,0:T(8,128)(2,1)}, bf16[384,896]{1,0:T(8,128)(2,1)}, bf16[384,896]{1,0:T(8,128)(2,1)}) custom-call(s32[1]{0:T(128)} %bitcast.1.at, bf16[1152,1024]{1,0:T(8,128)(2,1)} %copy-done.46, bf16[512,1024]{1,0:T(8,128)(2,1)} %copy-done.56, bf16[1024,384]{1,0:T(8,128)(2,1)} %get-tuple-element.271.refs_2_.refs_0_, ...), custom_call_target="tpu_custom_call" | custom-call | flops 1 | bytes 1 | tf_op jit(solution)/shard_map/grad_last/pallas_call | solution.py:57
  302.2 4.0 project.10
  309.4 4.4 all-to-all-start.2
  313.8 13.6 %collective-permute-done.40.b_ref = bf16[288,768]{1,0:T(8,128)(2,1)S(1)} collective-permute-done((bf16[288,768]{1,0:T(8,128)(2,1)S(1)}, bf16[288,768]{1,0:T(8,128)(2,1)S(1)}, u32[]{:S(2)}, u32[]{:S(2)}) %collective-permute-start.40) | collective-permute-done | bytes 442400 | tf_op jit(solution)/shard_map/ppermute | solution.py:28
  349.3 8.0 %collective-permute-done.44.y_ref = bf16[256,1152]{1,0:T(8,128)(2,1)} collective-permute-done((bf16[256,1152]{1,0:T(8,128)(2,1)}, bf16[256,1152]{1,0:T(8,128)(2,1)}, u32[]{:S(2)}, u32[]{:S(2)}) %collective-permute-start.44) | collective-permute-done | bytes 589856 | tf_op jit(solution)/shard_map/ppermute | solution.py:28
  362.5 12.5 %collective-permute-done.45.b_ref = bf16[288,768]{1,0:T(8,128)(2,1)S(1)} collective-permute-done((bf16[288,768]{1,0:T(8,128)(2,1)S(1)}, bf16[288,768]{1,0:T(8,128)(2,1)S(1)}, u32[]{:S(2)}, u32[]{:S(2)}) %collective-permute-start.45) | collective-permute-done | bytes 442400 | tf_op jit(solution)/shard_map/ppermute | solution.py:28
  380.2 4.1 all-to-all-start.3
  392.2 5.3 %place_rows.1 = f32[1536,1152]{1,0:T(8,128)} custom-call(s32[4]{0:T(128)S(1)} %pad_add_fusion.at, bf16[384,1152]{1,0:T(8,128)(2,1)S(1)} %copy-done.45, bf16[384,1152]{1,0:T(8,128)(2,1)} %collective-permute-done.41.refs_1_, bf16[384,1152]{1,0:T(8,128)(2,1)} %collective-permute-done.42.refs_2_, bf16[384,1152]{1,0:T(8,128)(2,1)} %collective-permute-done.52.refs_3_), custom_call_target="tpu_custom_call" | custom-call | flops 1 | bytes 1 | tf_op jit(solution)/shard_map/place_rows/pallas_call | solution.py:57
  399.3 10.5 %collective-permute-done.55 = bf16[192,896]{1,0:T(8,128)(2,1)} collective-permute-done((bf16[192,896]{1,0:T(8,128)(2,1)}, bf16[192,896]{1,0:T(8,128)(2,1)}, u32[]{:S(2)}, u32[]{:S(2)}) %collective-permute-start.55) | collective-permute-done | bytes 344096 | tf_op jit(solution)/shard_map/ppermute | solution.py:28
  411.6 12.2 %collective-permute-done.54 = bf16[192,896]{1,0:T(8,128)(2,1)} collective-permute-done((bf16[192,896]{1,0:T(8,128)(2,1)}, bf16[192,896]{1,0:T(8,128)(2,1)}, u32[]{:S(2)}, u32[]{:S(2)}) %collective-permute-start.54) | collective-permute-done | bytes 344096 | tf_op jit(solution)/shard_map/ppermute | solution.py:28
  432.1 6.1 %place_first.1.refs_4_ = f32[576,6144]{1,0:T(8,128)} custom-call(s32[4]{0:T(128)S(1)} %pad_add_fusion.at, bf16[576,768]{1,0:T(8,128)(2,1)} %join_halves.6.refs_0_, bf16[576,768]{1,0:T(8,128)(2,1)} %collective-permute-done.47.refs_1_, bf16[576,768]{1,0:T(8,128)(2,1)} %collective-permute-done.48.refs_2_, bf16[576,768]{1,0:T(8,128)(2,1)} %collective-permute-done.53.refs_3_), custom_call_target="tpu_custom_call" | custom-call | flops 1 | bytes 1 | tf_op jit(solution)/shard_map/place_first/pallas_call | solution.py:57
  453.7 5.5 %place_second.1 = f32[576,6144]{1,0:T(8,128)} custom-call(s32[4]{0:T(128)S(1)} %pad_add_fusion.at, bf16[576,768]{1,0:T(8,128)(2,1)S(1)} %join_halves.7.refs_0_, bf16[576,768]{1,0:T(8,128)(2,1)} %collective-permute-done.58.refs_1_, bf16[576,768]{1,0:T(8,128)(2,1)} %collective-permute-done.59.refs_2_, ...), custom_call_target="tpu_custom_call", output_to_operand_aliasing={{}: (5, {})} | custom-call | flops 1 | bytes 1 | tf_op jit(solution)/shard_map/place_second/pallas_call | solution.py:857
  468.8 13.3 %collective-permute-done.70.refs_5_.refs_9_ = bf16[384,896]{1,0:T(8,128)(2,1)S(1)} collective-permute-done((bf16[384,896]{1,0:T(8,128)(2,1)S(1)}, bf16[384,896]{1,0:T(8,128)(2,1)S(1)}, u32[]{:S(2)}, u32[]{:S(2)}) %collective-permute-start.70) | collective-permute-done | bytes 688160 | tf_op jit(solution)/shard_map/ppermute | solution.py:28
  484.3 10.4 %place_last.1 = (f32[576,3456]{1,0:T(8,128)}, f32[576,1152]{1,0:T(8,128)}) custom-call(s32[4]{0:T(128)S(1)} %pad_add_fusion.at, bf16[384,896]{1,0:T(8,128)(2,1)S(1)} %join_halves.8.refs_0_, bf16[384,896]{1,0:T(8,128)(2,1)} %collective-permute-done.66.refs_1_, bf16[384,896]{1,0:T(8,128)(2,1)} %collective-permute-done.67.refs_2_, ...), custom_call_target="tpu_custom_call" | custom-call | flops 1 | bytes 1 | tf_op jit(solution)/shard_map/place_last/pallas_call | solution.py:57
  (404 shorter events, 228.9 us)
Async XLA Ops:
  9.1 40.2 %collective-permute-start.8 = (bf16[576,864]{1,0:T(8,128)(2,1)S(1)}, bf16[576,864]{1,0:T(8,128)(2,1)}, u32[]{:S(2)}, u32[]{:S(2)}) collective-permute-start(bf16[576,864]{1,0:T(8,128)(2,1)S(1)} %cut_qkv.1.mine_ref), channel_id=1, source_target_pairs={{0,16},{16,0},{1,17},{17,1},{2,18},{18,2},{3,19},{19,3},{4,20},{20... | collective-permute-start | bytes 2985992 | tf_op jit(solution)/shard_map/ppermute | solution.py:28
  12.1 29.5 %all-to-all-start = ((bf16[4,64,1152]{2,1,0:T(8,128)(2,1)}), bf16[4,64,1152]{2,1,0:T(8,128)(2,1)S(1)}, u32[]{:S(2)}, u32[]{:S(2)}) async-start(bf16[4,64,1152]{2,1,0:T(8,128)(2,1)} %bitcast.26), calls=%async_computation | async-start | bytes 1179648 | tf_op jit(solution)/shard_map/all_to_all | solution.py:1000
  26.6 34.7 %collective-permute-start.6 = (bf16[384,1152]{1,0:T(8,128)(2,1)S(1)}, bf16[384,1152]{1,0:T(8,128)(2,1)}, u32[]{:S(2)}, u32[]{:S(2)}) collective-permute-start(bf16[384,1152]{1,0:T(8,128)(2,1)S(1)} %get-tuple-element.192.c_ref), channel_id=1, source_target_pairs={{0,16},{16,0},{1,17},{17,1},{2,18},{18,2},{3,19},{19,3},{4,20},{20... | collective-permute-start | bytes 2654216 | tf_op jit(solution)/shard_map/ppermute | solution.py:28
  61.3 40.8 %collective-permute-start.15 = (bf16[576,1536]{1,0:T(8,128)(2,1)}, bf16[576,1536]{1,0:T(8,128)(2,1)}, u32[]{:S(2)}, u32[]{:S(2)}) collective-permute-start(bf16[576,1536]{1,0:T(8,128)(2,1)} %get-tuple-element.220.a_ref), channel_id=1, source_target_pairs={{0,16},{16,0},{1,17},{17,1},{2,18},{18,2},{3,19},{19,3},{4,20},{20... | collective-permute-start | bytes 5308424 | tf_op jit(solution)/shard_map/ppermute | solution.py:28
  63.0 21.6 %all-to-all-start.1 = ((bf16[4,64,1152]{2,1,0:T(8,128)(2,1)}), bf16[4,64,1152]{2,1,0:T(8,128)(2,1)S(1)}, u32[]{:S(2)}, u32[]{:S(2)}) async-start(bf16[4,64,1152]{2,1,0:T(8,128)(2,1)} %bitcast.67), calls=%async_computation.1 | async-start | bytes 1179648 | tf_op jit(solution)/shard_map/all_to_all | solution.py:1000
  171.6 21.7 %collective-permute-start.27 = (bf16[384,1152]{1,0:T(8,128)(2,1)S(1)}, bf16[384,1152]{1,0:T(8,128)(2,1)S(1)}, u32[]{:S(2)}, u32[]{:S(2)}) collective-permute-start(bf16[384,1152]{1,0:T(8,128)(2,1)S(1)} %get-tuple-element.249), channel_id=1, source_target_pairs={{0,16},{16,0},{1,17},{17,1},{2,18},{18,2},{3,19},{19,3},{4,20},{20... | collective-permute-start | bytes 2654216 | tf_op jit(solution)/shard_map/ppermute | solution.py:28
  203.1 22.1 %collective-permute-start.30 = (bf16[576,768]{1,0:T(8,128)(2,1)}, bf16[576,768]{1,0:T(8,128)(2,1)}, u32[]{:S(2)}, u32[]{:S(2)}) collective-permute-start(bf16[576,768]{1,0:T(8,128)(2,1)} %get-tuple-element.251), channel_id=1, source_target_pairs={{0,16},{16,0},{1,17},{17,1},{2,18},{18,2},{3,19},{19,3},{4,20},{20... | collective-permute-start | bytes 2654216 | tf_op jit(solution)/shard_map/ppermute | solution.py:28
  205.8 35.7 %collective-permute-start.28 = (bf16[256,1152]{1,0:T(8,128)(2,1)}, bf16[256,1152]{1,0:T(8,128)(2,1)}, u32[]{:S(2)}, u32[]{:S(2)}) collective-permute-start(bf16[256,1152]{1,0:T(8,128)(2,1)} %add_second.6), channel_id=1, source_target_pairs={{0,2},{1,3},{2,0},{3,1},{4,6},{5,7},{6,4},{7,5},{8,10},{9,11},{10,... | collective-permute-start | bytes 1769480 | tf_op jit(solution)/shard_map/ppermute | solution.py:28
  228.3 21.1 %collective-permute-start.34 = (bf16[288,768]{1,0:T(8,128)(2,1)S(1)}, bf16[288,768]{1,0:T(8,128)(2,1)}, u32[]{:S(2)}, u32[]{:S(2)}) collective-permute-start(bf16[288,768]{1,0:T(8,128)(2,1)S(1)} %get-tuple-element.274), channel_id=1, source_target_pairs={{0,4},{4,0},{8,12},{12,8},{1,5},{5,1},{9,13},{13,9},{2,6},{6,2},{1... | collective-permute-start | bytes 1327112 | tf_op jit(solution)/shard_map/ppermute | solution.py:28
  228.6 22.7 %collective-permute-start.33 = (bf16[192,1152]{1,0:T(8,128)(2,1)}, bf16[192,1152]{1,0:T(8,128)(2,1)}, u32[]{:S(2)}, u32[]{:S(2)}) collective-permute-start(bf16[192,1152]{1,0:T(8,128)(2,1)} %add_convert_fusion.5), channel_id=1, source_target_pairs={{0,8},{4,12},{8,0},{12,4},{1,9},{5,13},{9,1},{13,5},{2,10},{6,14},... | collective-permute-start | bytes 1327112 | tf_op jit(solution)/shard_map/ppermute | solution.py:28
  231.2 24.7 %collective-permute-start.32 = (bf16[576,768]{1,0:T(8,128)(2,1)}, bf16[576,768]{1,0:T(8,128)(2,1)}, u32[]{:S(2)}, u32[]{:S(2)}) collective-permute-start(bf16[576,768]{1,0:T(8,128)(2,1)} %get-tuple-element.253), channel_id=1, source_target_pairs={{0,16},{16,0},{1,17},{17,1},{2,18},{18,2},{3,19},{19,3},{4,20},{20... | collective-permute-start | bytes 2654216 | tf_op jit(solution)/shard_map/ppermute | solution.py:28
  252.5 19.7 %collective-permute-start.35 = (bf16[192,1152]{1,0:T(8,128)(2,1)S(1)}, bf16[192,1152]{1,0:T(8,128)(2,1)S(1)}, u32[]{:S(2)}, u32[]{:S(2)}) collective-permute-start(bf16[192,1152]{1,0:T(8,128)(2,1)S(1)} %add_convert_fusion.3.a_ref), channel_id=1, source_target_pairs={{0,4},{4,0},{8,12},{12,8},{1,5},{5,1},{9,13},{13,9},{2,6},{6,2},{1... | collective-permute-start | bytes 1327112 | tf_op jit(solution)/shard_map/ppermute | solution.py:28
  253.1 29.7 %collective-permute-start.37 = (bf16[288,768]{1,0:T(8,128)(2,1)}, bf16[288,768]{1,0:T(8,128)(2,1)}, u32[]{:S(2)}, u32[]{:S(2)}) collective-permute-start(bf16[288,768]{1,0:T(8,128)(2,1)} %add_convert_fusion.4), channel_id=1, source_target_pairs={{0,8},{4,12},{8,0},{12,4},{1,9},{5,13},{9,1},{13,5},{2,10},{6,14},... | collective-permute-start | bytes 1327112 | tf_op jit(solution)/shard_map/ppermute | solution.py:28
  273.1 29.0 %collective-permute-start.41 = (bf16[384,1152]{1,0:T(8,128)(2,1)S(1)}, bf16[384,1152]{1,0:T(8,128)(2,1)}, u32[]{:S(2)}, u32[]{:S(2)}) collective-permute-start(bf16[384,1152]{1,0:T(8,128)(2,1)S(1)} %join_halves.5.refs_0_), channel_id=1, source_target_pairs={{0,2},{1,3},{2,0},{3,1},{4,6},{5,7},{6,4},{7,5},{8,10},{9,11},{10,... | collective-permute-start | bytes 2654216 | tf_op jit(solution)/shard_map/ppermute | solution.py:28
  274.1 28.1 %collective-permute-start.42 = (bf16[384,1152]{1,0:T(8,128)(2,1)S(1)}, bf16[384,1152]{1,0:T(8,128)(2,1)}, u32[]{:S(2)}, u32[]{:S(2)}) collective-permute-start(bf16[384,1152]{1,0:T(8,128)(2,1)S(1)} %join_halves.5.refs_0_), channel_id=1, source_target_pairs={{0,1},{1,0},{2,3},{3,2},{4,5},{5,4},{6,7},{7,6},{8,9},{9,8},{10,11... | collective-permute-start | bytes 2654216 | tf_op jit(solution)/shard_map/ppermute | solution.py:28
  306.2 32.5 %collective-permute-start.43 = (bf16[512,1152]{1,0:T(8,128)(2,1)}, bf16[512,1152]{1,0:T(8,128)(2,1)}, u32[]{:S(2)}, u32[]{:S(2)}) collective-permute-start(bf16[512,1152]{1,0:T(8,128)(2,1)} %project.10), channel_id=1, source_target_pairs={{0,1},{1,0},{2,3},{3,2},{4,5},{5,4},{6,7},{7,6},{8,9},{9,8},{10,11... | collective-permute-start | bytes 3538952 | tf_op jit(solution)/shard_map/ppermute | solution.py:28
  306.2 21.3 %collective-permute-start.40 = (bf16[288,768]{1,0:T(8,128)(2,1)S(1)}, bf16[288,768]{1,0:T(8,128)(2,1)S(1)}, u32[]{:S(2)}, u32[]{:S(2)}) collective-permute-start(bf16[288,768]{1,0:T(8,128)(2,1)S(1)} %add_convert_fusion.2.a_ref), channel_id=1, source_target_pairs={{0,4},{4,0},{8,12},{12,8},{1,5},{5,1},{9,13},{13,9},{2,6},{6,2},{1... | collective-permute-start | bytes 1327112 | tf_op jit(solution)/shard_map/ppermute | solution.py:28
  306.5 35.2 %collective-permute-start.39 = (bf16[288,768]{1,0:T(8,128)(2,1)}, bf16[288,768]{1,0:T(8,128)(2,1)}, u32[]{:S(2)}, u32[]{:S(2)}) collective-permute-start(bf16[288,768]{1,0:T(8,128)(2,1)} %add_convert_fusion.1), channel_id=1, source_target_pairs={{0,8},{4,12},{8,0},{12,4},{1,9},{5,13},{9,1},{13,5},{2,10},{6,14},... | collective-permute-start | bytes 1327112 | tf_op jit(solution)/shard_map/ppermute | solution.py:28
  308.4 35.4 %collective-permute-start.38 = (bf16[384,896]{1,0:T(8,128)(2,1)}, bf16[384,896]{1,0:T(8,128)(2,1)}, u32[]{:S(2)}, u32[]{:S(2)}) collective-permute-start(bf16[384,896]{1,0:T(8,128)(2,1)} %get-tuple-element.296), channel_id=1, source_target_pairs={{0,16},{16,0},{1,17},{17,1},{2,18},{18,2},{3,19},{19,3},{4,20},{20... | collective-permute-start | bytes 2064392 | tf_op jit(solution)/shard_map/ppermute | solution.py:28
  309.4 39.9 %all-to-all-start.2 = ((bf16[4,64,1152]{2,1,0:T(8,128)(2,1)}), bf16[4,64,1152]{2,1,0:T(8,128)(2,1)}, u32[]{:S(2)}, u32[]{:S(2)}) async-start(bf16[4,64,1152]{2,1,0:T(8,128)(2,1)} %bitcast.30), calls=%async_computation.2 | async-start | bytes 1179648 | tf_op jit(solution)/shard_map/all_to_all | solution.py:1000
  347.3 32.9 %collective-permute-start.47 = (bf16[576,768]{1,0:T(8,128)(2,1)}, bf16[576,768]{1,0:T(8,128)(2,1)}, u32[]{:S(2)}, u32[]{:S(2)}) collective-permute-start(bf16[576,768]{1,0:T(8,128)(2,1)} %join_halves.6.refs_0_), channel_id=1, source_target_pairs={{0,2},{1,3},{2,0},{3,1},{4,6},{5,7},{6,4},{7,5},{8,10},{9,11},{10,... | collective-permute-start | bytes 2654216 | tf_op jit(solution)/shard_map/ppermute | solution.py:28
  348.3 31.9 %collective-permute-start.48 = (bf16[576,768]{1,0:T(8,128)(2,1)}, bf16[576,768]{1,0:T(8,128)(2,1)}, u32[]{:S(2)}, u32[]{:S(2)}) collective-permute-start(bf16[576,768]{1,0:T(8,128)(2,1)} %join_halves.6.refs_0_), channel_id=1, source_target_pairs={{0,1},{1,0},{2,3},{3,2},{4,5},{5,4},{6,7},{7,6},{8,9},{9,8},{10,11... | collective-permute-start | bytes 2654216 | tf_op jit(solution)/shard_map/ppermute | solution.py:28
  348.3 29.3 %collective-permute-start.49 = (bf16[384,896]{1,0:T(8,128)(2,1)}, bf16[384,896]{1,0:T(8,128)(2,1)}, u32[]{:S(2)}, u32[]{:S(2)}) collective-permute-start(bf16[384,896]{1,0:T(8,128)(2,1)} %get-tuple-element.315), channel_id=1, source_target_pairs={{0,16},{16,0},{1,17},{17,1},{2,18},{18,2},{3,19},{19,3},{4,20},{20... | collective-permute-start | bytes 2064392 | tf_op jit(solution)/shard_map/ppermute | solution.py:28
  357.3 33.9 %collective-permute-start.52 = (bf16[384,1152]{1,0:T(8,128)(2,1)}, bf16[384,1152]{1,0:T(8,128)(2,1)}, u32[]{:S(2)}, u32[]{:S(2)}) collective-permute-start(bf16[384,1152]{1,0:T(8,128)(2,1)} %collective-permute-done.41.refs_1_), channel_id=1, source_target_pairs={{0,1},{1,0},{2,3},{3,2},{4,5},{5,4},{6,7},{7,6},{8,9},{9,8},{10,11... | collective-permute-start | bytes 2654216 | tf_op jit(solution)/shard_map/ppermute | solution.py:28
  380.2 43.6 %all-to-all-start.3 = ((bf16[4,64,1152]{2,1,0:T(8,128)(2,1)}), bf16[4,64,1152]{2,1,0:T(8,128)(2,1)}, u32[]{:S(2)}, u32[]{:S(2)}) async-start(bf16[4,64,1152]{2,1,0:T(8,128)(2,1)} %bitcast.66), calls=%async_computation.3 | async-start | bytes 1179648 | tf_op jit(solution)/shard_map/all_to_all | solution.py:1000
  386.9 22.9 %collective-permute-start.55 = (bf16[192,896]{1,0:T(8,128)(2,1)}, bf16[192,896]{1,0:T(8,128)(2,1)}, u32[]{:S(2)}, u32[]{:S(2)}) collective-permute-start(bf16[192,896]{1,0:T(8,128)(2,1)} %copy-done.79), channel_id=1, source_target_pairs={{0,4},{4,0},{8,12},{12,8},{1,5},{5,1},{9,13},{13,9},{2,6},{6,2},{1... | collective-permute-start | bytes 1032200 | tf_op jit(solution)/shard_map/ppermute | solution.py:28
  388.9 34.9 %collective-permute-start.54 = (bf16[192,896]{1,0:T(8,128)(2,1)}, bf16[192,896]{1,0:T(8,128)(2,1)}, u32[]{:S(2)}, u32[]{:S(2)}) collective-permute-start(bf16[192,896]{1,0:T(8,128)(2,1)} %add_convert_fusion.9), channel_id=1, source_target_pairs={{0,8},{4,12},{8,0},{12,4},{1,9},{5,13},{9,1},{13,5},{2,10},{6,14},... | collective-permute-start | bytes 1032200 | tf_op jit(solution)/shard_map/ppermute | solution.py:28
  391.2 40.9 %collective-permute-start.53 = (bf16[576,768]{1,0:T(8,128)(2,1)}, bf16[576,768]{1,0:T(8,128)(2,1)}, u32[]{:S(2)}, u32[]{:S(2)}) collective-permute-start(bf16[576,768]{1,0:T(8,128)(2,1)} %collective-permute-done.47.refs_1_), channel_id=1, source_target_pairs={{0,1},{1,0},{2,3},{3,2},{4,5},{5,4},{6,7},{7,6},{8,9},{9,8},{10,11... | collective-permute-start | bytes 2654216 | tf_op jit(solution)/shard_map/ppermute | solution.py:28
  391.2 47.9 %collective-permute-start.58 = (bf16[576,768]{1,0:T(8,128)(2,1)S(1)}, bf16[576,768]{1,0:T(8,128)(2,1)}, u32[]{:S(2)}, u32[]{:S(2)}) collective-permute-start(bf16[576,768]{1,0:T(8,128)(2,1)S(1)} %join_halves.7.refs_0_), channel_id=1, source_target_pairs={{0,2},{1,3},{2,0},{3,1},{4,6},{5,7},{6,4},{7,5},{8,10},{9,11},{10,... | collective-permute-start | bytes 2654216 | tf_op jit(solution)/shard_map/ppermute | solution.py:28
  398.2 42.1 %collective-permute-start.59 = (bf16[576,768]{1,0:T(8,128)(2,1)S(1)}, bf16[576,768]{1,0:T(8,128)(2,1)}, u32[]{:S(2)}, u32[]{:S(2)}) collective-permute-start(bf16[576,768]{1,0:T(8,128)(2,1)S(1)} %join_halves.7.refs_0_), channel_id=1, source_target_pairs={{0,1},{1,0},{2,3},{3,2},{4,5},{5,4},{6,7},{7,6},{8,9},{9,8},{10,11... | collective-permute-start | bytes 2654216 | tf_op jit(solution)/shard_map/ppermute | solution.py:28
  411.6 35.9 %collective-permute-start.63 = (bf16[192,896]{1,0:T(8,128)(2,1)}, bf16[192,896]{1,0:T(8,128)(2,1)}, u32[]{:S(2)}, u32[]{:S(2)}) collective-permute-start(bf16[192,896]{1,0:T(8,128)(2,1)} %add_convert_fusion.8), channel_id=1, source_target_pairs={{0,8},{4,12},{8,0},{12,4},{1,9},{5,13},{9,1},{13,5},{2,10},{6,14},... | collective-permute-start | bytes 1032200 | tf_op jit(solution)/shard_map/ppermute | solution.py:28
  462.9 19.2 %collective-permute-start.70 = (bf16[384,896]{1,0:T(8,128)(2,1)S(1)}, bf16[384,896]{1,0:T(8,128)(2,1)S(1)}, u32[]{:S(2)}, u32[]{:S(2)}) collective-permute-start(bf16[384,896]{1,0:T(8,128)(2,1)S(1)} %join_halves.9.refs_4_.refs_8_), channel_id=1, source_target_pairs={{0,2},{1,3},{2,0},{3,1},{4,6},{5,7},{6,4},{7,5},{8,10},{9,11},{10,... | collective-permute-start | bytes 2064392 | tf_op jit(solution)/shard_map/ppermute | solution.py:28
  (135 other events, 1165.9 us)

commit v3 on v2

--- a/solution.py
+++ b/solution.py
@@ -187,6 +187,10 @@
         [pl.BlockSpec(a.shape, lambda h, o=None: (h, 0)) for a in (mine_up, mine_down)],
         [shape_of((2 * a.shape[0], a.shape[1]), low) for a in (mine_up, mine_down)],
     )
+
+
+def copied(a):
+    return kernel(copy_kernel, "copied", None, [a], (1,), [whole(a.shape)], whole(a.shape), shape_of(a.shape, a.dtype))
 
 
 def tables_kernel(n_row, tile, tile_cols, head_dim, at, cos_ref, a_ref, b_ref):
@@ -343,7 +347,7 @@
         [block, whole(cos.shape), whole(cos.shape), whole(cos.shape), whole(gain.shape)],
         [pl.BlockSpec((tokens, LANES), lambda h, o=None: (0, h)), block],
         [shape_of((tokens, heads * LANES), low), shape_of((tokens, columns), low)],
-        megabytes=60,
+        megabytes=32,
     )
 
 
@@ -428,32 +432,40 @@
             pltpu.VMEM((LANES, tokens), wide),
             pltpu.VMEM((tokens, LANES), low),
         ],
-        megabytes=60,
-    )
-
-
-def project_kernel(at, x_ref, w_ref, o_ref):
-    o_ref[...] = dot(x_ref[...], w_ref[...]).astype(o_ref.dtype)
-
-
-def project_back_kernel(at, *refs):
-    xs, (w_ref, o_ref) = refs[:-2], refs[-2:]
-    width = xs[0].shape[1]
-    value = sum(dot_t(x[...], w_ref[:, n * width : (n + 1) * width]) for n, x in enumerate(xs))
-    o_ref[...] = value.astype(o_ref.dtype)
-
-
-def project(xs, w, first, count, rows, dtype):
-    columns = w.shape[1] if len(xs) == 1 else w.shape[0]
-    return kernel(
-        project_kernel if len(xs) == 1 else project_back_kernel,
+        megabytes=32,
+    )
+
+
+def project_kernel(product, at, x_ref, w_ref, send_ref, keep_ref):
+    value = product(x_ref[...], w_ref[...])
+    half = pl.num_programs(0) // 2
+
+    @pl.when(pl.program_id(0) < half)
+    def _():
+        send_ref[...] = value.astype(low)
+
+    @pl.when(pl.program_id(0) >= half)
+    def _():
+        keep_ref[...] = value
+
+
+def project(x, w, rows, product=dot):
+    columns = w.shape[1] if product is dot else w.shape[0]
+    count = x.shape[0] // rows
+    half = count // 2
+    return kernel(
+        functools.partial(project_kernel, product),
         "project",
         None,
-        [*xs, w],
+        [x, w],
         (count,),
-        [pl.BlockSpec((rows, x.shape[1]), lambda s, o=None: (first + s, 0)) for x in xs] + [whole(w.shape)],
-        pl.BlockSpec((rows, columns), lambda s, o=None: (s, 0)),
-        shape_of((count * rows, columns), dtype),
+        [pl.BlockSpec((rows, x.shape[1]), lambda s, o=None: ((s + half) % count, 0)), whole(w.shape)],
+        [
+            pl.BlockSpec((rows, columns), lambda s, o=None: (jnp.minimum(s, half - 1), 0)),
+            pl.BlockSpec((rows, columns), lambda s, o=None: (jnp.maximum(s - half, 0), 0)),
+        ],
+        [shape_of((half * rows, columns), low), shape_of((half * rows, columns), wide)],
+        megabytes=36,
     )
 
 
@@ -701,45 +713,44 @@
     parts, gbs = refs[2 : 2 + n], refs[2 + n : 2 + 2 * n]
     outs = refs[2 + 2 * n : 6 + 2 * n]
     acc_ref, out_ref = refs[6 + 2 * n :]
-    s = pl.program_id(0)
-
-    @pl.when(s == 0)
-    def _():
-        for ref in outs:
-            ref[:, columns:] = jnp.zeros((ref.shape[0], ref.shape[1] - columns), low)
-
-    acc_ref[...] = dot(xt_ref[...], pick(s, parts))
+    padded = outs[0].shape[1]
+    wide_columns = parts[0].shape[1]
+    lane = lax.broadcasted_iota(jnp.int32, (wide_columns, padded), 0)
+    target = (lane // LANES) * head_dim + lane % LANES
+    column = lax.broadcasted_iota(jnp.int32, (wide_columns, padded), 1)
+    inside = lane % LANES < head_dim
+    per = columns // n
+    narrow = sum(
+        dot(part[...], jnp.where(inside & (column == target + p * per), 1.0, 0.0).astype(low))
+        for p, part in enumerate(parts)
+    ).astype(low)
+    acc_ref[...] = dot(xt_ref[...], narrow)
     for half, value in enumerate(halves_of(acc_ref, at)):
-        joined = [value[:, h * LANES : h * LANES + head_dim] for h in range(value.shape[1] // LANES)]
-        value = jnp.concatenate(joined, axis=1).astype(low)
-        width, rows = value.shape[1], value.shape[0] - cut
-        for c in range(n):
-
-            @pl.when(s == c)
-            def _():
-                outs[half][:, c * width : (c + 1) * width] = value[:cut]
-                outs[2 + half][:rows, c * width : (c + 1) * width] = value[cut:]
-
-    @pl.when(s == n - 1)
-    def _():
-        rows = gbs[0].shape[0]
-        out_ref[...] = sum(dot(mt_ref[:, j * rows : (j + 1) * rows], gbs[j][...]) for j in range(n))
-        for half, value in enumerate(halves_of(out_ref, at)):
-            ref = outs[2 + half]
-            heads = [value[h * LANES : h * LANES + head_dim] for h in range(value.shape[0] // LANES)]
-            value = jnp.concatenate(heads, axis=0)
-            length, width = value.shape[0], columns
-            start = xt_ref.shape[0] // 2 - cut
-            side, third = value.shape[1] - width, length // 3
-            ref[start : start + length, :width] = value[:, :width].astype(low)
-            rest = [value[k * third : (k + 1) * third, width:] for k in range(3)]
-            ref[start + length :, :width] = jnp.concatenate(rest, axis=1).astype(low)
-
-
-def grad_last(xt, parts, mixed_t, gbs, at, head_dim, cut):
-    n = len(parts)
+        outs[half][...] = value[:cut].astype(low)
+        outs[2 + half][: value.shape[0] - cut] = value[cut:].astype(low)
+
+    rows = gbs[0].shape[0]
+    out_ref[...] = sum(dot(mt_ref[:, j * rows : (j + 1) * rows], gbs[j][...]) for j in range(n))
+    for half, value in enumerate(halves_of(out_ref, at)):
+        ref = outs[2 + half]
+        heads = [value[h * LANES : h * LANES + head_dim] for h in range(value.shape[0] // LANES)]
+        value = jnp.concatenate(heads, axis=0)
+        length, third = value.shape[0], value.shape[0] // 3
+        start = xt_ref.shape[0] // 2 - cut
+        spare = jnp.zeros((third, padded - columns), wide)
+        ref[start : start + length] = jnp.where(
+            lax.broadcasted_iota(jnp.int32, (length, padded), 1) < columns, value[:, :padded], 0.0
+        ).astype(low)
+        rest = [value[k * third : (k + 1) * third, columns:] for k in range(3)]
+        ref[start + length :] = jnp.concatenate(rest + [spare], axis=1).astype(low)
+
+
+def grad_last(xt, joined, mixed_t, gbs, at, head_dim, cut):
+    n = joined.shape[1] // (3 * LANES)
+    assert n == len(gbs)
+    tokens, part = joined.shape[0], 3 * LANES
     width = xt.shape[0]
-    columns = n * parts[0].shape[1] // LANES * head_dim
+    columns = n * 3 * head_dim
     length = mixed_t.shape[0] // LANES * head_dim // 2
     assert gbs[0].shape[1] - columns == columns // 3 and length % 3 == 0
     padded = -(-columns // LANES) * LANES
@@ -748,16 +759,18 @@
         functools.partial(grad_last_kernel, n, head_dim, cut, columns),
         "grad_last",
         at,
-        [xt, mixed_t, *parts, *gbs],
-        (n,),
-        [whole(a.shape) for a in (xt, mixed_t, *parts, *gbs)],
+        [xt, mixed_t, *[joined] * n, *gbs],
+        (1,),
+        [whole(xt.shape), whole(mixed_t.shape)]
+        + [pl.BlockSpec((tokens, part), lambda s, o=None, h=h: (0, h)) for h in range(n)]
+        + [whole(b.shape) for b in gbs],
         [whole(a) for a in shapes for _ in range(2)],
         [shape_of(a, low) for a in shapes for _ in range(2)],
         scratch=[
-            pltpu.VMEM((width, parts[0].shape[1]), wide),
+            pltpu.VMEM((width, padded), wide),
             pltpu.VMEM((mixed_t.shape[0], gbs[0].shape[1]), wide),
         ],
-        megabytes=52,
+        megabytes=50,
     )
 
 
@@ -892,11 +905,9 @@
     )
 
 
-def place_last_kernel(count, halves, head_dim, steps, columns, at, *refs):
-    firsts, seconds, lasts = refs[:count], refs[count : 2 * count], refs[2 * count : 3 * count]
-    o_ref, out_ref = refs[3 * count :]
+def place_rows_of(srcs, at, halves, head_dim, columns, o_ref):
+    count = len(srcs)
     heads = columns // (3 * head_dim) // halves
-    s = pl.program_id(0)
 
     def put(d, block):
         for t in range(3):
@@ -909,11 +920,37 @@
                     ]
 
     for j in range(count):
-        block = jnp.where(s < steps, firsts[j][...], seconds[j][...]).astype(wide)
+        block = srcs[j][...].astype(wide)
         for d in range(count):
             pl.when(at[j] == d)(functools.partial(put, d, block))
 
-    @pl.when(s == 0)
+
+def place_top_kernel(halves, head_dim, columns, at, *refs):
+    place_rows_of(refs[:-1], at, halves, head_dim, columns, refs[-1])
+
+
+def place_top(blocks, at, halves, head_dim, rows, columns):
+    count = len(blocks)
+    cut, width = blocks[0].shape
+    step = 96
+    return kernel(
+        functools.partial(place_top_kernel, halves, head_dim, columns),
+        "place_top",
+        at,
+        blocks,
+        (cut // step,),
+        [pl.BlockSpec((step, width), lambda s, o: (s, 0))] * count,
+        pl.BlockSpec((step, columns * count), lambda s, o: (s, 0)),
+        shape_of((rows, columns * count), wide),
+    )
+
+
+def place_last_kernel(count, halves, head_dim, columns, at, *refs):
+    seconds, lasts = refs[:count], refs[count : 2 * count]
+    _, o_ref, out_ref = refs[2 * count :]
+    place_rows_of(seconds, at, halves, head_dim, columns, o_ref)
+
+    @pl.when(pl.program_id(0) == 0)
     def _():
         length = out_ref.shape[0] // count
         for j in range(count):
@@ -925,27 +962,30 @@
             out_ref[pl.ds(at_row, length), width:] = jnp.concatenate(rest, axis=0)
 
 
-def place_last(firsts, seconds, at, halves, head_dim, rows, length, columns):
-    count = len(firsts)
-    cut, width = firsts[0].shape
-    step = 96
-    steps, total = cut // step, rows // step
-    last = seconds[0].shape[0] - (rows - cut)
-    assert last == rows - cut
-    outs = [(rows, columns * count), (count * length, columns // 3 * 4)]
-    return kernel(
-        functools.partial(place_last_kernel, count, halves, head_dim, steps, columns),
-        "place_last",
-        at,
-        [*firsts, *seconds, *seconds],
-        (total,),
-        [pl.BlockSpec((step, width), lambda s, o: (jnp.minimum(s, steps - 1), 0))] * count
-        + [pl.BlockSpec((step, width), lambda s, o: (jnp.maximum(s - steps, 0), 0))] * count
-        + [pl.BlockSpec((last, width), lambda s, o: (1, 0))] * count,
-        [pl.BlockSpec((step, columns * count), lambda s, o: (s, 0)), whole(outs[1])],
-        [shape_of(a, wide) for a in outs],
-        megabytes=40,
-    )
+def place_last(blocks, top, at, halves, head_dim, length, columns):
+    count = len(blocks)
+    step, width = 96, blocks[0].shape[1]
+    rows = top.shape[0]
+    last = blocks[0].shape[0] // 2
+    steps = last // step
+    skip = rows // step - steps
+    outs = [top.shape, (count * length, columns // 3 * 4)]
+    return pl.pallas_call(
+        functools.partial(place_last_kernel, count, halves, head_dim, columns),
+        grid_spec=pltpu.PrefetchScalarGridSpec(
+            num_scalar_prefetch=1,
+            grid=(steps,),
+            in_specs=[pl.BlockSpec((step, width), lambda s, o: (s, 0))] * count
+            + [pl.BlockSpec((last, width), lambda s, o: (1, 0))] * count
+            + [pl.BlockSpec(memory_space=pl.ANY)],
+            out_specs=[pl.BlockSpec((step, columns * count), lambda s, o: (skip + s, 0)), whole(outs[1])],
+        ),
+        out_shape=[shape_of(a, wide) for a in outs],
+        input_output_aliases={2 * count + 1: 0},
+        compiler_params=pltpu.CompilerParams(vmem_limit_bytes=32 * 1024 * 1024),
+        cost_estimate=pl.CostEstimate(flops=1, bytes_accessed=1, transcendentals=0),
+        name="place_last",
+    )(at, *blocks, *blocks, top)
 
 
 def program(sizes, tokens, condition, valid, positions, w_qkv, w_out, w_up, w_down, w_ada, qk_gain, cotangent):
@@ -1068,10 +1108,9 @@
     cot_y, cot_core, mixed = lax.optimization_barrier((cot_y, cot_core, mixed))
     if paired:
         mixed, other_up = lax.optimization_barrier((mixed, other_up))
-    sent = project([mixed], w_out_mine, 2, 2, own, low)
+    sent, keep = project(mixed, w_out_mine, own)
     got = core_swap(sent)
     cot_last = core_swap(after(cot_y, sent))
-    keep = project([after(mixed, sent)], w_out_mine, 0, 2, own, wide)
     got = after(got, keep)
     sent = add_second(keep, got)
     got_y = y_swap(sent)
@@ -1115,6 +1154,24 @@
             self.got, self.core = y_swap(self.value), core_swap(self.value)
             return self.value
 
+        def rows_in(self, *earlier):
+            other = after(self.got, *earlier)
+            self.sent = (self.value.astype(wide) + other.astype(wide)).astype(low)
+            self.got = over_rows(self.sent)
+            return self.sent
+
+        def rows_out(self, *earlier):
+            parts = after(self.got, *earlier).reshape(n_row, -1, self.got.shape[1])
+            shard = jnp.sum(parts.astype(wide), axis=0).astype(low)
+            self.sent = cat(*[shard] * n_row)
+            self.got = over_rows(self.sent)
+            return self.sent
+
+        def y_rows(self, *earlier):
+            self.value = after(self.got, *earlier)
+            self.got, self.core = y_swap(self.value), core_swap(self.value)
+            return self.value
+
         def end(self, *earlier):
             self.got, self.core = lax.optimization_barrier((self.got, self.core) + earlier)[:2]
             self.last = core_swap(self.got)
@@ -1137,9 +1194,8 @@
         keep, got, after(got_y, t), hidden, branch, cot_row, modulation, live
     )
     gb_y, gb_core = y_swap(gb_own), core_swap(gb_own)
-    mlp_sent = project([after(act, gb_own)], w_down_mine, 2, 2, own, low)
+    mlp_sent, mlp_keep = project(after(act, gb_own), w_down_mine, own)
     mlp_got = core_swap(mlp_sent)
-    mlp_keep = project([after(act, mlp_sent)], w_down_mine, 0, 2, own, wide)
     t = mlp_keep
     if paired:
         t = d.z_one(t)
@@ -1149,99 +1205,83 @@
     mlp_next = add_second(mlp_keep, mlp_got)
     mlp_y = y_swap(mlp_next)
     gbs = [gb_own, gb_y, gb_core, after(gb_last, mlp_next)]
-    heads_back = []
-
-    def back_of(head, *earlier):
-        heads_back.append(
-            attn_bwd(
-                gbs, after(joined, *earlier), aug, mixed, w_out_mine, cos_all, sin_a, sin_b, gain, head_dim, head, 1
-            )
-        )
-        return heads_back[-1][0]
-
-    t = back_of(0)
+    joined_back, g_gain = attn_bwd(
+        gbs, joined, aug, mixed, w_out_mine, cos_all, sin_a, sin_b, gain, head_dim, 0, my_heads
+    )
+    t = joined_back
     if paired:
         t = d.z_two(t)
         t = u_one.z_one(t)
-    t = back_of(1, t)
+    sent, keep = project(after(joined_back, t), w_qkv_mine, own, dot_t)
+    got = core_swap(sent)
+    t = sent
+    if paired:
+        rows = width // 2
+        length = my_heads * head_dim // halves
+        cut = (rows + length + length // 3) // 2
+        g = grad_last(attn_t, after(joined_back, t), mixed_t, gbs, at_img, head_dim, cut)
+        q_one, q_two = Piece(g[0], g[1]), Piece(g[2], g[3])
+        t = g[0]
+    got = after(got, t)
+    sent = add_second(keep, got)
+    got_y = y_swap(sent)
+    t = sent
+    if paired:
+        t = u_two.z_one(t)
+        t = d.z_three(t)
     out_own, sums_out = result(mlp_keep, mlp_got, after(mlp_y, t), hidden, cot_row, modulation, live)
     output = over_rows(out_own)
     t = out_own
     if paired:
         t = u_one.z_two(t)
-        t = d.z_three(t)
-        t = u_two.z_one(t)
-    t = back_of(2, t)
-    if paired:
-        t = d.y(t)
-    t = back_of(3, t)
-    assert my_heads == 4
-    if paired:
-        t = u_one.z_three(t)
-        t = u_two.z_two(t)
-    grad_heads = [g for g, _ in heads_back]
-    g_gain = sum(g for _, g in heads_back)
-    if paired:
-        rows = width // 2
-        length = my_heads * head_dim // halves
-        cut = (rows + length + length // 3) // 2
-        g = grad_last(attn_t, grad_heads[:3] + [after(grad_heads[3], t)], mixed_t, gbs, at_img, head_dim, cut)
-        q_one, q_two = Piece(g[0], g[1]), Piece(g[2], g[3])
-        t = d.end(g[0])
-    sent = project(grad_heads[:3] + [after(grad_heads[3], t)], w_qkv_mine, 2, 2, own, low)
-    got = core_swap(sent)
-    t = sent
-    if paired:
-        t = u_one.y(t)
-    keep = project(grad_heads[:3] + [after(grad_heads[3], t)], w_qkv_mine, 0, 2, own, wide)
-    got = after(got, keep)
-    sent = add_second(keep, got)
-    got_y = y_swap(sent)
-    t = sent
-    if paired:
-        t = u_two.z_three(t)
-        t = q_one.z_one(t)
-    output = after(output, t)
-    grad_own, sums_last = last_back(keep, got, after(got_y, output), tok_row, grad_hidden, modulation, live)
-    t = grad_own
-    if paired:
-        t = u_two.y(t)
-    grad_tokens = over_rows(after(grad_own, t))
+    grad_own, sums_last = last_back(keep, got, after(got_y, t), tok_row, grad_hidden, modulation, live)
     vector = (sums_two + sums_last + sums_out)[:6]
     got = core_swap(vector)
     t = vector
     if paired:
-        t = q_one.z_two(t)
-        t = q_two.z_one(t)
-        t = u_one.end(t)
+        t = d.y(t)
+        t = q_one.z_one(t)
     vector = vector + after(got, t)
     got = y_swap(vector)
     t = vector
     if paired:
-        sum_down = place_rows(d.blocks(t), at_columns, 384)
-        t = sum_down
+        t = u_two.z_two(t)
+        t = u_one.z_three(t)
+        t = q_two.z_one(t)
+        t = d.end(t)
     grad_mod = (vector + after(got, t)).astype(low)
     blocks = grad_mod.reshape(n_row, n_col, mod_span)
     mine = lax.dynamic_slice_in_dim(blocks, at_col[0], 1, axis=1)[:, 0]
-    share = over_rows(after(mine, grad_tokens))
+    share_z = z_swaps([lax.dynamic_slice_in_dim(mine, me_row ^ k, 1, axis=0) for k in order_row])
     t = mine
     if paired:
+        t = u_one.y(t)
+        t = q_one.z_two(t)
+    output = copied(after(output, t))
+    grad_tokens = over_rows(after(grad_own, output))
+    t = output
+    if paired:
+        sum_down = place_rows(d.blocks(t), at_columns, 384)
+        t = u_two.z_three(sum_down)
         t = q_two.z_two(t)
-        t = q_one.z_three(t)
-        sum_up = place_first(u_one.blocks(t), at_columns, halves)
-        t = sum_up
-    share = after(share, t)
+    at_image = [jnp.argmax(jnp.stack([(me_row ^ b) == k for k in order_row])) for b in range(images)]
+    share_rel = cat(*[after(v, t) for v in share_z])
+    share = cat(*[lax.dynamic_slice_in_dim(share_rel, a, 1, axis=0) for a in at_image])
     back = lax.dot_general(share, w_ada, (((1,), (1,)), ((), ())), preferred_element_type=wide)
     flat = jnp.concatenate([back.reshape(-1), g_gain[:, :head_dim].reshape(-1)]).reshape(1, -1)
     got = swap(flat, "row", n_row, 1)
     t = flat
     if paired:
         other_share = x_swap(share)
-        t = u_two.end(t)
-        t = q_one.y(t)
+        t = u_one.end(t)
+        t = u_two.y(t)
+        t = q_one.z_three(t)
     flat = flat + after(got, t)
     got = swap(flat, "row", n_row, 2)
     t = flat
+    if paired:
+        sum_up = place_first(u_one.blocks(t), at_columns, halves)
+        t = q_two.z_three(sum_up)
 
     def outer_product(a, b):
         return lax.dot_general(a, b, (((0,), (0,)), ((), ())), preferred_element_type=wide)
@@ -1257,7 +1297,8 @@
     got = core_swap(flat)
     t = flat
     if paired:
-        t = q_two.z_three(t)
+        t = q_one.y(t)
+        t = u_two.end(t)
     flat = flat + after(got, t)
     got = y_swap(flat)
     t = flat
@@ -1265,6 +1306,7 @@
     output = output.reshape(tokens.shape)
     t = grad_tokens
     if paired:
+        t = q_two.y(t)
         sum_up = place_second(u_two.blocks(t), sum_up, at_columns, halves)
         t = sum_up
     flat = (flat + after(got, t))[0]
@@ -1274,20 +1316,12 @@
     grad_condition = grad_silu * (s * (1.0 + cond * (1.0 - s)))
     if paired:
         gains_other = x_swap(gains)
-        t = q_two.y(grad_condition)
-        t = q_one.end(t)
+        t = q_one.end(grad_condition)
         gains = gains + after(gains_other, t)
-        t = q_two.end(gains)
-        sum_qkv, sum_out = place_last(
-            q_one.blocks(t),
-            q_two.blocks(t),
-            at_columns,
-            halves,
-            head_dim,
-            rows,
-            length,
-            3 * my_heads * head_dim,
-        )
+        columns = 3 * my_heads * head_dim
+        top = place_top(q_one.blocks(gains), at_columns, halves, head_dim, rows, columns)
+        t = q_two.end(top)
+        sum_qkv, sum_out = place_last(q_two.blocks(t), top, at_columns, halves, head_dim, length, columns)
     else:
         gains = lax.psum(gains, "img")
 
@@ -1307,7 +1341,7 @@
             wholes = jnp.transpose(wholes.reshape(n_col, halves, -1, columns), (1, 0, 2, 3)).reshape(-1, columns)
             return lax.psum_scatter(wholes, "img", scatter_dimension=0, tiled=True).astype(wide)
 
-        g_qkv = weight_grad(attn_in, jnp.concatenate(grad_heads, axis=1)).reshape(width, my_heads, 3, LANES)[..., :head_dim]
+        g_qkv = weight_grad(attn_in, joined_back).reshape(width, my_heads, 3, LANES)[..., :head_dim]
         g_qkv = jnp.swapaxes(g_qkv, 1, 2).reshape(width, -1)
         g_out = weight_grad(mixed, cat(*gbs)).reshape(my_heads, LANES, width)[:, :head_dim].reshape(-1, width)
         sum_up = reduce_columns(weight_grad(cat(*xs), grad_gu), 2 * halves)

time: 504 us -> 472 us (0.937)
  Pallas kernels: 182 us -> 160 us
  waiting for transfers between devices: 144 us -> 127 us
  between operations: 4.69 us -> 12.3 us
    pallas_call x46 -> x41, Pallas kernels: 176 us -> 149 us  [kernel(): pl.pallas_call(functools.partial(body, None) if none else body, grid_spec...]
    ppermute x74 -> x77, waiting for transfers between devices: 144 us -> 127 us  [swap(): return lax.ppermute(value, axis, [(a, a ^ bit) for a in range(size)])]
    ppermute x74 -> x77, starting transfers between devices: 58.8 us -> 64.9 us  [swap(): return lax.ppermute(value, axis, [(a, a ^ bit) for a in range(size)])]
    pallas_call x0 -> x1, Pallas kernels: none -> 5.65 us  [place_last(): pl.pallas_call(functools.partial(place_last_kernel, count, halves, head_d...]
    all_to_all x5 -> x4, starting transfers between devices: 21.9 us -> 18.1 us  [over_rows(): return lax.all_to_all(v, 'row', split_axis=0, concat_axis=0, tiled=True)]
    unnamed x181 -> x170, local copies, waits for them, and re-layouts: 55.5 us -> 53.9 us
  transfers between devices with their start and end apart: 79 -> 81, of which waited for: 27 -> 27; matrix products, arithmetic and copies ran while one was open for 6% -> 6% of each run, Pallas kernels for 29% -> 26%
where the time goes in v3:
time: 472 us; the launch traced here: 466 us
  Pallas kernels  160 us (34%)
  waiting for transfers between devices  127 us (27%)
  starting transfers between devices  83 us (18%)
  local copies, waits for them, and re-layouts  57.3 us (12%)
  other arithmetic  21.9 us (5%)
  between operations  12.3 us (3%)
    pallas_call x41, Pallas kernels, kernel(): pl.pallas_call(functools.partial(body, None) if none else body, grid_spec...  149 us
    ppermute x77, waiting for transfers between devices, swap(): return lax.ppermute(value, axis, [(a, a ^ bit) for a in range(size)])  127 us
    ppermute x77, starting transfers between devices, swap(): return lax.ppermute(value, axis, [(a, a ^ bit) for a in range(size)])  64.9 us
    unnamed x170, local copies, waits for them, and re-layouts  53.9 us
    all_to_all x4, starting transfers between devices, over_rows(): return lax.all_to_all(v, 'row', split_axis=0, concat_axis=0, tiled=True)  18.1 us
  transfers between devices with their start and end apart: 81, of which 27 were waited for; matrix products, arithmetic and copies ran while one was open for 6% of the time, Pallas kernels for 26%

profile of v3, /device:TPU:0, one launch (start us, length us, event | category | flops | bytes accessed | tf_op | source)
XLA Modules:
  0.0 465.6 jit_solution(2153351834837964673)
XLA Ops:
  12.2 4.9 %all-to-all-start = ((bf16[4,64,1152]{2,1,0:T(8,128)(2,1)}), bf16[4,64,1152]{2,1,0:T(8,128)(2,1)S(1)}, u32[]{:S(2)}, u32[]{:S(2)}) async-start(bf16[4,64,1152]{2,1,0:T(8,128)(2,1)} %bitcast.26), calls=%async_computation | async-start | bytes 1179648 | tf_op jit(solution)/shard_map/all_to_all | solution.py:1040
  52.4 5.1 %collective-permute-done.7.refs_1_ = bf16[256,1152]{1,0:T(8,128)(2,1)} collective-permute-done((bf16[256,1152]{1,0:T(8,128)(2,1)S(1)}, bf16[256,1152]{1,0:T(8,128)(2,1)}, u32[]{:S(2)}, u32[]{:S(2)}) %collective-permute-start.7) | collective-permute-done | bytes 589856 | tf_op jit(solution)/shard_map/ppermute | solution.py:28
  57.5 3.9 collective-permute-done.11
  63.1 5.5 %all-to-all-start.1 = ((bf16[4,64,1152]{2,1,0:T(8,128)(2,1)}), bf16[4,64,1152]{2,1,0:T(8,128)(2,1)S(1)}, u32[]{:S(2)}, u32[]{:S(2)}) async-start(bf16[4,64,1152]{2,1,0:T(8,128)(2,1)} %bitcast.87), calls=%async_computation.1 | async-start | bytes 1179648 | tf_op jit(solution)/shard_map/all_to_all | solution.py:1040
  73.9 6.9 %project_qkv.1 = (bf16[1024,1152]{1,0:T(8,128)(2,1)S(1)}, f32[1024,1536]{1,0:T(8,128)S(1)}) custom-call(bf16[256,1152]{1,0:T(8,128)(2,1)S(1)} %bitcast.80, bf16[256,1152]{1,0:T(8,128)(2,1)} %collective-permute-done.7.refs_1_, bf16[256,1152]{1,0:T(8,128)(2,1)S(1)} %copy-done.69, bf16[256,1152]{1,0:T(8,128)(2,1)S(1)} %collective-permute-done.12.refs_3_, ...), custom_call_target="tpu_custom_call" | custom-call | flops 1 | bytes 1 | tf_op jit(solution)/shard_map/project_qkv/pallas_call | solution.py:57
  90.6 11.0 %attn_fwd.1 = (bf16[1024,512]{1,0:T(8,128)(2,1)S(1)}, bf16[1024,1536]{1,0:T(8,128)(2,1)S(1)}) custom-call(f32[1024,1536]{1,0:T(8,128)S(1)} %copy-done.6, f32[1024,128]{1,0:T(8,128)S(1)} %copy-done.33, f32[1024,128]{1,0:T(8,128)S(1)} %copy-done.36, f32[1024,128]{1,0:T(8,128)S(1)} %copy-done.39, f32[2,128]{1,0:T(2,128)S(1)} %pad.4.gain_ref.refs_11_), custom_call_target="tpu_custom_call" | custom-call | flops 1 | bytes 1 | tf_op jit(solution)/shard_map/attn_fwd/pallas_call | solution.py:57
  117.2 5.5 %collective-permute-done.17.y_ref = bf16[256,1152]{1,0:T(8,128)(2,1)S(1)} collective-permute-done((bf16[256,1152]{1,0:T(8,128)(2,1)S(1)}, bf16[256,1152]{1,0:T(8,128)(2,1)S(1)}, u32[]{:S(2)}, u32[]{:S(2)}) %collective-permute-start.17) | collective-permute-done | bytes 589856 | tf_op jit(solution)/shard_map/ppermute | solution.py:28
  126.4 13.7 %collective-permute-done.19.refs_1_ = bf16[256,1152]{1,0:T(8,128)(2,1)S(1)} collective-permute-done((bf16[256,1152]{1,0:T(8,128)(2,1)S(1)}, bf16[256,1152]{1,0:T(8,128)(2,1)S(1)}, u32[]{:S(2)}, u32[]{:S(2)}) %collective-permute-start.19) | collective-permute-done | bytes 589856 | tf_op jit(solution)/shard_map/ppermute | solution.py:28
  142.1 18.5 %feed_forward.1 = (bf16[1024,768]{1,0:T(8,128)(2,1)}, bf16[1024,1536]{1,0:T(8,128)(2,1)}, bf16[1024,1152]{1,0:T(8,128)(2,1)}, bf16[512,1152]{1,0:T(8,128)(2,1)S(1)}, f32[512,1152]{1,0:T(8,128)}) custom-call(s32[1]{0:T(128)} %dynamic_slice.52.live, bf16[256,1152]{1,0:T(8,128)(2,1)S(1)} %get-tuple-element.237.refs_0_, ...), custom_call_target="tpu_custom_call" | custom-call | flops 1 | bytes 1 | tf_op jit(solution)/shard_map/feed_forward/pallas_call | solution.py:57
  167.2 4.1 grad_part.3
  172.1 4.2 grad_part.4
  176.3 4.1 grad_part.5
  189.8 3.3 collective-permute-done.27.b_ref
  194.1 5.5 %collective-permute-done.25.refs_1_.refs_7_ = bf16[256,1152]{1,0:T(8,128)(2,1)S(1)} collective-permute-done((bf16[256,1152]{1,0:T(8,128)(2,1)S(1)}, bf16[256,1152]{1,0:T(8,128)(2,1)S(1)}, u32[]{:S(2)}, u32[]{:S(2)}) %collective-permute-start.25) | collective-permute-done | bytes 589856 | tf_op jit(solution)/shard_map/ppermute | solution.py:28
  207.2 20.8 %attn_bwd.1 = (bf16[1024,1536]{1,0:T(8,128)(2,1)S(1)}, f32[2,128]{1,0:T(2,128)S(1)}) custom-call(bf16[256,1152]{1,0:T(8,128)(2,1)S(1)} %get-tuple-element.257.refs_0_.refs_6_, bf16[256,1152]{1,0:T(8,128)(2,1)S(1)} %collective-permute-done.25.refs_1_.refs_7_, bf16[256,1152]{1,0:T(8,128)(2,1)S(1)} %collective-permute-done.26.refs_2_.refs_8_, ...), custom_call_target="tpu_custom_call" | custom-call | flops 1 | bytes 1 | tf_op jit(solution)/shard_map/attn_bwd/pallas_call | solution.py:57
  231.6 6.4 %project.5 = (bf16[512,1152]{1,0:T(8,128)(2,1)}, f32[512,1152]{1,0:T(8,128)S(1)}) custom-call(bf16[1024,1536]{1,0:T(8,128)(2,1)S(1)} %get-tuple-element.281.x_ref.refs_2_.refs_3_.refs_4_.refs_5_, bf16[1152,1536]{1,0:T(8,128)(2,1)S(1)} %copy-done.4), custom_call_target="tpu_custom_call" | custom-call | flops 1 | bytes 1 | tf_op jit(solution)/shard_map/project/pallas_call | solution.py:57
  244.3 13.2 %grad_last.1 = (bf16[384,896]{1,0:T(8,128)(2,1)}, bf16[384,896]{1,0:T(8,128)(2,1)S(1)}, bf16[384,896]{1,0:T(8,128)(2,1)}, bf16[384,896]{1,0:T(8,128)(2,1)}) custom-call(s32[1]{0:T(128)} %bitcast.1.at, bf16[1152,1024]{1,0:T(8,128)(2,1)} %copy-done.31, bf16[512,1024]{1,0:T(8,128)(2,1)} %copy-done.48, bf16[1024,1536]{1,0:T(8,128)(2,1)} %copy-done.1, ...), custom_call_target="tpu_custom_call" | custom-call | flops 1 | bytes 1 | tf_op jit(solution)/shard_map/grad_last/pallas_call | solution.py:57
  279.0 17.5 %collective-permute-done.36.b_ref = bf16[192,1152]{1,0:T(8,128)(2,1)S(1)} collective-permute-done((bf16[192,1152]{1,0:T(8,128)(2,1)S(1)}, bf16[192,1152]{1,0:T(8,128)(2,1)S(1)}, u32[]{:S(2)}, u32[]{:S(2)}) %collective-permute-start.36) | collective-permute-done | bytes 442400 | tf_op jit(solution)/shard_map/ppermute | solution.py:28
  299.9 3.6 all-to-all-start.2
  319.4 6.0 %collective-permute-done.47.b_ref = bf16[384,896]{1,0:T(8,128)(2,1)} collective-permute-done((bf16[384,896]{1,0:T(8,128)(2,1)}, bf16[384,896]{1,0:T(8,128)(2,1)}, u32[]{:S(2)}, u32[]{:S(2)}) %collective-permute-start.47) | collective-permute-done | bytes 688160 | tf_op jit(solution)/shard_map/ppermute | solution.py:28
  347.0 4.2 all-to-all-start.3
  354.3 5.3 %place_rows.1 = f32[1536,1152]{1,0:T(8,128)} custom-call(s32[4]{0:T(128)S(1)} %pad_add_fusion.at, bf16[384,1152]{1,0:T(8,128)(2,1)S(1)} %join_halves.5.refs_0_, bf16[384,1152]{1,0:T(8,128)(2,1)} %collective-permute-done.45.refs_1_, bf16[384,1152]{1,0:T(8,128)(2,1)} %collective-permute-done.46.refs_2_, bf16[384,1152]{1,0:T(8,128)(2,1)} %collective-permute-done.50.refs_3_), custom_call_target="tpu_custom_call" | custom-call | flops 1 | bytes 1 | tf_op jit(solution)/shard_map/place_rows/pallas_call | solution.py:57
  365.6 5.2 %collective-permute-done.51 = bf16[1,432]{1,0:T(2,128)(2,1)S(1)} collective-permute-done((bf16[1,432]{1,0:T(2,128)(2,1)S(1)}, bf16[1,432]{1,0:T(2,128)(2,1)S(1)}, u32[]{:S(2)}, u32[]{:S(2)}) %collective-permute-start.51) | collective-permute-done | bytes 896 | tf_op jit(solution)/shard_map/ppermute | solution.py:28
  370.9 4.0 collective-permute-start.56
  377.1 17.6 %collective-permute-done.56.b_ref = bf16[288,768]{1,0:T(8,128)(2,1)S(1)} collective-permute-done((bf16[288,768]{1,0:T(8,128)(2,1)S(1)}, bf16[288,768]{1,0:T(8,128)(2,1)S(1)}, u32[]{:S(2)}, u32[]{:S(2)}) %collective-permute-start.56) | collective-permute-done | bytes 442400 | tf_op jit(solution)/shard_map/ppermute | solution.py:28
  400.6 5.5 %place_first.1.refs_4_ = f32[576,6144]{1,0:T(8,128)} custom-call(s32[4]{0:T(128)S(1)} %pad_add_fusion.at, bf16[576,768]{1,0:T(8,128)(2,1)S(1)} %join_halves.6.refs_0_, bf16[576,768]{1,0:T(8,128)(2,1)} %collective-permute-done.57.refs_1_, bf16[576,768]{1,0:T(8,128)(2,1)} %collective-permute-done.58.refs_2_, bf16[576,768]{1,0:T(8,128)(2,1)S(1)} %collective-permute-done.62.refs_3_), custom_call_target="tpu_custom_call" | custom-call | flops 1 | bytes 1 | tf_op jit(solution)/shard_map/place_first/pallas_call | solution.py:57
  409.8 6.5 %collective-permute-done.66.b_ref = bf16[192,896]{1,0:T(8,128)(2,1)S(1)} collective-permute-done((bf16[192,896]{1,0:T(8,128)(2,1)S(1)}, bf16[192,896]{1,0:T(8,128)(2,1)S(1)}, u32[]{:S(2)}, u32[]{:S(2)}) %collective-permute-start.66) | collective-permute-done | bytes 344096 | tf_op jit(solution)/shard_map/ppermute | solution.py:28
  426.1 3.9 collective-permute-done.69.b_ref
  432.4 5.8 %place_second.1 = f32[576,6144]{1,0:T(8,128)} custom-call(s32[4]{0:T(128)S(1)} %pad_add_fusion.at, bf16[576,768]{1,0:T(8,128)(2,1)} %join_halves.7.refs_0_, bf16[576,768]{1,0:T(8,128)(2,1)} %collective-permute-done.64.refs_1_, bf16[576,768]{1,0:T(8,128)(2,1)S(1)} %copy-done.56, ...), custom_call_target="tpu_custom_call", output_to_operand_aliasing={{}: (5, {})} | custom-call | flops 1 | bytes 1 | tf_op jit(solution)/shard_map/place_second/pallas_call | solution.py:870
  445.8 6.5 %place_top.1.refs_8_ = f32[576,3456]{1,0:T(8,128)} custom-call(s32[4]{0:T(128)S(1)} %pad_add_fusion.at, bf16[384,896]{1,0:T(8,128)(2,1)S(1)} %join_halves.8.refs_0_, bf16[384,896]{1,0:T(8,128)(2,1)} %collective-permute-done.72.refs_1_, bf16[384,896]{1,0:T(8,128)(2,1)S(1)} %copy-done.67, bf16[384,896]{1,0:T(8,128)(2,1)} %collective-permute-done.74.refs_3_), custom_call_target="tpu_custom_call" | custom-call | flops 1 | bytes 1 | tf_op jit(solution)/shard_map/place_top/pallas_call | solution.py:57
  452.3 5.4 %collective-permute-done.70.refs_1_.refs_5_ = bf16[384,896]{1,0:T(8,128)(2,1)S(1)} collective-permute-done((bf16[384,896]{1,0:T(8,128)(2,1)S(1)}, bf16[384,896]{1,0:T(8,128)(2,1)S(1)}, u32[]{:S(2)}, u32[]{:S(2)}) %collective-permute-start.70) | collective-permute-done | bytes 688160 | tf_op jit(solution)/shard_map/ppermute | solution.py:28
  459.8 5.6 %place_last.1 = (f32[576,3456]{1,0:T(8,128)}, f32[576,1152]{1,0:T(8,128)}) custom-call(s32[4]{0:T(128)S(1)} %pad_add_fusion.at, bf16[384,896]{1,0:T(8,128)(2,1)S(1)} %join_halves.9.refs_0_.refs_4_, bf16[384,896]{1,0:T(8,128)(2,1)S(1)} %collective-permute-done.70.refs_1_.refs_5_, ...), custom_call_target="tpu_custom_call", output_to_operand_aliasing={{0}: (9, {})} | custom-call | flops 1 | bytes 1 | tf_op jit(solution)/shard_map/place_last/pallas_call | solution.py:973
  (397 shorter events, 214.2 us)
Async XLA Ops:
  9.2 38.7 %collective-permute-start.8 = (bf16[576,864]{1,0:T(8,128)(2,1)S(1)}, bf16[576,864]{1,0:T(8,128)(2,1)}, u32[]{:S(2)}, u32[]{:S(2)}) collective-permute-start(bf16[576,864]{1,0:T(8,128)(2,1)S(1)} %cut_qkv.1.mine_ref), channel_id=1, source_target_pairs={{0,16},{16,0},{1,17},{17,1},{2,18},{18,2},{3,19},{19,3},{4,20},{20... | collective-permute-start | bytes 2985992 | tf_op jit(solution)/shard_map/ppermute | solution.py:28
  12.2 29.4 %all-to-all-start = ((bf16[4,64,1152]{2,1,0:T(8,128)(2,1)}), bf16[4,64,1152]{2,1,0:T(8,128)(2,1)S(1)}, u32[]{:S(2)}, u32[]{:S(2)}) async-start(bf16[4,64,1152]{2,1,0:T(8,128)(2,1)} %bitcast.26), calls=%async_computation | async-start | bytes 1179648 | tf_op jit(solution)/shard_map/all_to_all | solution.py:1040
  27.5 33.9 %collective-permute-start.6 = (bf16[384,1152]{1,0:T(8,128)(2,1)}, bf16[384,1152]{1,0:T(8,128)(2,1)}, u32[]{:S(2)}, u32[]{:S(2)}) collective-permute-start(bf16[384,1152]{1,0:T(8,128)(2,1)} %get-tuple-element.191.c_ref), channel_id=1, source_target_pairs={{0,16},{16,0},{1,17},{17,1},{2,18},{18,2},{3,19},{19,3},{4,20},{20... | collective-permute-start | bytes 2654216 | tf_op jit(solution)/shard_map/ppermute | solution.py:28
  61.4 40.2 %collective-permute-start.15 = (bf16[576,1536]{1,0:T(8,128)(2,1)}, bf16[576,1536]{1,0:T(8,128)(2,1)}, u32[]{:S(2)}, u32[]{:S(2)}) collective-permute-start(bf16[576,1536]{1,0:T(8,128)(2,1)} %get-tuple-element.219.a_ref), channel_id=1, source_target_pairs={{0,16},{16,0},{1,17},{17,1},{2,18},{18,2},{3,19},{19,3},{4,20},{20... | collective-permute-start | bytes 5308424 | tf_op jit(solution)/shard_map/ppermute | solution.py:28
  63.1 21.8 %all-to-all-start.1 = ((bf16[4,64,1152]{2,1,0:T(8,128)(2,1)}), bf16[4,64,1152]{2,1,0:T(8,128)(2,1)S(1)}, u32[]{:S(2)}, u32[]{:S(2)}) async-start(bf16[4,64,1152]{2,1,0:T(8,128)(2,1)} %bitcast.87), calls=%async_computation.1 | async-start | bytes 1179648 | tf_op jit(solution)/shard_map/all_to_all | solution.py:1040
  199.7 28.3 %collective-permute-start.29 = (bf16[192,1152]{1,0:T(8,128)(2,1)S(1)}, bf16[192,1152]{1,0:T(8,128)(2,1)S(1)}, u32[]{:S(2)}, u32[]{:S(2)}) collective-permute-start(bf16[192,1152]{1,0:T(8,128)(2,1)S(1)} %get-tuple-element.264), channel_id=1, source_target_pairs={{0,4},{4,0},{8,12},{12,8},{1,5},{5,1},{9,13},{13,9},{2,6},{6,2},{1... | collective-permute-start | bytes 1327112 | tf_op jit(solution)/shard_map/ppermute | solution.py:28
  201.5 27.4 %collective-permute-start.33 = (bf16[576,768]{1,0:T(8,128)(2,1)S(1)}, bf16[576,768]{1,0:T(8,128)(2,1)S(1)}, u32[]{:S(2)}, u32[]{:S(2)}) collective-permute-start(bf16[576,768]{1,0:T(8,128)(2,1)S(1)} %get-tuple-element.251), channel_id=1, source_target_pairs={{0,16},{16,0},{1,17},{17,1},{2,18},{18,2},{3,19},{19,3},{4,20},{20... | collective-permute-start | bytes 2654216 | tf_op jit(solution)/shard_map/ppermute | solution.py:28
  239.4 22.4 %collective-permute-start.32 = (bf16[576,768]{1,0:T(8,128)(2,1)S(1)}, bf16[576,768]{1,0:T(8,128)(2,1)S(1)}, u32[]{:S(2)}, u32[]{:S(2)}) collective-permute-start(bf16[576,768]{1,0:T(8,128)(2,1)S(1)} %get-tuple-element.253), channel_id=1, source_target_pairs={{0,16},{16,0},{1,17},{17,1},{2,18},{18,2},{3,19},{19,3},{4,20},{20... | collective-permute-start | bytes 2654216 | tf_op jit(solution)/shard_map/ppermute | solution.py:28
  239.7 26.4 %collective-permute-start.31 = (bf16[192,1152]{1,0:T(8,128)(2,1)}, bf16[192,1152]{1,0:T(8,128)(2,1)}, u32[]{:S(2)}, u32[]{:S(2)}) collective-permute-start(bf16[192,1152]{1,0:T(8,128)(2,1)} %add_convert_fusion.5), channel_id=1, source_target_pairs={{0,8},{4,12},{8,0},{12,4},{1,9},{5,13},{9,1},{13,5},{2,10},{6,14},... | collective-permute-start | bytes 1327112 | tf_op jit(solution)/shard_map/ppermute | solution.py:28
  242.2 25.2 %collective-permute-start.28 = (bf16[256,1152]{1,0:T(8,128)(2,1)}, bf16[256,1152]{1,0:T(8,128)(2,1)}, u32[]{:S(2)}, u32[]{:S(2)}) collective-permute-start(bf16[256,1152]{1,0:T(8,128)(2,1)} %add_second.6), channel_id=1, source_target_pairs={{0,2},{1,3},{2,0},{3,1},{4,6},{5,7},{6,4},{7,5},{8,10},{9,11},{10,... | collective-permute-start | bytes 1769480 | tf_op jit(solution)/shard_map/ppermute | solution.py:28
  243.8 28.0 %collective-permute-start.38 = (bf16[288,768]{1,0:T(8,128)(2,1)}, bf16[288,768]{1,0:T(8,128)(2,1)}, u32[]{:S(2)}, u32[]{:S(2)}) collective-permute-start(bf16[288,768]{1,0:T(8,128)(2,1)} %get-tuple-element.276), channel_id=1, source_target_pairs={{0,4},{4,0},{8,12},{12,8},{1,5},{5,1},{9,13},{13,9},{2,6},{6,2},{1... | collective-permute-start | bytes 1327112 | tf_op jit(solution)/shard_map/ppermute | solution.py:28
  258.3 40.7 %collective-permute-start.35 = (bf16[384,896]{1,0:T(8,128)(2,1)}, bf16[384,896]{1,0:T(8,128)(2,1)S(1)}, u32[]{:S(2)}, u32[]{:S(2)}) collective-permute-start(bf16[384,896]{1,0:T(8,128)(2,1)} %get-tuple-element.282), channel_id=1, source_target_pairs={{0,16},{16,0},{1,17},{17,1},{2,18},{18,2},{3,19},{19,3},{4,20},{20... | collective-permute-start | bytes 2064392 | tf_op jit(solution)/shard_map/ppermute | solution.py:28
  266.1 41.7 %collective-permute-start.41 = (bf16[288,768]{1,0:T(8,128)(2,1)}, bf16[288,768]{1,0:T(8,128)(2,1)}, u32[]{:S(2)}, u32[]{:S(2)}) collective-permute-start(bf16[288,768]{1,0:T(8,128)(2,1)} %get-tuple-element.285), channel_id=1, source_target_pairs={{0,4},{4,0},{8,12},{12,8},{1,5},{5,1},{9,13},{13,9},{2,6},{6,2},{1... | collective-permute-start | bytes 1327112 | tf_op jit(solution)/shard_map/ppermute | solution.py:28
  267.4 29.1 %collective-permute-start.36 = (bf16[192,1152]{1,0:T(8,128)(2,1)S(1)}, bf16[192,1152]{1,0:T(8,128)(2,1)S(1)}, u32[]{:S(2)}, u32[]{:S(2)}) collective-permute-start(bf16[192,1152]{1,0:T(8,128)(2,1)S(1)} %add_convert_fusion.4.a_ref), channel_id=1, source_target_pairs={{0,4},{4,0},{8,12},{12,8},{1,5},{5,1},{9,13},{13,9},{2,6},{6,2},{1... | collective-permute-start | bytes 1327112 | tf_op jit(solution)/shard_map/ppermute | solution.py:28
  274.0 37.7 %collective-permute-start.40 = (bf16[288,768]{1,0:T(8,128)(2,1)}, bf16[288,768]{1,0:T(8,128)(2,1)}, u32[]{:S(2)}, u32[]{:S(2)}) collective-permute-start(bf16[288,768]{1,0:T(8,128)(2,1)} %add_convert_fusion.3), channel_id=1, source_target_pairs={{0,8},{4,12},{8,0},{12,4},{1,9},{5,13},{9,1},{13,5},{2,10},{6,14},... | collective-permute-start | bytes 1327112 | tf_op jit(solution)/shard_map/ppermute | solution.py:28
  278.9 28.4 %collective-permute-start.42 = (f32[6,1152]{1,0:T(8,128)S(1)}, f32[6,1152]{1,0:T(8,128)S(1)}, u32[]{:S(2)}, u32[]{:S(2)}) collective-permute-start(f32[6,1152]{1,0:T(8,128)S(1)} %slice_add_fusion), channel_id=1, source_target_pairs={{0,1},{1,0},{2,3},{3,2},{4,5},{5,4},{6,7},{7,6},{8,9},{9,8},{10,11... | collective-permute-start | bytes 82952 | tf_op jit(solution)/shard_map/ppermute | solution.py:28
  297.4 31.9 %collective-permute-start.45 = (bf16[384,1152]{1,0:T(8,128)(2,1)S(1)}, bf16[384,1152]{1,0:T(8,128)(2,1)}, u32[]{:S(2)}, u32[]{:S(2)}) collective-permute-start(bf16[384,1152]{1,0:T(8,128)(2,1)S(1)} %join_halves.5.refs_0_), channel_id=1, source_target_pairs={{0,2},{1,3},{2,0},{3,1},{4,6},{5,7},{6,4},{7,5},{8,10},{9,11},{10,... | collective-permute-start | bytes 2654216 | tf_op jit(solution)/shard_map/ppermute | solution.py:28
  299.9 29.4 %collective-permute-start.46 = (bf16[384,1152]{1,0:T(8,128)(2,1)S(1)}, bf16[384,1152]{1,0:T(8,128)(2,1)}, u32[]{:S(2)}, u32[]{:S(2)}) collective-permute-start(bf16[384,1152]{1,0:T(8,128)(2,1)S(1)} %join_halves.5.refs_0_), channel_id=1, source_target_pairs={{0,1},{1,0},{2,3},{3,2},{4,5},{5,4},{6,7},{7,6},{8,9},{9,8},{10,11... | collective-permute-start | bytes 2654216 | tf_op jit(solution)/shard_map/ppermute | solution.py:28
  299.9 46.2 %all-to-all-start.2 = ((bf16[4,64,1152]{2,1,0:T(8,128)(2,1)}), bf16[4,64,1152]{2,1,0:T(8,128)(2,1)S(1)}, u32[]{:S(2)}, u32[]{:S(2)}) async-start(bf16[4,64,1152]{2,1,0:T(8,128)(2,1)} %bitcast.85), calls=%async_computation.2 | async-start | bytes 1179648 | tf_op jit(solution)/shard_map/all_to_all | solution.py:1040
  307.7 34.9 %collective-permute-start.39 = (bf16[192,896]{1,0:T(8,128)(2,1)}, bf16[192,896]{1,0:T(8,128)(2,1)}, u32[]{:S(2)}, u32[]{:S(2)}) collective-permute-start(bf16[192,896]{1,0:T(8,128)(2,1)} %get-tuple-element.300), channel_id=1, source_target_pairs={{0,4},{4,0},{8,12},{12,8},{1,5},{5,1},{9,13},{13,9},{2,6},{6,2},{1... | collective-permute-start | bytes 1032200 | tf_op jit(solution)/shard_map/ppermute | solution.py:28
  313.0 25.8 %collective-permute-start.43 = (bf16[288,768]{1,0:T(8,128)(2,1)S(1)}, bf16[288,768]{1,0:T(8,128)(2,1)S(1)}, u32[]{:S(2)}, u32[]{:S(2)}) collective-permute-start(bf16[288,768]{1,0:T(8,128)(2,1)S(1)} %add_convert_fusion.1.a_ref), channel_id=1, source_target_pairs={{0,4},{4,0},{8,12},{12,8},{1,5},{5,1},{9,13},{13,9},{2,6},{6,2},{1... | collective-permute-start | bytes 1327112 | tf_op jit(solution)/shard_map/ppermute | solution.py:28
  334.8 26.9 %collective-permute-start.49 = (bf16[288,768]{1,0:T(8,128)(2,1)}, bf16[288,768]{1,0:T(8,128)(2,1)}, u32[]{:S(2)}, u32[]{:S(2)}) collective-permute-start(bf16[288,768]{1,0:T(8,128)(2,1)} %add_convert_fusion.2), channel_id=1, source_target_pairs={{0,8},{4,12},{8,0},{12,4},{1,9},{5,13},{9,1},{13,5},{2,10},{6,14},... | collective-permute-start | bytes 1327112 | tf_op jit(solution)/shard_map/ppermute | solution.py:28
  337.3 25.4 %collective-permute-start.48 = (bf16[192,896]{1,0:T(8,128)(2,1)}, bf16[192,896]{1,0:T(8,128)(2,1)}, u32[]{:S(2)}, u32[]{:S(2)}) collective-permute-start(bf16[192,896]{1,0:T(8,128)(2,1)} %copy-done.78), channel_id=1, source_target_pairs={{0,4},{4,0},{8,12},{12,8},{1,5},{5,1},{9,13},{13,9},{2,6},{6,2},{1... | collective-permute-start | bytes 1032200 | tf_op jit(solution)/shard_map/ppermute | solution.py:28
  342.7 32.7 %collective-permute-start.57 = (bf16[576,768]{1,0:T(8,128)(2,1)S(1)}, bf16[576,768]{1,0:T(8,128)(2,1)}, u32[]{:S(2)}, u32[]{:S(2)}) collective-permute-start(bf16[576,768]{1,0:T(8,128)(2,1)S(1)} %join_halves.6.refs_0_), channel_id=1, source_target_pairs={{0,2},{1,3},{2,0},{3,1},{4,6},{5,7},{6,4},{7,5},{8,10},{9,11},{10,... | collective-permute-start | bytes 2654216 | tf_op jit(solution)/shard_map/ppermute | solution.py:28
  347.0 76.8 %all-to-all-start.3 = ((bf16[4,64,1152]{2,1,0:T(8,128)(2,1)}), bf16[4,64,1152]{2,1,0:T(8,128)(2,1)}, u32[]{:S(2)}, u32[]{:S(2)}) async-start(bf16[4,64,1152]{2,1,0:T(8,128)(2,1)} %bitcast.84), calls=%async_computation.3 | async-start | bytes 1179648 | tf_op jit(solution)/shard_map/all_to_all | solution.py:1040
  351.2 24.6 %collective-permute-start.58 = (bf16[576,768]{1,0:T(8,128)(2,1)S(1)}, bf16[576,768]{1,0:T(8,128)(2,1)}, u32[]{:S(2)}, u32[]{:S(2)}) collective-permute-start(bf16[576,768]{1,0:T(8,128)(2,1)S(1)} %join_halves.6.refs_0_), channel_id=1, source_target_pairs={{0,1},{1,0},{2,3},{3,2},{4,5},{5,4},{6,7},{7,6},{8,9},{9,8},{10,11... | collective-permute-start | bytes 2654216 | tf_op jit(solution)/shard_map/ppermute | solution.py:28
  370.8 25.4 %collective-permute-start.55 = (bf16[192,896]{1,0:T(8,128)(2,1)S(1)}, bf16[192,896]{1,0:T(8,128)(2,1)}, u32[]{:S(2)}, u32[]{:S(2)}) collective-permute-start(bf16[192,896]{1,0:T(8,128)(2,1)S(1)} %copy-done.80), channel_id=1, source_target_pairs={{0,8},{4,12},{8,0},{12,4},{1,9},{5,13},{9,1},{13,5},{2,10},{6,14},... | collective-permute-start | bytes 1032200 | tf_op jit(solution)/shard_map/ppermute | solution.py:28
  370.9 23.8 %collective-permute-start.56 = (bf16[288,768]{1,0:T(8,128)(2,1)S(1)}, bf16[288,768]{1,0:T(8,128)(2,1)S(1)}, u32[]{:S(2)}, u32[]{:S(2)}) collective-permute-start(bf16[288,768]{1,0:T(8,128)(2,1)S(1)} %add_convert_fusion.a_ref), channel_id=1, source_target_pairs={{0,4},{4,0},{8,12},{12,8},{1,5},{5,1},{9,13},{13,9},{2,6},{6,2},{1... | collective-permute-start | bytes 1327112 | tf_op jit(solution)/shard_map/ppermute | solution.py:28
  374.9 31.3 %collective-permute-start.61 = (bf16[192,896]{1,0:T(8,128)(2,1)}, bf16[192,896]{1,0:T(8,128)(2,1)}, u32[]{:S(2)}, u32[]{:S(2)}) collective-permute-start(bf16[192,896]{1,0:T(8,128)(2,1)} %add_convert_fusion.8), channel_id=1, source_target_pairs={{0,8},{4,12},{8,0},{12,4},{1,9},{5,13},{9,1},{13,5},{2,10},{6,14},... | collective-permute-start | bytes 1032200 | tf_op jit(solution)/shard_map/ppermute | solution.py:28
  375.4 32.0 %collective-permute-start.60 = (bf16[4,432]{1,0:T(4,128)(2,1)S(1)}, bf16[4,432]{1,0:T(4,128)(2,1)S(1)}, u32[]{:S(2)}, u32[]{:S(2)}) collective-permute-start(bf16[4,432]{1,0:T(4,128)(2,1)S(1)} %pad_maximum_fusion.3), channel_id=1, source_target_pairs={{0,16},{16,0},{1,17},{17,1},{2,18},{18,2},{3,19},{19,3},{4,20},{20... | collective-permute-start | bytes 10376 | tf_op jit(solution)/shard_map/ppermute | solution.py:28
  375.8 22.0 %collective-permute-start.54 = (f32[1,4752]{1,0:T(1,128)S(1)}, f32[1,4752]{1,0:T(1,128)S(1)}, u32[]{:S(2)}, u32[]{:S(2)}) collective-permute-start(f32[1,4752]{1,0:T(1,128)S(1)} %reshape.77), channel_id=1, source_target_pairs={{0,4},{4,0},{8,12},{12,8},{1,5},{5,1},{9,13},{13,9},{2,6},{6,2},{1... | collective-permute-start | bytes 57032 | tf_op jit(solution)/shard_map/ppermute | solution.py:28
  396.2 22.4 %collective-permute-start.64 = (bf16[576,768]{1,0:T(8,128)(2,1)}, bf16[576,768]{1,0:T(8,128)(2,1)}, u32[]{:S(2)}, u32[]{:S(2)}) collective-permute-start(bf16[576,768]{1,0:T(8,128)(2,1)} %join_halves.7.refs_0_), channel_id=1, source_target_pairs={{0,2},{1,3},{2,0},{3,1},{4,6},{5,7},{6,4},{7,5},{8,10},{9,11},{10,... | collective-permute-start | bytes 2654216 | tf_op jit(solution)/shard_map/ppermute | solution.py:28
  (134 other events, 1068.2 us)

commit v4 on v3

--- a/solution.py
+++ b/solution.py
@@ -1006,9 +1006,9 @@
 
     steps = lax.dynamic_index_in_dim(positions, me_row, 1, keepdims=False)
     bit = me_row % 2
-    at_col, at_img, at_columns, at_halves, live, at_tables, source = lax.optimization_barrier(
+    at_col = integers(me_col)
+    at_img, at_columns, at_halves, live, at_tables, source, at_image = lax.optimization_barrier(
         (
-            integers(me_col),
             integers(me_img if paired else jnp.zeros_like(me_img)),
             integers(*[me_col ^ j for j in order_col]),
             integers(1 - bit, bit),
@@ -1021,6 +1021,7 @@
                 ]
             ),
             integers(*[(me_row ^ k) * n_col + (me_col ^ j) for j in order_col for k in order_row]),
+            integers(*[me_row ^ k for k in order_row]),
         )
     )
 
@@ -1151,7 +1152,7 @@
 
         def y(self, *earlier):
             self.value = join_halves(self.keep, after(self.got, *earlier), at_halves)
-            self.got, self.core = y_swap(self.value), core_swap(self.value)
+            self.got = y_swap(self.value)
             return self.value
 
         def rows_in(self, *earlier):
@@ -1173,12 +1174,12 @@
             return self.value
 
         def end(self, *earlier):
-            self.got, self.core = lax.optimization_barrier((self.got, self.core) + earlier)[:2]
-            self.last = core_swap(self.got)
+            self.got, self.value = lax.optimization_barrier((self.got, self.value) + earlier)[:2]
+            self.core, self.last = core_swap(self.value), core_swap(self.got)
             return self.got
 
         def blocks(self, *earlier):
-            return [self.value, self.got, self.core, after(self.last, *earlier)]
+            return [self.value, self.got, after(self.core, *earlier), after(self.last, *earlier)]
 
     got = after(got, keep)
     sent = add_second(keep, got)
@@ -1239,15 +1240,15 @@
     got = core_swap(vector)
     t = vector
     if paired:
-        t = d.y(t)
         t = q_one.z_one(t)
+        t = q_two.z_one(t)
     vector = vector + after(got, t)
     got = y_swap(vector)
     t = vector
     if paired:
+        t = d.y(t)
         t = u_two.z_two(t)
         t = u_one.z_three(t)
-        t = q_two.z_one(t)
         t = d.end(t)
     grad_mod = (vector + after(got, t)).astype(low)
     blocks = grad_mod.reshape(n_row, n_col, mod_span)
@@ -1258,15 +1259,14 @@
         t = u_one.y(t)
         t = q_one.z_two(t)
     output = copied(after(output, t))
-    grad_tokens = over_rows(after(grad_own, output))
     t = output
     if paired:
         sum_down = place_rows(d.blocks(t), at_columns, 384)
         t = u_two.z_three(sum_down)
         t = q_two.z_two(t)
-    at_image = [jnp.argmax(jnp.stack([(me_row ^ b) == k for k in order_row])) for b in range(images)]
     share_rel = cat(*[after(v, t) for v in share_z])
-    share = cat(*[lax.dynamic_slice_in_dim(share_rel, a, 1, axis=0) for a in at_image])
+    pick_image = at_image[None, :] == jnp.arange(images)[:, None]
+    share = jnp.sum(jnp.where(pick_image[:, :, None], share_rel.astype(wide)[None], 0.0), axis=1).astype(low)
     back = lax.dot_general(share, w_ada, (((1,), (1,)), ((), ())), preferred_element_type=wide)
     flat = jnp.concatenate([back.reshape(-1), g_gain[:, :head_dim].reshape(-1)]).reshape(1, -1)
     got = swap(flat, "row", n_row, 1)
@@ -1274,14 +1274,15 @@
     if paired:
         other_share = x_swap(share)
         t = u_one.end(t)
-        t = u_two.y(t)
+        sum_up = place_first(u_one.blocks(t), at_columns, halves)
+        t = u_two.y(sum_up)
         t = q_one.z_three(t)
     flat = flat + after(got, t)
     got = swap(flat, "row", n_row, 2)
     t = flat
     if paired:
-        sum_up = place_first(u_one.blocks(t), at_columns, halves)
-        t = q_two.z_three(sum_up)
+        t = q_two.z_three(t)
+    grad_tokens = over_rows(after(grad_own, t))
 
     def outer_product(a, b):
         return lax.dot_general(a, b, (((0,), (0,)), ((), ())), preferred_element_type=wide)
@@ -1302,9 +1303,7 @@
     flat = flat + after(got, t)
     got = y_swap(flat)
     t = flat
-    grad_tokens = after(grad_tokens, t).astype(wide).reshape(tokens.shape)
     output = output.reshape(tokens.shape)
-    t = grad_tokens
     if paired:
         t = q_two.y(t)
         sum_up = place_second(u_two.blocks(t), sum_up, at_columns, halves)
@@ -1320,10 +1319,12 @@
         gains = gains + after(gains_other, t)
         columns = 3 * my_heads * head_dim
         top = place_top(q_one.blocks(gains), at_columns, halves, head_dim, rows, columns)
-        t = q_two.end(top)
+        grad_tokens = after(grad_tokens, top).astype(wide).reshape(tokens.shape)
+        t = q_two.end(grad_tokens)
         sum_qkv, sum_out = place_last(q_two.blocks(t), top, at_columns, halves, head_dim, length, columns)
     else:
         gains = lax.psum(gains, "img")
+        grad_tokens = grad_tokens.astype(wide).reshape(tokens.shape)
 
         def weight_grad(a, b):
             return lax.dot_general(a, b, (((0,), (0,)), ((), ())), preferred_element_type=wide).astype(low)

time: 472 us -> 448 us (0.949)
  local copies, waits for them, and re-layouts: 57.3 us -> 49.7 us
  between operations: 12.3 us -> 4.8 us
  other arithmetic: 21.9 us -> 16.8 us
  starting transfers between devices: 83 us -> 87.9 us
    unnamed x170 -> x162, local copies, waits for them, and re-layouts: 53.9 us -> 47 us
  transfers between devices with their start and end apart: 81 -> 81, of which waited for: 27 -> 34; matrix products, arithmetic and copies ran while one was open for 6% -> 5% of each run, Pallas kernels for 26% -> 27%
where the time goes in v4:
time: 448 us; the launch traced here: 442 us
  Pallas kernels  157 us (35%)
  waiting for transfers between devices  123 us (27%)
  starting transfers between devices  87.9 us (20%)
  local copies, waits for them, and re-layouts  49.7 us (11%)
  other arithmetic  16.8 us (4%)
  between operations  4.8 us (1%)
    pallas_call x41, Pallas kernels, kernel(): pl.pallas_call(functools.partial(body, None) if none else body, grid_spec...  146 us
    ppermute x77, waiting for transfers between devices, swap(): return lax.ppermute(value, axis, [(a, a ^ bit) for a in range(size)])  123 us
    ppermute x77, starting transfers between devices, swap(): return lax.ppermute(value, axis, [(a, a ^ bit) for a in range(size)])  69.1 us
    unnamed x162, local copies, waits for them, and re-layouts  47 us
    all_to_all x4, starting transfers between devices, over_rows(): return lax.all_to_all(v, 'row', split_axis=0, concat_axis=0, tiled=True)  18.7 us
  transfers between devices with their start and end apart: 81, of which 34 were waited for; matrix products, arithmetic and copies ran while one was open for 5% of the time, Pallas kernels for 27%

profile of v4, /device:TPU:0, one launch (start us, length us, event | category | flops | bytes accessed | tf_op | source)
XLA Modules:
  0.0 441.9 jit_solution(13283340267928666040)
XLA Ops:
  6.7 4.9 %all-to-all-start = ((bf16[4,64,1152]{2,1,0:T(8,128)(2,1)}), bf16[4,64,1152]{2,1,0:T(8,128)(2,1)S(1)}, u32[]{:S(2)}, u32[]{:S(2)}) async-start(bf16[4,64,1152]{2,1,0:T(8,128)(2,1)} %bitcast.30), calls=%async_computation | async-start | bytes 1179648 | tf_op jit(solution)/shard_map/all_to_all | solution.py:1041
  12.0 3.9 collective-permute-start.2
  49.8 5.1 %collective-permute-done.7.refs_1_ = bf16[256,1152]{1,0:T(8,128)(2,1)} collective-permute-done((bf16[256,1152]{1,0:T(8,128)(2,1)S(1)}, bf16[256,1152]{1,0:T(8,128)(2,1)}, u32[]{:S(2)}, u32[]{:S(2)}) %collective-permute-start.7) | collective-permute-done | bytes 589856 | tf_op jit(solution)/shard_map/ppermute | solution.py:28
  57.5 5.5 %all-to-all-start.1 = ((bf16[4,64,1152]{2,1,0:T(8,128)(2,1)}), bf16[4,64,1152]{2,1,0:T(8,128)(2,1)S(1)}, u32[]{:S(2)}, u32[]{:S(2)}) async-start(bf16[4,64,1152]{2,1,0:T(8,128)(2,1)} %bitcast.74), calls=%async_computation.1 | async-start | bytes 1179648 | tf_op jit(solution)/shard_map/all_to_all | solution.py:1041
  68.4 6.7 %project_qkv.1 = (bf16[1024,1152]{1,0:T(8,128)(2,1)S(1)}, f32[1024,1536]{1,0:T(8,128)S(1)}) custom-call(bf16[256,1152]{1,0:T(8,128)(2,1)S(1)} %bitcast.67, bf16[256,1152]{1,0:T(8,128)(2,1)} %collective-permute-done.7.refs_1_, bf16[256,1152]{1,0:T(8,128)(2,1)S(1)} %copy-done.65, bf16[256,1152]{1,0:T(8,128)(2,1)S(1)} %collective-permute-done.12.refs_3_, ...), custom_call_target="tpu_custom_call" | custom-call | flops 1 | bytes 1 | tf_op jit(solution)/shard_map/project_qkv/pallas_call | solution.py:57
  85.1 10.7 %attn_fwd.1 = (bf16[1024,512]{1,0:T(8,128)(2,1)S(1)}, bf16[1024,1536]{1,0:T(8,128)(2,1)S(1)}) custom-call(f32[1024,1536]{1,0:T(8,128)S(1)} %copy-done.6, f32[1024,128]{1,0:T(8,128)S(1)} %copy-done.33, f32[1024,128]{1,0:T(8,128)S(1)} %copy-done.36, f32[1024,128]{1,0:T(8,128)S(1)} %copy-done.39, f32[2,128]{1,0:T(2,128)S(1)} %pad.4.gain_ref.refs_11_), custom_call_target="tpu_custom_call" | custom-call | flops 1 | bytes 1 | tf_op jit(solution)/shard_map/attn_fwd/pallas_call | solution.py:57
  110.8 5.9 %collective-permute-done.17.y_ref = bf16[256,1152]{1,0:T(8,128)(2,1)S(1)} collective-permute-done((bf16[256,1152]{1,0:T(8,128)(2,1)S(1)}, bf16[256,1152]{1,0:T(8,128)(2,1)S(1)}, u32[]{:S(2)}, u32[]{:S(2)}) %collective-permute-start.17) | collective-permute-done | bytes 589856 | tf_op jit(solution)/shard_map/ppermute | solution.py:28
  121.3 13.7 %collective-permute-done.19.refs_1_ = bf16[256,1152]{1,0:T(8,128)(2,1)S(1)} collective-permute-done((bf16[256,1152]{1,0:T(8,128)(2,1)S(1)}, bf16[256,1152]{1,0:T(8,128)(2,1)S(1)}, u32[]{:S(2)}, u32[]{:S(2)}) %collective-permute-start.19) | collective-permute-done | bytes 589856 | tf_op jit(solution)/shard_map/ppermute | solution.py:28
  137.0 18.4 %feed_forward.1 = (bf16[1024,768]{1,0:T(8,128)(2,1)}, bf16[1024,1536]{1,0:T(8,128)(2,1)}, bf16[1024,1152]{1,0:T(8,128)(2,1)}, bf16[512,1152]{1,0:T(8,128)(2,1)S(1)}, f32[512,1152]{1,0:T(8,128)}) custom-call(s32[1]{0:T(128)} %dynamic_slice.40.live, bf16[256,1152]{1,0:T(8,128)(2,1)S(1)} %get-tuple-element.237.refs_0_, ...), custom_call_target="tpu_custom_call" | custom-call | flops 1 | bytes 1 | tf_op jit(solution)/shard_map/feed_forward/pallas_call | solution.py:57
  162.1 4.7 %grad_part.3 = (bf16[384,1152]{1,0:T(8,128)(2,1)}, bf16[384,1152]{1,0:T(8,128)(2,1)S(1)}) custom-call(s32[1]{0:T(128)} %bitcast.at, bf16[1024,768]{1,0:T(8,128)(2,1)S(1)} %copy-done.18, bf16[1024,1152]{1,0:T(8,128)(2,1)S(1)} %copy-done.28), custom_call_target="tpu_custom_call" | custom-call | flops 1 | bytes 1 | tf_op jit(solution)/shard_map/grad_part/pallas_call | solution.py:57
  168.2 4.2 grad_part.4
  173.3 4.7 %grad_part.5 = (bf16[576,768]{1,0:T(8,128)(2,1)}, bf16[576,768]{1,0:T(8,128)(2,1)S(1)}) custom-call(s32[1]{0:T(128)} %bitcast.at, bf16[256,1152]{1,0:T(8,128)(2,1)S(1)} %get-tuple-element.237.refs_0_, bf16[256,1152]{1,0:T(8,128)(2,1)S(1)} %collective-permute-done.19.refs_1_, bf16[256,1152]{1,0:T(8,128)(2,1)S(1)} %collective-permute-done.20.refs_2_, ...), custom_call_target="tpu_custom_call" | custom-call | flops 1 | bytes 1 | tf_op jit(solution)/shard_map/grad_part/pallas_call | solution.py:57
  191.8 6.1 %collective-permute-done.25.refs_1_.refs_7_ = bf16[256,1152]{1,0:T(8,128)(2,1)S(1)} collective-permute-done((bf16[256,1152]{1,0:T(8,128)(2,1)S(1)}, bf16[256,1152]{1,0:T(8,128)(2,1)S(1)}, u32[]{:S(2)}, u32[]{:S(2)}) %collective-permute-start.25) | collective-permute-done | bytes 589856 | tf_op jit(solution)/shard_map/ppermute | solution.py:28
  204.5 20.5 %attn_bwd.1 = (bf16[1024,1536]{1,0:T(8,128)(2,1)S(1)}, f32[2,128]{1,0:T(2,128)S(1)}) custom-call(bf16[256,1152]{1,0:T(8,128)(2,1)S(1)} %get-tuple-element.257.refs_0_.refs_6_, bf16[256,1152]{1,0:T(8,128)(2,1)S(1)} %collective-permute-done.25.refs_1_.refs_7_, bf16[256,1152]{1,0:T(8,128)(2,1)S(1)} %collective-permute-done.26.refs_2_.refs_8_, ...), custom_call_target="tpu_custom_call" | custom-call | flops 1 | bytes 1 | tf_op jit(solution)/shard_map/attn_bwd/pallas_call | solution.py:57
  228.5 6.2 %project.5 = (bf16[512,1152]{1,0:T(8,128)(2,1)}, f32[512,1152]{1,0:T(8,128)S(1)}) custom-call(bf16[1024,1536]{1,0:T(8,128)(2,1)S(1)} %get-tuple-element.281.x_ref.refs_2_.refs_3_.refs_4_.refs_5_, bf16[1152,1536]{1,0:T(8,128)(2,1)S(1)} %copy-done.4), custom_call_target="tpu_custom_call" | custom-call | flops 1 | bytes 1 | tf_op jit(solution)/shard_map/project/pallas_call | solution.py:57
  241.8 12.9 %grad_last.1 = (bf16[384,896]{1,0:T(8,128)(2,1)S(1)}, bf16[384,896]{1,0:T(8,128)(2,1)S(1)}, bf16[384,896]{1,0:T(8,128)(2,1)}, bf16[384,896]{1,0:T(8,128)(2,1)}) custom-call(s32[1]{0:T(128)} %bitcast.at, bf16[1152,1024]{1,0:T(8,128)(2,1)} %copy-done.31, bf16[512,1024]{1,0:T(8,128)(2,1)} %copy-done.50, bf16[1024,1536]{1,0:T(8,128)(2,1)} %copy-done.1, ...), custom_call_target="tpu_custom_call" | custom-call | flops 1 | bytes 1 | tf_op jit(solution)/shard_map/grad_last/pallas_call | solution.py:57
  270.9 6.1 %collective-permute-done.36.y_ref = bf16[256,1152]{1,0:T(8,128)(2,1)S(1)} collective-permute-done((bf16[256,1152]{1,0:T(8,128)(2,1)S(1)}, bf16[256,1152]{1,0:T(8,128)(2,1)S(1)}, u32[]{:S(2)}, u32[]{:S(2)}) %collective-permute-start.36) | collective-permute-done | bytes 589856 | tf_op jit(solution)/shard_map/ppermute | solution.py:28
  282.9 4.9 %collective-permute-done.43.b_ref = bf16[384,896]{1,0:T(8,128)(2,1)S(1)} collective-permute-done((bf16[384,896]{1,0:T(8,128)(2,1)S(1)}, bf16[384,896]{1,0:T(8,128)(2,1)S(1)}, u32[]{:S(2)}, u32[]{:S(2)}) %collective-permute-start.43) | collective-permute-done | bytes 688160 | tf_op jit(solution)/shard_map/ppermute | solution.py:28
  291.7 3.9 all-to-all-start.2
  302.1 9.8 %collective-permute-done.47.refs_1_ = bf16[384,1152]{1,0:T(8,128)(2,1)} collective-permute-done((bf16[384,1152]{1,0:T(8,128)(2,1)S(1)}, bf16[384,1152]{1,0:T(8,128)(2,1)}, u32[]{:S(2)}, u32[]{:S(2)}) %collective-permute-start.47) | collective-permute-done | bytes 884768 | tf_op jit(solution)/shard_map/ppermute | solution.py:28
  312.5 5.8 %collective-permute-done.44.b_ref = bf16[288,768]{1,0:T(8,128)(2,1)S(1)} collective-permute-done((bf16[288,768]{1,0:T(8,128)(2,1)S(1)}, bf16[288,768]{1,0:T(8,128)(2,1)S(1)}, u32[]{:S(2)}, u32[]{:S(2)}) %collective-permute-start.44) | collective-permute-done | bytes 442400 | tf_op jit(solution)/shard_map/ppermute | solution.py:28
  333.1 5.3 %place_rows.1 = f32[1536,1152]{1,0:T(8,128)} custom-call(s32[4]{0:T(128)S(1)} %pad_add_fusion.at, bf16[384,1152]{1,0:T(8,128)(2,1)S(1)} %join_halves.5.refs_0_, bf16[384,1152]{1,0:T(8,128)(2,1)} %collective-permute-done.47.refs_1_, bf16[384,1152]{1,0:T(8,128)(2,1)} %collective-permute-done.48.refs_2_, bf16[384,1152]{1,0:T(8,128)(2,1)} %collective-permute-done.49.refs_3_), custom_call_target="tpu_custom_call" | custom-call | flops 1 | bytes 1 | tf_op jit(solution)/shard_map/place_rows/pallas_call | solution.py:57
  338.5 7.4 %collective-permute-done.46 = bf16[288,768]{1,0:T(8,128)(2,1)} collective-permute-done((bf16[288,768]{1,0:T(8,128)(2,1)}, bf16[288,768]{1,0:T(8,128)(2,1)}, u32[]{:S(2)}, u32[]{:S(2)}) %collective-permute-start.46) | collective-permute-done | bytes 442400 | tf_op jit(solution)/shard_map/ppermute | solution.py:28
  358.3 5.2 %place_first.1.refs_4_ = f32[576,6144]{1,0:T(8,128)} custom-call(s32[4]{0:T(128)S(1)} %pad_add_fusion.at, bf16[576,768]{1,0:T(8,128)(2,1)S(1)} %join_halves.6.refs_0_, bf16[576,768]{1,0:T(8,128)(2,1)} %collective-permute-done.58.refs_1_, bf16[576,768]{1,0:T(8,128)(2,1)S(1)} %collective-permute-done.59.refs_2_, ...), custom_call_target="tpu_custom_call" | custom-call | flops 1 | bytes 1 | tf_op jit(solution)/shard_map/place_first/pallas_call | solution.py:57
  363.6 8.7 %collective-permute-done.57.b_ref = bf16[288,768]{1,0:T(8,128)(2,1)S(1)} collective-permute-done((bf16[288,768]{1,0:T(8,128)(2,1)S(1)}, bf16[288,768]{1,0:T(8,128)(2,1)S(1)}, u32[]{:S(2)}, u32[]{:S(2)}) %collective-permute-start.57) | collective-permute-done | bytes 442400 | tf_op jit(solution)/shard_map/ppermute | solution.py:28
  373.0 3.7 collective-permute-start.66
  379.8 6.8 %collective-permute-done.50 = bf16[192,896]{1,0:T(8,128)(2,1)S(1)} collective-permute-done((bf16[192,896]{1,0:T(8,128)(2,1)}, bf16[192,896]{1,0:T(8,128)(2,1)S(1)}, u32[]{:S(2)}, u32[]{:S(2)}) %collective-permute-start.50) | collective-permute-done | bytes 344096 | tf_op jit(solution)/shard_map/ppermute | solution.py:28
  401.0 4.5 %all-to-all-start.3 = ((bf16[4,64,1152]{2,1,0:T(8,128)(2,1)}), bf16[4,64,1152]{2,1,0:T(8,128)(2,1)}, u32[]{:S(2)}, u32[]{:S(2)}) async-start(bf16[4,64,1152]{2,1,0:T(8,128)(2,1)} %bitcast.71), calls=%async_computation.3 | async-start | bytes 1179648 | tf_op jit(solution)/shard_map/all_to_all | solution.py:1041
  409.3 5.8 %place_second.1 = f32[576,6144]{1,0:T(8,128)} custom-call(s32[4]{0:T(128)S(1)} %pad_add_fusion.at, bf16[576,768]{1,0:T(8,128)(2,1)S(1)} %join_halves.7.refs_0_, bf16[576,768]{1,0:T(8,128)(2,1)} %collective-permute-done.66.refs_1_, bf16[576,768]{1,0:T(8,128)(2,1)} %collective-permute-done.68.refs_2_, ...), custom_call_target="tpu_custom_call", output_to_operand_aliasing={{}: (5, {})} | custom-call | flops 1 | bytes 1 | tf_op jit(solution)/shard_map/place_second/pallas_call | solution.py:870
  418.2 3.6 collective-permute-done.72
  422.3 6.7 %place_top.1.refs_8_ = f32[576,3456]{1,0:T(8,128)} custom-call(s32[4]{0:T(128)S(1)} %pad_add_fusion.at, bf16[384,896]{1,0:T(8,128)(2,1)S(1)} %join_halves.8.refs_0_, bf16[384,896]{1,0:T(8,128)(2,1)} %collective-permute-done.64.refs_1_, bf16[384,896]{1,0:T(8,128)(2,1)} %collective-permute-done.71.refs_2_, bf16[384,896]{1,0:T(8,128)(2,1)} %collective-permute-done.73.refs_3_), custom_call_target="tpu_custom_call" | custom-call | flops 1 | bytes 1 | tf_op jit(solution)/shard_map/place_top/pallas_call | solution.py:57
  436.8 4.6 %place_last.1 = (f32[576,3456]{1,0:T(8,128)}, f32[576,1152]{1,0:T(8,128)}) custom-call(s32[4]{0:T(128)S(1)} %pad_add_fusion.at, bf16[384,896]{1,0:T(8,128)(2,1)S(1)} %join_halves.9.refs_0_.refs_4_, bf16[384,896]{1,0:T(8,128)(2,1)S(1)} %collective-permute-done.74.refs_1_.refs_5_, ...), custom_call_target="tpu_custom_call", output_to_operand_aliasing={{0}: (9, {})} | custom-call | flops 1 | bytes 1 | tf_op jit(solution)/shard_map/place_last/pallas_call | solution.py:973
  (386 shorter events, 210.1 us)
Async XLA Ops:
  3.7 41.6 %collective-permute-start.8 = (bf16[576,864]{1,0:T(8,128)(2,1)S(1)}, bf16[576,864]{1,0:T(8,128)(2,1)}, u32[]{:S(2)}, u32[]{:S(2)}) collective-permute-start(bf16[576,864]{1,0:T(8,128)(2,1)S(1)} %cut_qkv.1.mine_ref), channel_id=1, source_target_pairs={{0,16},{16,0},{1,17},{17,1},{2,18},{18,2},{3,19},{19,3},{4,20},{20... | collective-permute-start | bytes 2985992 | tf_op jit(solution)/shard_map/ppermute | solution.py:28
  6.7 32.4 %all-to-all-start = ((bf16[4,64,1152]{2,1,0:T(8,128)(2,1)}), bf16[4,64,1152]{2,1,0:T(8,128)(2,1)S(1)}, u32[]{:S(2)}, u32[]{:S(2)}) async-start(bf16[4,64,1152]{2,1,0:T(8,128)(2,1)} %bitcast.30), calls=%async_computation | async-start | bytes 1179648 | tf_op jit(solution)/shard_map/all_to_all | solution.py:1041
  12.0 23.3 %collective-permute-start.2 = (f32[1,432]{1,0:T(1,128)S(1)}, f32[1,432]{1,0:T(1,128)S(1)}, u32[]{:S(2)}, u32[]{:S(2)}) collective-permute-start(f32[1,432]{1,0:T(1,128)S(1)} %get-tuple-element.364), channel_id=1, source_target_pairs={{0,12},{4,8},{8,4},{12,0},{1,13},{5,9},{9,5},{13,1},{2,14},{6,10},... | collective-permute-start | bytes 5192 | tf_op jit(solution)/shard_map/ppermute | solution.py:28
  25.4 30.4 %collective-permute-start.6 = (bf16[384,1152]{1,0:T(8,128)(2,1)}, bf16[384,1152]{1,0:T(8,128)(2,1)}, u32[]{:S(2)}, u32[]{:S(2)}) collective-permute-start(bf16[384,1152]{1,0:T(8,128)(2,1)} %get-tuple-element.191.c_ref), channel_id=1, source_target_pairs={{0,16},{16,0},{1,17},{17,1},{2,18},{18,2},{3,19},{19,3},{4,20},{20... | collective-permute-start | bytes 2654216 | tf_op jit(solution)/shard_map/ppermute | solution.py:28
  55.7 40.2 %collective-permute-start.15 = (bf16[576,1536]{1,0:T(8,128)(2,1)}, bf16[576,1536]{1,0:T(8,128)(2,1)}, u32[]{:S(2)}, u32[]{:S(2)}) collective-permute-start(bf16[576,1536]{1,0:T(8,128)(2,1)} %get-tuple-element.219.a_ref), channel_id=1, source_target_pairs={{0,16},{16,0},{1,17},{17,1},{2,18},{18,2},{3,19},{19,3},{4,20},{20... | collective-permute-start | bytes 5308424 | tf_op jit(solution)/shard_map/ppermute | solution.py:28
  57.5 21.7 %all-to-all-start.1 = ((bf16[4,64,1152]{2,1,0:T(8,128)(2,1)}), bf16[4,64,1152]{2,1,0:T(8,128)(2,1)S(1)}, u32[]{:S(2)}, u32[]{:S(2)}) async-start(bf16[4,64,1152]{2,1,0:T(8,128)(2,1)} %bitcast.74), calls=%async_computation.1 | async-start | bytes 1179648 | tf_op jit(solution)/shard_map/all_to_all | solution.py:1041
  166.8 21.9 %collective-permute-start.27 = (bf16[384,1152]{1,0:T(8,128)(2,1)}, bf16[384,1152]{1,0:T(8,128)(2,1)S(1)}, u32[]{:S(2)}, u32[]{:S(2)}) collective-permute-start(bf16[384,1152]{1,0:T(8,128)(2,1)} %get-tuple-element.249), channel_id=1, source_target_pairs={{0,16},{16,0},{1,17},{17,1},{2,18},{18,2},{3,19},{19,3},{4,20},{20... | collective-permute-start | bytes 2654216 | tf_op jit(solution)/shard_map/ppermute | solution.py:28
  197.9 27.1 %collective-permute-start.29 = (bf16[192,1152]{1,0:T(8,128)(2,1)S(1)}, bf16[192,1152]{1,0:T(8,128)(2,1)S(1)}, u32[]{:S(2)}, u32[]{:S(2)}) collective-permute-start(bf16[192,1152]{1,0:T(8,128)(2,1)S(1)} %get-tuple-element.264), channel_id=1, source_target_pairs={{0,4},{4,0},{8,12},{12,8},{1,5},{5,1},{9,13},{13,9},{2,6},{6,2},{1... | collective-permute-start | bytes 1327112 | tf_op jit(solution)/shard_map/ppermute | solution.py:28
  199.5 26.4 %collective-permute-start.33 = (bf16[576,768]{1,0:T(8,128)(2,1)S(1)}, bf16[576,768]{1,0:T(8,128)(2,1)S(1)}, u32[]{:S(2)}, u32[]{:S(2)}) collective-permute-start(bf16[576,768]{1,0:T(8,128)(2,1)S(1)} %copy-done.73), channel_id=1, source_target_pairs={{0,16},{16,0},{1,17},{17,1},{2,18},{18,2},{3,19},{19,3},{4,20},{20... | collective-permute-start | bytes 2654216 | tf_op jit(solution)/shard_map/ppermute | solution.py:28
  236.1 22.7 %collective-permute-start.32 = (bf16[576,768]{1,0:T(8,128)(2,1)}, bf16[576,768]{1,0:T(8,128)(2,1)S(1)}, u32[]{:S(2)}, u32[]{:S(2)}) collective-permute-start(bf16[576,768]{1,0:T(8,128)(2,1)} %get-tuple-element.253), channel_id=1, source_target_pairs={{0,16},{16,0},{1,17},{17,1},{2,18},{18,2},{3,19},{19,3},{4,20},{20... | collective-permute-start | bytes 2654216 | tf_op jit(solution)/shard_map/ppermute | solution.py:28
  237.2 25.4 %collective-permute-start.31 = (bf16[192,1152]{1,0:T(8,128)(2,1)}, bf16[192,1152]{1,0:T(8,128)(2,1)}, u32[]{:S(2)}, u32[]{:S(2)}) collective-permute-start(bf16[192,1152]{1,0:T(8,128)(2,1)} %add_convert_fusion.5), channel_id=1, source_target_pairs={{0,8},{4,12},{8,0},{12,4},{1,9},{5,13},{9,1},{13,5},{2,10},{6,14},... | collective-permute-start | bytes 1327112 | tf_op jit(solution)/shard_map/ppermute | solution.py:28
  239.7 25.7 %collective-permute-start.28 = (bf16[256,1152]{1,0:T(8,128)(2,1)}, bf16[256,1152]{1,0:T(8,128)(2,1)S(1)}, u32[]{:S(2)}, u32[]{:S(2)}) collective-permute-start(bf16[256,1152]{1,0:T(8,128)(2,1)} %add_second.6), channel_id=1, source_target_pairs={{0,2},{1,3},{2,0},{3,1},{4,6},{5,7},{6,4},{7,5},{8,10},{9,11},{10,... | collective-permute-start | bytes 1769480 | tf_op jit(solution)/shard_map/ppermute | solution.py:28
  241.4 25.9 %collective-permute-start.37 = (bf16[288,768]{1,0:T(8,128)(2,1)}, bf16[288,768]{1,0:T(8,128)(2,1)}, u32[]{:S(2)}, u32[]{:S(2)}) collective-permute-start(bf16[288,768]{1,0:T(8,128)(2,1)} %get-tuple-element.276), channel_id=1, source_target_pairs={{0,4},{4,0},{8,12},{12,8},{1,5},{5,1},{9,13},{13,9},{2,6},{6,2},{1... | collective-permute-start | bytes 1327112 | tf_op jit(solution)/shard_map/ppermute | solution.py:28
  254.8 26.2 %collective-permute-start.35 = (bf16[384,896]{1,0:T(8,128)(2,1)S(1)}, bf16[384,896]{1,0:T(8,128)(2,1)S(1)}, u32[]{:S(2)}, u32[]{:S(2)}) collective-permute-start(bf16[384,896]{1,0:T(8,128)(2,1)S(1)} %get-tuple-element.282), channel_id=1, source_target_pairs={{0,16},{16,0},{1,17},{17,1},{2,18},{18,2},{3,19},{19,3},{4,20},{20... | collective-permute-start | bytes 2064392 | tf_op jit(solution)/shard_map/ppermute | solution.py:28
  258.7 29.1 %collective-permute-start.43 = (bf16[384,896]{1,0:T(8,128)(2,1)S(1)}, bf16[384,896]{1,0:T(8,128)(2,1)S(1)}, u32[]{:S(2)}, u32[]{:S(2)}) collective-permute-start(bf16[384,896]{1,0:T(8,128)(2,1)S(1)} %copy-done.79), channel_id=1, source_target_pairs={{0,16},{16,0},{1,17},{17,1},{2,18},{18,2},{3,19},{19,3},{4,20},{20... | collective-permute-start | bytes 2064392 | tf_op jit(solution)/shard_map/ppermute | solution.py:28
  265.5 24.2 %collective-permute-start.41 = (bf16[192,1152]{1,0:T(8,128)(2,1)S(1)}, bf16[192,1152]{1,0:T(8,128)(2,1)S(1)}, u32[]{:S(2)}, u32[]{:S(2)}) collective-permute-start(bf16[192,1152]{1,0:T(8,128)(2,1)S(1)} %add_convert_fusion.4.a_ref), channel_id=1, source_target_pairs={{0,4},{4,0},{8,12},{12,8},{1,5},{5,1},{9,13},{13,9},{2,6},{6,2},{1... | collective-permute-start | bytes 1327112 | tf_op jit(solution)/shard_map/ppermute | solution.py:28
  267.3 28.2 %collective-permute-start.40 = (bf16[288,768]{1,0:T(8,128)(2,1)}, bf16[288,768]{1,0:T(8,128)(2,1)}, u32[]{:S(2)}, u32[]{:S(2)}) collective-permute-start(bf16[288,768]{1,0:T(8,128)(2,1)} %get-tuple-element.285), channel_id=1, source_target_pairs={{0,4},{4,0},{8,12},{12,8},{1,5},{5,1},{9,13},{13,9},{2,6},{6,2},{1... | collective-permute-start | bytes 1327112 | tf_op jit(solution)/shard_map/ppermute | solution.py:28
  276.9 21.1 %collective-permute-start.39 = (bf16[288,768]{1,0:T(8,128)(2,1)}, bf16[288,768]{1,0:T(8,128)(2,1)}, u32[]{:S(2)}, u32[]{:S(2)}) collective-permute-start(bf16[288,768]{1,0:T(8,128)(2,1)} %add_convert_fusion.3), channel_id=1, source_target_pairs={{0,8},{4,12},{8,0},{12,4},{1,9},{5,13},{9,1},{13,5},{2,10},{6,14},... | collective-permute-start | bytes 1327112 | tf_op jit(solution)/shard_map/ppermute | solution.py:28
  290.3 21.6 %collective-permute-start.47 = (bf16[384,1152]{1,0:T(8,128)(2,1)S(1)}, bf16[384,1152]{1,0:T(8,128)(2,1)}, u32[]{:S(2)}, u32[]{:S(2)}) collective-permute-start(bf16[384,1152]{1,0:T(8,128)(2,1)S(1)} %join_halves.5.refs_0_), channel_id=1, source_target_pairs={{0,2},{1,3},{2,0},{3,1},{4,6},{5,7},{6,4},{7,5},{8,10},{9,11},{10,... | collective-permute-start | bytes 2654216 | tf_op jit(solution)/shard_map/ppermute | solution.py:28
  291.7 38.3 %all-to-all-start.2 = ((bf16[4,64,1152]{2,1,0:T(8,128)(2,1)}), bf16[4,64,1152]{2,1,0:T(8,128)(2,1)S(1)}, u32[]{:S(2)}, u32[]{:S(2)}) async-start(bf16[4,64,1152]{2,1,0:T(8,128)(2,1)} %bitcast.72), calls=%async_computation.2 | async-start | bytes 1179648 | tf_op jit(solution)/shard_map/all_to_all | solution.py:1041
  301.5 24.3 %collective-permute-start.38 = (bf16[192,896]{1,0:T(8,128)(2,1)}, bf16[192,896]{1,0:T(8,128)(2,1)}, u32[]{:S(2)}, u32[]{:S(2)}) collective-permute-start(bf16[192,896]{1,0:T(8,128)(2,1)} %get-tuple-element.299), channel_id=1, source_target_pairs={{0,4},{4,0},{8,12},{12,8},{1,5},{5,1},{9,13},{13,9},{2,6},{6,2},{1... | collective-permute-start | bytes 1032200 | tf_op jit(solution)/shard_map/ppermute | solution.py:28
  311.9 20.5 %collective-permute-start.49 = (bf16[384,1152]{1,0:T(8,128)(2,1)}, bf16[384,1152]{1,0:T(8,128)(2,1)}, u32[]{:S(2)}, u32[]{:S(2)}) collective-permute-start(bf16[384,1152]{1,0:T(8,128)(2,1)} %collective-permute-done.47.refs_1_), channel_id=1, source_target_pairs={{0,1},{1,0},{2,3},{3,2},{4,5},{5,4},{6,7},{7,6},{8,9},{9,8},{10,11... | collective-permute-start | bytes 2654216 | tf_op jit(solution)/shard_map/ppermute | solution.py:28
  312.5 34.5 %collective-permute-start.45 = (bf16[192,896]{1,0:T(8,128)(2,1)}, bf16[192,896]{1,0:T(8,128)(2,1)}, u32[]{:S(2)}, u32[]{:S(2)}) collective-permute-start(bf16[192,896]{1,0:T(8,128)(2,1)} %copy-done.74), channel_id=1, source_target_pairs={{0,4},{4,0},{8,12},{12,8},{1,5},{5,1},{9,13},{13,9},{2,6},{6,2},{1... | collective-permute-start | bytes 1032200 | tf_op jit(solution)/shard_map/ppermute | solution.py:28
  325.8 20.1 %collective-permute-start.46 = (bf16[288,768]{1,0:T(8,128)(2,1)}, bf16[288,768]{1,0:T(8,128)(2,1)}, u32[]{:S(2)}, u32[]{:S(2)}) collective-permute-start(bf16[288,768]{1,0:T(8,128)(2,1)} %add_convert_fusion.2), channel_id=1, source_target_pairs={{0,8},{4,12},{8,0},{12,4},{1,9},{5,13},{9,1},{13,5},{2,10},{6,14},... | collective-permute-start | bytes 1327112 | tf_op jit(solution)/shard_map/ppermute | solution.py:28
  330.8 19.9 %collective-permute-start.58 = (bf16[576,768]{1,0:T(8,128)(2,1)S(1)}, bf16[576,768]{1,0:T(8,128)(2,1)}, u32[]{:S(2)}, u32[]{:S(2)}) collective-permute-start(bf16[576,768]{1,0:T(8,128)(2,1)S(1)} %join_halves.6.refs_0_), channel_id=1, source_target_pairs={{0,2},{1,3},{2,0},{3,1},{4,6},{5,7},{6,4},{7,5},{8,10},{9,11},{10,... | collective-permute-start | bytes 2654216 | tf_op jit(solution)/shard_map/ppermute | solution.py:28
  351.4 20.9 %collective-permute-start.57 = (bf16[288,768]{1,0:T(8,128)(2,1)S(1)}, bf16[288,768]{1,0:T(8,128)(2,1)S(1)}, u32[]{:S(2)}, u32[]{:S(2)}) collective-permute-start(bf16[288,768]{1,0:T(8,128)(2,1)S(1)} %add_convert_fusion.a_ref), channel_id=1, source_target_pairs={{0,4},{4,0},{8,12},{12,8},{1,5},{5,1},{9,13},{13,9},{2,6},{6,2},{1... | collective-permute-start | bytes 1327112 | tf_op jit(solution)/shard_map/ppermute | solution.py:28
  353.4 26.1 %collective-permute-start.56 = (bf16[192,896]{1,0:T(8,128)(2,1)S(1)}, bf16[192,896]{1,0:T(8,128)(2,1)S(1)}, u32[]{:S(2)}, u32[]{:S(2)}) collective-permute-start(bf16[192,896]{1,0:T(8,128)(2,1)S(1)} %copy-done.76), channel_id=1, source_target_pairs={{0,8},{4,12},{8,0},{12,4},{1,9},{5,13},{9,1},{13,5},{2,10},{6,14},... | collective-permute-start | bytes 1032200 | tf_op jit(solution)/shard_map/ppermute | solution.py:28
  354.9 32.7 %collective-permute-start.63 = (bf16[4,432]{1,0:T(4,128)(2,1)S(1)}, bf16[4,432]{1,0:T(4,128)(2,1)S(1)}, u32[]{:S(2)}, u32[]{:S(2)}) collective-permute-start(bf16[4,432]{1,0:T(4,128)(2,1)S(1)} %select_reduce_fusion), channel_id=1, source_target_pairs={{0,16},{16,0},{1,17},{17,1},{2,18},{18,2},{3,19},{19,3},{4,20},{20... | collective-permute-start | bytes 10376 | tf_op jit(solution)/shard_map/ppermute | solution.py:28
  356.5 23.1 %collective-permute-start.55 = (f32[1,4752]{1,0:T(1,128)S(1)}, f32[1,4752]{1,0:T(1,128)S(1)}, u32[]{:S(2)}, u32[]{:S(2)}) collective-permute-start(f32[1,4752]{1,0:T(1,128)S(1)} %reshape.124), channel_id=1, source_target_pairs={{0,4},{4,0},{8,12},{12,8},{1,5},{5,1},{9,13},{13,9},{2,6},{6,2},{1... | collective-permute-start | bytes 57032 | tf_op jit(solution)/shard_map/ppermute | solution.py:28
  356.8 29.7 %collective-permute-start.50 = (bf16[192,896]{1,0:T(8,128)(2,1)}, bf16[192,896]{1,0:T(8,128)(2,1)S(1)}, u32[]{:S(2)}, u32[]{:S(2)}) collective-permute-start(bf16[192,896]{1,0:T(8,128)(2,1)} %add_convert_fusion.8), channel_id=1, source_target_pairs={{0,8},{4,12},{8,0},{12,4},{1,9},{5,13},{9,1},{13,5},{2,10},{6,14},... | collective-permute-start | bytes 1032200 | tf_op jit(solution)/shard_map/ppermute | solution.py:28
  373.0 22.5 %collective-permute-start.66 = (bf16[576,768]{1,0:T(8,128)(2,1)S(1)}, bf16[576,768]{1,0:T(8,128)(2,1)}, u32[]{:S(2)}, u32[]{:S(2)}) collective-permute-start(bf16[576,768]{1,0:T(8,128)(2,1)S(1)} %join_halves.7.refs_0_), channel_id=1, source_target_pairs={{0,2},{1,3},{2,0},{3,1},{4,6},{5,7},{6,4},{7,5},{8,10},{9,11},{10,... | collective-permute-start | bytes 2654216 | tf_op jit(solution)/shard_map/ppermute | solution.py:28
  401.0 28.0 %all-to-all-start.3 = ((bf16[4,64,1152]{2,1,0:T(8,128)(2,1)}), bf16[4,64,1152]{2,1,0:T(8,128)(2,1)}, u32[]{:S(2)}, u32[]{:S(2)}) async-start(bf16[4,64,1152]{2,1,0:T(8,128)(2,1)} %bitcast.71), calls=%async_computation.3 | async-start | bytes 1179648 | tf_op jit(solution)/shard_map/all_to_all | solution.py:1041
  (130 other events, 1001.4 us)

commit v5 on v4

--- a/solution.py
+++ b/solution.py
@@ -52,7 +52,7 @@
     return jax.ShapeDtypeStruct(shape, dtype)
 
 
-def kernel(body, name, scalars, args, grid, in_specs, out_specs, out_shape, scratch=(), megabytes=32):
+def kernel(body, name, scalars, args, grid, in_specs, out_specs, out_shape, scratch=(), megabytes=24):
     none = scalars is None
     return pl.pallas_call(
         functools.partial(body, None) if none else body,
@@ -347,7 +347,7 @@
         [block, whole(cos.shape), whole(cos.shape), whole(cos.shape), whole(gain.shape)],
         [pl.BlockSpec((tokens, LANES), lambda h, o=None: (0, h)), block],
         [shape_of((tokens, heads * LANES), low), shape_of((tokens, columns), low)],
-        megabytes=32,
+        megabytes=24,
     )
 
 
@@ -432,7 +432,7 @@
             pltpu.VMEM((LANES, tokens), wide),
             pltpu.VMEM((tokens, LANES), low),
         ],
-        megabytes=32,
+        megabytes=24,
     )
 
 
@@ -465,7 +465,7 @@
             pl.BlockSpec((rows, columns), lambda s, o=None: (jnp.maximum(s - half, 0), 0)),
         ],
         [shape_of((half * rows, columns), low), shape_of((half * rows, columns), wide)],
-        megabytes=36,
+        megabytes=24,
     )
 
 
@@ -646,7 +646,7 @@
             shape_of((half * rows, width), low),
             shape_of((half * rows, width), wide),
         ],
-        megabytes=48,
+        megabytes=36,
     )
 
 
@@ -704,7 +704,7 @@
         [out, out],
         [shape_of((width // 2, columns), low)] * 2,
         scratch=[pltpu.VMEM((width, tokens), low), pltpu.VMEM((width, chunk), wide)],
-        megabytes=36,
+        megabytes=24,
     )
 
 
@@ -770,7 +770,7 @@
             pltpu.VMEM((width, padded), wide),
             pltpu.VMEM((mixed_t.shape[0], gbs[0].shape[1]), wide),
         ],
-        megabytes=50,
+        megabytes=36,
     )
 
 

time: 448 us -> 431 us (0.962)
  local copies, waits for them, and re-layouts: 49.7 us -> 37.7 us
  Pallas kernels: 157 us -> 148 us
  waiting for transfers between devices: 123 us -> 131 us
    unnamed x162 -> x136, local copies, waits for them, and re-layouts: 47 us -> 35.1 us
    pallas_call x41, Pallas kernels: 146 us -> 138 us  [kernel(): pl.pallas_call(functools.partial(body, None) if none else body, grid_spec...]
    ppermute x77, waiting for transfers between devices: 123 us -> 131 us  [swap(): return lax.ppermute(value, axis, [(a, a ^ bit) for a in range(size)])]
    ppermute x77, starting transfers between devices: 69.1 us -> 64.1 us  [swap(): return lax.ppermute(value, axis, [(a, a ^ bit) for a in range(size)])]
  transfers between devices with their start and end apart: 81 -> 81, of which waited for: 34 -> 33; matrix products, arithmetic and copies ran while one was open for 5% -> 5% of each run, Pallas kernels for 27% -> 27%
where the time goes in v5:
time: 431 us; the launch traced here: 425 us
  Pallas kernels  148 us (34%)
  waiting for transfers between devices  131 us (30%)
  starting transfers between devices  84.2 us (20%)
  local copies, waits for them, and re-layouts  37.7 us (9%)
  other arithmetic  16 us (4%)
  between operations  4.71 us (1%)
    pallas_call x41, Pallas kernels, kernel(): pl.pallas_call(functools.partial(body, None) if none else body, grid_spec...  138 us
    ppermute x77, waiting for transfers between devices, swap(): return lax.ppermute(value, axis, [(a, a ^ bit) for a in range(size)])  131 us
    ppermute x77, starting transfers between devices, swap(): return lax.ppermute(value, axis, [(a, a ^ bit) for a in range(size)])  64.1 us
    unnamed x136, local copies, waits for them, and re-layouts  35.1 us
    all_to_all x4, starting transfers between devices, over_rows(): return lax.all_to_all(v, 'row', split_axis=0, concat_axis=0, tiled=True)  20.2 us
  transfers between devices with their start and end apart: 81, of which 33 were waited for; matrix products, arithmetic and copies ran while one was open for 5% of the time, Pallas kernels for 27%

profile of v5, /device:TPU:0, one launch (start us, length us, event | category | flops | bytes accessed | tf_op | source)
XLA Modules:
  0.0 425.0 jit_solution(3375787576676297606)
XLA Ops:
  6.7 4.9 %all-to-all-start = ((bf16[4,64,1152]{2,1,0:T(8,128)(2,1)}), bf16[4,64,1152]{2,1,0:T(8,128)(2,1)S(1)}, u32[]{:S(2)}, u32[]{:S(2)}) async-start(bf16[4,64,1152]{2,1,0:T(8,128)(2,1)} %bitcast.30), calls=%async_computation | async-start | bytes 1179648 | tf_op jit(solution)/shard_map/all_to_all | solution.py:1041
  12.0 3.9 collective-permute-start.2
  49.6 5.1 %collective-permute-done.7.refs_1_ = bf16[256,1152]{1,0:T(8,128)(2,1)} collective-permute-done((bf16[256,1152]{1,0:T(8,128)(2,1)S(1)}, bf16[256,1152]{1,0:T(8,128)(2,1)}, u32[]{:S(2)}, u32[]{:S(2)}) %collective-permute-start.7) | collective-permute-done | bytes 589856 | tf_op jit(solution)/shard_map/ppermute | solution.py:28
  57.5 5.5 %all-to-all-start.1 = ((bf16[4,64,1152]{2,1,0:T(8,128)(2,1)}), bf16[4,64,1152]{2,1,0:T(8,128)(2,1)S(1)}, u32[]{:S(2)}, u32[]{:S(2)}) async-start(bf16[4,64,1152]{2,1,0:T(8,128)(2,1)} %bitcast.76), calls=%async_computation.1 | async-start | bytes 1179648 | tf_op jit(solution)/shard_map/all_to_all | solution.py:1041
  68.4 6.7 %project_qkv.1 = (bf16[1024,1152]{1,0:T(8,128)(2,1)S(1)}, f32[1024,1536]{1,0:T(8,128)S(1)}) custom-call(bf16[256,1152]{1,0:T(8,128)(2,1)S(1)} %bitcast.69, bf16[256,1152]{1,0:T(8,128)(2,1)} %collective-permute-done.7.refs_1_, bf16[256,1152]{1,0:T(8,128)(2,1)S(1)} %copy-done.51, bf16[256,1152]{1,0:T(8,128)(2,1)S(1)} %collective-permute-done.12.refs_3_, ...), custom_call_target="tpu_custom_call" | custom-call | flops 1 | bytes 1 | tf_op jit(solution)/shard_map/project_qkv/pallas_call | solution.py:57
  85.1 10.9 %attn_fwd.1 = (bf16[1024,512]{1,0:T(8,128)(2,1)S(1)}, bf16[1024,1536]{1,0:T(8,128)(2,1)S(1)}) custom-call(f32[1024,1536]{1,0:T(8,128)S(1)} %copy-done.5, f32[1024,128]{1,0:T(8,128)S(1)} %copy-done.25, f32[1024,128]{1,0:T(8,128)S(1)} %copy-done.28, f32[1024,128]{1,0:T(8,128)S(1)} %copy-done.31, f32[2,128]{1,0:T(2,128)S(1)} %pad.4.gain_ref.refs_11_), custom_call_target="tpu_custom_call" | custom-call | flops 1 | bytes 1 | tf_op jit(solution)/shard_map/attn_fwd/pallas_call | solution.py:57
  111.8 5.1 %collective-permute-done.17.y_ref = bf16[256,1152]{1,0:T(8,128)(2,1)S(1)} collective-permute-done((bf16[256,1152]{1,0:T(8,128)(2,1)S(1)}, bf16[256,1152]{1,0:T(8,128)(2,1)S(1)}, u32[]{:S(2)}, u32[]{:S(2)}) %collective-permute-start.17) | collective-permute-done | bytes 589856 | tf_op jit(solution)/shard_map/ppermute | solution.py:28
  120.4 13.8 %collective-permute-done.19.refs_1_ = bf16[256,1152]{1,0:T(8,128)(2,1)S(1)} collective-permute-done((bf16[256,1152]{1,0:T(8,128)(2,1)S(1)}, bf16[256,1152]{1,0:T(8,128)(2,1)S(1)}, u32[]{:S(2)}, u32[]{:S(2)}) %collective-permute-start.19) | collective-permute-done | bytes 589856 | tf_op jit(solution)/shard_map/ppermute | solution.py:28
  136.2 16.1 %feed_forward.1 = (bf16[1024,768]{1,0:T(8,128)(2,1)S(1)}, bf16[1024,1536]{1,0:T(8,128)(2,1)S(1)}, bf16[1024,1152]{1,0:T(8,128)(2,1)S(1)}, bf16[512,1152]{1,0:T(8,128)(2,1)S(1)}, f32[512,1152]{1,0:T(8,128)S(1)}) custom-call(s32[1]{0:T(128)} %dynamic_slice.40.live, bf16[256,1152]{1,0:T(8,128)(2,1)S(1)} %get-tuple-element.237.refs_0_, ...), custom_call_target="tpu_custom_call" | custom-call | flops 1 | bytes 1 | tf_op jit(solution)/shard_map/feed_forward/pallas_call | solution.py:57
  156.9 4.1 grad_part.3
  162.6 4.9 %grad_part.4 = (bf16[576,768]{1,0:T(8,128)(2,1)}, bf16[576,768]{1,0:T(8,128)(2,1)S(1)}) custom-call(s32[1]{0:T(128)} %bitcast.at, bf16[256,1152]{1,0:T(8,128)(2,1)S(1)} %get-tuple-element.237.refs_0_, bf16[256,1152]{1,0:T(8,128)(2,1)S(1)} %collective-permute-done.19.refs_1_, bf16[256,1152]{1,0:T(8,128)(2,1)S(1)} %collective-permute-done.20.refs_2_, ...), custom_call_target="tpu_custom_call" | custom-call | flops 1 | bytes 1 | tf_op jit(solution)/shard_map/grad_part/pallas_call | solution.py:57
  167.4 4.1 grad_part.5
  178.0 4.5 %collective-permute-done.27.b_ref = bf16[384,1152]{1,0:T(8,128)(2,1)S(1)} collective-permute-done((bf16[384,1152]{1,0:T(8,128)(2,1)S(1)}, bf16[384,1152]{1,0:T(8,128)(2,1)S(1)}, u32[]{:S(2)}, u32[]{:S(2)}) %collective-permute-start.27) | collective-permute-done | bytes 884768 | tf_op jit(solution)/shard_map/ppermute | solution.py:28
  183.5 6.1 %collective-permute-done.25.refs_1_.refs_7_ = bf16[256,1152]{1,0:T(8,128)(2,1)S(1)} collective-permute-done((bf16[256,1152]{1,0:T(8,128)(2,1)S(1)}, bf16[256,1152]{1,0:T(8,128)(2,1)S(1)}, u32[]{:S(2)}, u32[]{:S(2)}) %collective-permute-start.25) | collective-permute-done | bytes 589856 | tf_op jit(solution)/shard_map/ppermute | solution.py:28
  192.9 20.5 %attn_bwd.1 = (bf16[1024,1536]{1,0:T(8,128)(2,1)S(1)}, f32[2,128]{1,0:T(2,128)S(1)}) custom-call(bf16[256,1152]{1,0:T(8,128)(2,1)S(1)} %get-tuple-element.257.refs_0_.refs_6_, bf16[256,1152]{1,0:T(8,128)(2,1)S(1)} %collective-permute-done.25.refs_1_.refs_7_, bf16[256,1152]{1,0:T(8,128)(2,1)S(1)} %collective-permute-done.26.refs_2_.refs_8_, ...), custom_call_target="tpu_custom_call" | custom-call | flops 1 | bytes 1 | tf_op jit(solution)/shard_map/attn_bwd/pallas_call | solution.py:57
  215.5 5.4 %project.5 = (bf16[512,1152]{1,0:T(8,128)(2,1)S(1)}, f32[512,1152]{1,0:T(8,128)S(1)}) custom-call(bf16[1024,1536]{1,0:T(8,128)(2,1)S(1)} %get-tuple-element.281.x_ref.refs_2_.refs_3_.refs_4_.refs_5_, bf16[1152,1536]{1,0:T(8,128)(2,1)S(1)} %copy-done.3), custom_call_target="tpu_custom_call" | custom-call | flops 1 | bytes 1 | tf_op jit(solution)/shard_map/project/pallas_call | solution.py:57
  226.6 9.0 %grad_last.1 = (bf16[384,896]{1,0:T(8,128)(2,1)S(1)}, bf16[384,896]{1,0:T(8,128)(2,1)S(1)}, bf16[384,896]{1,0:T(8,128)(2,1)S(1)}, bf16[384,896]{1,0:T(8,128)(2,1)S(1)}) custom-call(s32[1]{0:T(128)} %bitcast.at, bf16[1152,1024]{1,0:T(8,128)(2,1)S(1)} %copy-done.15, bf16[512,1024]{1,0:T(8,128)(2,1)S(1)} %copy-done.41, ...), custom_call_target="tpu_custom_call" | custom-call | flops 1 | bytes 1 | tf_op jit(solution)/shard_map/grad_last/pallas_call | solution.py:57
  236.9 6.5 %collective-permute-done.32.b_ref = bf16[576,768]{1,0:T(8,128)(2,1)S(1)} collective-permute-done((bf16[576,768]{1,0:T(8,128)(2,1)S(1)}, bf16[576,768]{1,0:T(8,128)(2,1)S(1)}, u32[]{:S(2)}, u32[]{:S(2)}) %collective-permute-start.32) | collective-permute-done | bytes 884768 | tf_op jit(solution)/shard_map/ppermute | solution.py:28
  254.8 7.0 %collective-permute-done.36.y_ref = bf16[256,1152]{1,0:T(8,128)(2,1)S(1)} collective-permute-done((bf16[256,1152]{1,0:T(8,128)(2,1)S(1)}, bf16[256,1152]{1,0:T(8,128)(2,1)S(1)}, u32[]{:S(2)}, u32[]{:S(2)}) %collective-permute-start.36) | collective-permute-done | bytes 589856 | tf_op jit(solution)/shard_map/ppermute | solution.py:28
  267.8 4.6 %collective-permute-done.43.b_ref = bf16[384,896]{1,0:T(8,128)(2,1)S(1)} collective-permute-done((bf16[384,896]{1,0:T(8,128)(2,1)S(1)}, bf16[384,896]{1,0:T(8,128)(2,1)S(1)}, u32[]{:S(2)}, u32[]{:S(2)}) %collective-permute-start.43) | collective-permute-done | bytes 688160 | tf_op jit(solution)/shard_map/ppermute | solution.py:28
  287.0 8.7 %collective-permute-done.47.refs_1_ = bf16[384,1152]{1,0:T(8,128)(2,1)} collective-permute-done((bf16[384,1152]{1,0:T(8,128)(2,1)S(1)}, bf16[384,1152]{1,0:T(8,128)(2,1)}, u32[]{:S(2)}, u32[]{:S(2)}) %collective-permute-start.47) | collective-permute-done | bytes 884768 | tf_op jit(solution)/shard_map/ppermute | solution.py:28
  297.0 5.6 %collective-permute-done.44.b_ref = bf16[288,768]{1,0:T(8,128)(2,1)S(1)} collective-permute-done((bf16[288,768]{1,0:T(8,128)(2,1)S(1)}, bf16[288,768]{1,0:T(8,128)(2,1)S(1)}, u32[]{:S(2)}, u32[]{:S(2)}) %collective-permute-start.44) | collective-permute-done | bytes 442400 | tf_op jit(solution)/shard_map/ppermute | solution.py:28
  317.6 5.3 %place_rows.1 = f32[1536,1152]{1,0:T(8,128)} custom-call(s32[4]{0:T(128)S(1)} %pad_add_fusion.at, bf16[384,1152]{1,0:T(8,128)(2,1)S(1)} %join_halves.5.refs_0_, bf16[384,1152]{1,0:T(8,128)(2,1)} %collective-permute-done.47.refs_1_, bf16[384,1152]{1,0:T(8,128)(2,1)} %collective-permute-done.48.refs_2_, bf16[384,1152]{1,0:T(8,128)(2,1)} %collective-permute-done.49.refs_3_), custom_call_target="tpu_custom_call" | custom-call | flops 1 | bytes 1 | tf_op jit(solution)/shard_map/place_rows/pallas_call | solution.py:57
  322.9 8.2 %collective-permute-done.46 = bf16[288,768]{1,0:T(8,128)(2,1)} collective-permute-done((bf16[288,768]{1,0:T(8,128)(2,1)}, bf16[288,768]{1,0:T(8,128)(2,1)}, u32[]{:S(2)}, u32[]{:S(2)}) %collective-permute-start.46) | collective-permute-done | bytes 442400 | tf_op jit(solution)/shard_map/ppermute | solution.py:28
  342.7 5.2 %place_first.1.refs_4_ = f32[576,6144]{1,0:T(8,128)} custom-call(s32[4]{0:T(128)S(1)} %pad_add_fusion.at, bf16[576,768]{1,0:T(8,128)(2,1)S(1)} %join_halves.6.refs_0_, bf16[576,768]{1,0:T(8,128)(2,1)} %collective-permute-done.58.refs_1_, bf16[576,768]{1,0:T(8,128)(2,1)S(1)} %collective-permute-done.59.refs_2_, ...), custom_call_target="tpu_custom_call" | custom-call | flops 1 | bytes 1 | tf_op jit(solution)/shard_map/place_first/pallas_call | solution.py:57
  348.0 9.3 %collective-permute-done.57.b_ref = bf16[288,768]{1,0:T(8,128)(2,1)S(1)} collective-permute-done((bf16[288,768]{1,0:T(8,128)(2,1)S(1)}, bf16[288,768]{1,0:T(8,128)(2,1)S(1)}, u32[]{:S(2)}, u32[]{:S(2)}) %collective-permute-start.57) | collective-permute-done | bytes 442400 | tf_op jit(solution)/shard_map/ppermute | solution.py:28
  358.4 5.8 %collective-permute-done.56 = bf16[192,896]{1,0:T(8,128)(2,1)S(1)} collective-permute-done((bf16[192,896]{1,0:T(8,128)(2,1)S(1)}, bf16[192,896]{1,0:T(8,128)(2,1)S(1)}, u32[]{:S(2)}, u32[]{:S(2)}) %collective-permute-start.56) | collective-permute-done | bytes 344096 | tf_op jit(solution)/shard_map/ppermute | solution.py:28
  364.4 7.1 %collective-permute-done.50 = bf16[192,896]{1,0:T(8,128)(2,1)S(1)} collective-permute-done((bf16[192,896]{1,0:T(8,128)(2,1)}, bf16[192,896]{1,0:T(8,128)(2,1)S(1)}, u32[]{:S(2)}, u32[]{:S(2)}) %collective-permute-start.50) | collective-permute-done | bytes 344096 | tf_op jit(solution)/shard_map/ppermute | solution.py:28
  382.8 5.9 %all-to-all-start.3 = ((bf16[4,64,1152]{2,1,0:T(8,128)(2,1)}), bf16[4,64,1152]{2,1,0:T(8,128)(2,1)}, u32[]{:S(2)}, u32[]{:S(2)}) async-start(bf16[4,64,1152]{2,1,0:T(8,128)(2,1)} %bitcast.73), calls=%async_computation.3 | async-start | bytes 1179648 | tf_op jit(solution)/shard_map/all_to_all | solution.py:1041
  392.5 5.8 %place_second.1 = f32[576,6144]{1,0:T(8,128)} custom-call(s32[4]{0:T(128)S(1)} %pad_add_fusion.at, bf16[576,768]{1,0:T(8,128)(2,1)S(1)} %join_halves.7.refs_0_, bf16[576,768]{1,0:T(8,128)(2,1)} %collective-permute-done.66.refs_1_, bf16[576,768]{1,0:T(8,128)(2,1)} %collective-permute-done.68.refs_2_, ...), custom_call_target="tpu_custom_call", output_to_operand_aliasing={{}: (5, {})} | custom-call | flops 1 | bytes 1 | tf_op jit(solution)/shard_map/place_second/pallas_call | solution.py:870
  405.2 6.7 %place_top.1.refs_8_ = f32[576,3456]{1,0:T(8,128)} custom-call(s32[4]{0:T(128)S(1)} %pad_add_fusion.at, bf16[384,896]{1,0:T(8,128)(2,1)S(1)} %join_halves.8.refs_0_, bf16[384,896]{1,0:T(8,128)(2,1)} %collective-permute-done.64.refs_1_, bf16[384,896]{1,0:T(8,128)(2,1)} %collective-permute-done.71.refs_2_, bf16[384,896]{1,0:T(8,128)(2,1)} %collective-permute-done.73.refs_3_), custom_call_target="tpu_custom_call" | custom-call | flops 1 | bytes 1 | tf_op jit(solution)/shard_map/place_top/pallas_call | solution.py:57
  420.0 4.6 %place_last.1 = (f32[576,3456]{1,0:T(8,128)}, f32[576,1152]{1,0:T(8,128)}) custom-call(s32[4]{0:T(128)S(1)} %pad_add_fusion.at, bf16[384,896]{1,0:T(8,128)(2,1)S(1)} %join_halves.9.refs_0_.refs_4_, bf16[384,896]{1,0:T(8,128)(2,1)S(1)} %collective-permute-done.74.refs_1_.refs_5_, ...), custom_call_target="tpu_custom_call", output_to_operand_aliasing={{0}: (9, {})} | custom-call | flops 1 | bytes 1 | tf_op jit(solution)/shard_map/place_last/pallas_call | solution.py:973
  (361 shorter events, 193.6 us)
Async XLA Ops:
  3.7 41.3 %collective-permute-start.8 = (bf16[576,864]{1,0:T(8,128)(2,1)S(1)}, bf16[576,864]{1,0:T(8,128)(2,1)}, u32[]{:S(2)}, u32[]{:S(2)}) collective-permute-start(bf16[576,864]{1,0:T(8,128)(2,1)S(1)} %cut_qkv.1.mine_ref), channel_id=1, source_target_pairs={{0,16},{16,0},{1,17},{17,1},{2,18},{18,2},{3,19},{19,3},{4,20},{20... | collective-permute-start | bytes 2985992 | tf_op jit(solution)/shard_map/ppermute | solution.py:28
  6.7 32.1 %all-to-all-start = ((bf16[4,64,1152]{2,1,0:T(8,128)(2,1)}), bf16[4,64,1152]{2,1,0:T(8,128)(2,1)S(1)}, u32[]{:S(2)}, u32[]{:S(2)}) async-start(bf16[4,64,1152]{2,1,0:T(8,128)(2,1)} %bitcast.30), calls=%async_computation | async-start | bytes 1179648 | tf_op jit(solution)/shard_map/all_to_all | solution.py:1041
  12.0 23.0 %collective-permute-start.2 = (f32[1,432]{1,0:T(1,128)S(1)}, f32[1,432]{1,0:T(1,128)S(1)}, u32[]{:S(2)}, u32[]{:S(2)}) collective-permute-start(f32[1,432]{1,0:T(1,128)S(1)} %get-tuple-element.364), channel_id=1, source_target_pairs={{0,12},{4,8},{8,4},{12,0},{1,13},{5,9},{9,5},{13,1},{2,14},{6,10},... | collective-permute-start | bytes 5192 | tf_op jit(solution)/shard_map/ppermute | solution.py:28
  25.4 30.4 %collective-permute-start.6 = (bf16[384,1152]{1,0:T(8,128)(2,1)}, bf16[384,1152]{1,0:T(8,128)(2,1)}, u32[]{:S(2)}, u32[]{:S(2)}) collective-permute-start(bf16[384,1152]{1,0:T(8,128)(2,1)} %get-tuple-element.191.c_ref), channel_id=1, source_target_pairs={{0,16},{16,0},{1,17},{17,1},{2,18},{18,2},{3,19},{19,3},{4,20},{20... | collective-permute-start | bytes 2654216 | tf_op jit(solution)/shard_map/ppermute | solution.py:28
  55.7 40.3 %collective-permute-start.15 = (bf16[576,1536]{1,0:T(8,128)(2,1)}, bf16[576,1536]{1,0:T(8,128)(2,1)}, u32[]{:S(2)}, u32[]{:S(2)}) collective-permute-start(bf16[576,1536]{1,0:T(8,128)(2,1)} %get-tuple-element.219.a_ref), channel_id=1, source_target_pairs={{0,16},{16,0},{1,17},{17,1},{2,18},{18,2},{3,19},{19,3},{4,20},{20... | collective-permute-start | bytes 5308424 | tf_op jit(solution)/shard_map/ppermute | solution.py:28
  57.5 21.7 %all-to-all-start.1 = ((bf16[4,64,1152]{2,1,0:T(8,128)(2,1)}), bf16[4,64,1152]{2,1,0:T(8,128)(2,1)S(1)}, u32[]{:S(2)}, u32[]{:S(2)}) async-start(bf16[4,64,1152]{2,1,0:T(8,128)(2,1)} %bitcast.76), calls=%async_computation.1 | async-start | bytes 1179648 | tf_op jit(solution)/shard_map/all_to_all | solution.py:1041
  161.0 21.5 %collective-permute-start.27 = (bf16[384,1152]{1,0:T(8,128)(2,1)S(1)}, bf16[384,1152]{1,0:T(8,128)(2,1)S(1)}, u32[]{:S(2)}, u32[]{:S(2)}) collective-permute-start(bf16[384,1152]{1,0:T(8,128)(2,1)S(1)} %get-tuple-element.249), channel_id=1, source_target_pairs={{0,16},{16,0},{1,17},{17,1},{2,18},{18,2},{3,19},{19,3},{4,20},{20... | collective-permute-start | bytes 2654216 | tf_op jit(solution)/shard_map/ppermute | solution.py:28
  189.7 23.8 %collective-permute-start.29 = (bf16[192,1152]{1,0:T(8,128)(2,1)S(1)}, bf16[192,1152]{1,0:T(8,128)(2,1)S(1)}, u32[]{:S(2)}, u32[]{:S(2)}) collective-permute-start(bf16[192,1152]{1,0:T(8,128)(2,1)S(1)} %get-tuple-element.264), channel_id=1, source_target_pairs={{0,4},{4,0},{8,12},{12,8},{1,5},{5,1},{9,13},{13,9},{2,6},{6,2},{1... | collective-permute-start | bytes 1327112 | tf_op jit(solution)/shard_map/ppermute | solution.py:28
  191.3 22.2 %collective-permute-start.33 = (bf16[576,768]{1,0:T(8,128)(2,1)}, bf16[576,768]{1,0:T(8,128)(2,1)S(1)}, u32[]{:S(2)}, u32[]{:S(2)}) collective-permute-start(bf16[576,768]{1,0:T(8,128)(2,1)} %get-tuple-element.251), channel_id=1, source_target_pairs={{0,16},{16,0},{1,17},{17,1},{2,18},{18,2},{3,19},{19,3},{4,20},{20... | collective-permute-start | bytes 2654216 | tf_op jit(solution)/shard_map/ppermute | solution.py:28
  220.9 22.5 %collective-permute-start.32 = (bf16[576,768]{1,0:T(8,128)(2,1)S(1)}, bf16[576,768]{1,0:T(8,128)(2,1)S(1)}, u32[]{:S(2)}, u32[]{:S(2)}) collective-permute-start(bf16[576,768]{1,0:T(8,128)(2,1)S(1)} %copy-done.59), channel_id=1, source_target_pairs={{0,16},{16,0},{1,17},{17,1},{2,18},{18,2},{3,19},{19,3},{4,20},{20... | collective-permute-start | bytes 2654216 | tf_op jit(solution)/shard_map/ppermute | solution.py:28
  222.4 25.2 %collective-permute-start.31 = (bf16[192,1152]{1,0:T(8,128)(2,1)S(1)}, bf16[192,1152]{1,0:T(8,128)(2,1)}, u32[]{:S(2)}, u32[]{:S(2)}) collective-permute-start(bf16[192,1152]{1,0:T(8,128)(2,1)S(1)} %add_convert_fusion.5), channel_id=1, source_target_pairs={{0,8},{4,12},{8,0},{12,4},{1,9},{5,13},{9,1},{13,5},{2,10},{6,14},... | collective-permute-start | bytes 1327112 | tf_op jit(solution)/shard_map/ppermute | solution.py:28
  225.0 24.4 %collective-permute-start.28 = (bf16[256,1152]{1,0:T(8,128)(2,1)}, bf16[256,1152]{1,0:T(8,128)(2,1)S(1)}, u32[]{:S(2)}, u32[]{:S(2)}) collective-permute-start(bf16[256,1152]{1,0:T(8,128)(2,1)} %add_second.6), channel_id=1, source_target_pairs={{0,2},{1,3},{2,0},{3,1},{4,6},{5,7},{6,4},{7,5},{8,10},{9,11},{10,... | collective-permute-start | bytes 1769480 | tf_op jit(solution)/shard_map/ppermute | solution.py:28
  225.8 25.8 %collective-permute-start.37 = (bf16[288,768]{1,0:T(8,128)(2,1)S(1)}, bf16[288,768]{1,0:T(8,128)(2,1)}, u32[]{:S(2)}, u32[]{:S(2)}) collective-permute-start(bf16[288,768]{1,0:T(8,128)(2,1)S(1)} %get-tuple-element.276), channel_id=1, source_target_pairs={{0,4},{4,0},{8,12},{12,8},{1,5},{5,1},{9,13},{13,9},{2,6},{6,2},{1... | collective-permute-start | bytes 1327112 | tf_op jit(solution)/shard_map/ppermute | solution.py:28
  235.6 30.3 %collective-permute-start.35 = (bf16[384,896]{1,0:T(8,128)(2,1)S(1)}, bf16[384,896]{1,0:T(8,128)(2,1)S(1)}, u32[]{:S(2)}, u32[]{:S(2)}) collective-permute-start(bf16[384,896]{1,0:T(8,128)(2,1)S(1)} %get-tuple-element.282), channel_id=1, source_target_pairs={{0,16},{16,0},{1,17},{17,1},{2,18},{18,2},{3,19},{19,3},{4,20},{20... | collective-permute-start | bytes 2064392 | tf_op jit(solution)/shard_map/ppermute | solution.py:28
  243.4 29.0 %collective-permute-start.43 = (bf16[384,896]{1,0:T(8,128)(2,1)S(1)}, bf16[384,896]{1,0:T(8,128)(2,1)S(1)}, u32[]{:S(2)}, u32[]{:S(2)}) collective-permute-start(bf16[384,896]{1,0:T(8,128)(2,1)S(1)} %get-tuple-element.302), channel_id=1, source_target_pairs={{0,16},{16,0},{1,17},{17,1},{2,18},{18,2},{3,19},{19,3},{4,20},{20... | collective-permute-start | bytes 2064392 | tf_op jit(solution)/shard_map/ppermute | solution.py:28
  249.5 23.9 %collective-permute-start.41 = (bf16[192,1152]{1,0:T(8,128)(2,1)S(1)}, bf16[192,1152]{1,0:T(8,128)(2,1)S(1)}, u32[]{:S(2)}, u32[]{:S(2)}) collective-permute-start(bf16[192,1152]{1,0:T(8,128)(2,1)S(1)} %add_convert_fusion.4.a_ref), channel_id=1, source_target_pairs={{0,4},{4,0},{8,12},{12,8},{1,5},{5,1},{9,13},{13,9},{2,6},{6,2},{1... | collective-permute-start | bytes 1327112 | tf_op jit(solution)/shard_map/ppermute | solution.py:28
  251.6 28.2 %collective-permute-start.40 = (bf16[288,768]{1,0:T(8,128)(2,1)}, bf16[288,768]{1,0:T(8,128)(2,1)}, u32[]{:S(2)}, u32[]{:S(2)}) collective-permute-start(bf16[288,768]{1,0:T(8,128)(2,1)} %get-tuple-element.285), channel_id=1, source_target_pairs={{0,4},{4,0},{8,12},{12,8},{1,5},{5,1},{9,13},{13,9},{2,6},{6,2},{1... | collective-permute-start | bytes 1327112 | tf_op jit(solution)/shard_map/ppermute | solution.py:28
  261.9 21.0 %collective-permute-start.39 = (bf16[288,768]{1,0:T(8,128)(2,1)}, bf16[288,768]{1,0:T(8,128)(2,1)}, u32[]{:S(2)}, u32[]{:S(2)}) collective-permute-start(bf16[288,768]{1,0:T(8,128)(2,1)} %add_convert_fusion.3), channel_id=1, source_target_pairs={{0,8},{4,12},{8,0},{12,4},{1,9},{5,13},{9,1},{13,5},{2,10},{6,14},... | collective-permute-start | bytes 1327112 | tf_op jit(solution)/shard_map/ppermute | solution.py:28
  274.2 21.4 %collective-permute-start.47 = (bf16[384,1152]{1,0:T(8,128)(2,1)S(1)}, bf16[384,1152]{1,0:T(8,128)(2,1)}, u32[]{:S(2)}, u32[]{:S(2)}) collective-permute-start(bf16[384,1152]{1,0:T(8,128)(2,1)S(1)} %join_halves.5.refs_0_), channel_id=1, source_target_pairs={{0,2},{1,3},{2,0},{3,1},{4,6},{5,7},{6,4},{7,5},{8,10},{9,11},{10,... | collective-permute-start | bytes 2654216 | tf_op jit(solution)/shard_map/ppermute | solution.py:28
  275.9 38.3 %all-to-all-start.2 = ((bf16[4,64,1152]{2,1,0:T(8,128)(2,1)}), bf16[4,64,1152]{2,1,0:T(8,128)(2,1)S(1)}, u32[]{:S(2)}, u32[]{:S(2)}) async-start(bf16[4,64,1152]{2,1,0:T(8,128)(2,1)} %bitcast.74), calls=%async_computation.2 | async-start | bytes 1179648 | tf_op jit(solution)/shard_map/all_to_all | solution.py:1041
  285.8 24.3 %collective-permute-start.38 = (bf16[192,896]{1,0:T(8,128)(2,1)}, bf16[192,896]{1,0:T(8,128)(2,1)}, u32[]{:S(2)}, u32[]{:S(2)}) collective-permute-start(bf16[192,896]{1,0:T(8,128)(2,1)} %get-tuple-element.299), channel_id=1, source_target_pairs={{0,4},{4,0},{8,12},{12,8},{1,5},{5,1},{9,13},{13,9},{2,6},{6,2},{1... | collective-permute-start | bytes 1032200 | tf_op jit(solution)/shard_map/ppermute | solution.py:28
  295.6 21.3 %collective-permute-start.49 = (bf16[384,1152]{1,0:T(8,128)(2,1)}, bf16[384,1152]{1,0:T(8,128)(2,1)}, u32[]{:S(2)}, u32[]{:S(2)}) collective-permute-start(bf16[384,1152]{1,0:T(8,128)(2,1)} %collective-permute-done.47.refs_1_), channel_id=1, source_target_pairs={{0,1},{1,0},{2,3},{3,2},{4,5},{5,4},{6,7},{7,6},{8,9},{9,8},{10,11... | collective-permute-start | bytes 2654216 | tf_op jit(solution)/shard_map/ppermute | solution.py:28
  296.2 36.1 %collective-permute-start.45 = (bf16[192,896]{1,0:T(8,128)(2,1)}, bf16[192,896]{1,0:T(8,128)(2,1)}, u32[]{:S(2)}, u32[]{:S(2)}) collective-permute-start(bf16[192,896]{1,0:T(8,128)(2,1)} %copy-done.60), channel_id=1, source_target_pairs={{0,4},{4,0},{8,12},{12,8},{1,5},{5,1},{9,13},{13,9},{2,6},{6,2},{1... | collective-permute-start | bytes 1032200 | tf_op jit(solution)/shard_map/ppermute | solution.py:28
  310.0 21.1 %collective-permute-start.46 = (bf16[288,768]{1,0:T(8,128)(2,1)}, bf16[288,768]{1,0:T(8,128)(2,1)}, u32[]{:S(2)}, u32[]{:S(2)}) collective-permute-start(bf16[288,768]{1,0:T(8,128)(2,1)} %add_convert_fusion.2), channel_id=1, source_target_pairs={{0,8},{4,12},{8,0},{12,4},{1,9},{5,13},{9,1},{13,5},{2,10},{6,14},... | collective-permute-start | bytes 1327112 | tf_op jit(solution)/shard_map/ppermute | solution.py:28
  315.0 21.1 %collective-permute-start.58 = (bf16[576,768]{1,0:T(8,128)(2,1)S(1)}, bf16[576,768]{1,0:T(8,128)(2,1)}, u32[]{:S(2)}, u32[]{:S(2)}) collective-permute-start(bf16[576,768]{1,0:T(8,128)(2,1)S(1)} %join_halves.6.refs_0_), channel_id=1, source_target_pairs={{0,2},{1,3},{2,0},{3,1},{4,6},{5,7},{6,4},{7,5},{8,10},{9,11},{10,... | collective-permute-start | bytes 2654216 | tf_op jit(solution)/shard_map/ppermute | solution.py:28
  336.7 20.6 %collective-permute-start.57 = (bf16[288,768]{1,0:T(8,128)(2,1)S(1)}, bf16[288,768]{1,0:T(8,128)(2,1)S(1)}, u32[]{:S(2)}, u32[]{:S(2)}) collective-permute-start(bf16[288,768]{1,0:T(8,128)(2,1)S(1)} %add_convert_fusion.a_ref), channel_id=1, source_target_pairs={{0,4},{4,0},{8,12},{12,8},{1,5},{5,1},{9,13},{13,9},{2,6},{6,2},{1... | collective-permute-start | bytes 1327112 | tf_op jit(solution)/shard_map/ppermute | solution.py:28
  338.3 25.8 %collective-permute-start.56 = (bf16[192,896]{1,0:T(8,128)(2,1)S(1)}, bf16[192,896]{1,0:T(8,128)(2,1)S(1)}, u32[]{:S(2)}, u32[]{:S(2)}) collective-permute-start(bf16[192,896]{1,0:T(8,128)(2,1)S(1)} %copy-done.62), channel_id=1, source_target_pairs={{0,8},{4,12},{8,0},{12,4},{1,9},{5,13},{9,1},{13,5},{2,10},{6,14},... | collective-permute-start | bytes 1032200 | tf_op jit(solution)/shard_map/ppermute | solution.py:28
  339.9 32.7 %collective-permute-start.63 = (bf16[4,432]{1,0:T(4,128)(2,1)S(1)}, bf16[4,432]{1,0:T(4,128)(2,1)S(1)}, u32[]{:S(2)}, u32[]{:S(2)}) collective-permute-start(bf16[4,432]{1,0:T(4,128)(2,1)S(1)} %select_reduce_fusion), channel_id=1, source_target_pairs={{0,16},{16,0},{1,17},{17,1},{2,18},{18,2},{3,19},{19,3},{4,20},{20... | collective-permute-start | bytes 10376 | tf_op jit(solution)/shard_map/ppermute | solution.py:28
  341.2 23.1 %collective-permute-start.55 = (f32[1,4752]{1,0:T(1,128)S(1)}, f32[1,4752]{1,0:T(1,128)S(1)}, u32[]{:S(2)}, u32[]{:S(2)}) collective-permute-start(f32[1,4752]{1,0:T(1,128)S(1)} %reshape.124), channel_id=1, source_target_pairs={{0,4},{4,0},{8,12},{12,8},{1,5},{5,1},{9,13},{13,9},{2,6},{6,2},{1... | collective-permute-start | bytes 57032 | tf_op jit(solution)/shard_map/ppermute | solution.py:28
  341.3 30.2 %collective-permute-start.50 = (bf16[192,896]{1,0:T(8,128)(2,1)}, bf16[192,896]{1,0:T(8,128)(2,1)S(1)}, u32[]{:S(2)}, u32[]{:S(2)}) collective-permute-start(bf16[192,896]{1,0:T(8,128)(2,1)} %add_convert_fusion.8), channel_id=1, source_target_pairs={{0,8},{4,12},{8,0},{12,4},{1,9},{5,13},{9,1},{13,5},{2,10},{6,14},... | collective-permute-start | bytes 1032200 | tf_op jit(solution)/shard_map/ppermute | solution.py:28
  358.0 20.6 %collective-permute-start.66 = (bf16[576,768]{1,0:T(8,128)(2,1)S(1)}, bf16[576,768]{1,0:T(8,128)(2,1)}, u32[]{:S(2)}, u32[]{:S(2)}) collective-permute-start(bf16[576,768]{1,0:T(8,128)(2,1)S(1)} %join_halves.7.refs_0_), channel_id=1, source_target_pairs={{0,2},{1,3},{2,0},{3,1},{4,6},{5,7},{6,4},{7,5},{8,10},{9,11},{10,... | collective-permute-start | bytes 2654216 | tf_op jit(solution)/shard_map/ppermute | solution.py:28
  382.8 29.1 %all-to-all-start.3 = ((bf16[4,64,1152]{2,1,0:T(8,128)(2,1)}), bf16[4,64,1152]{2,1,0:T(8,128)(2,1)}, u32[]{:S(2)}, u32[]{:S(2)}) async-start(bf16[4,64,1152]{2,1,0:T(8,128)(2,1)} %bitcast.73), calls=%async_computation.3 | async-start | bytes 1179648 | tf_op jit(solution)/shard_map/all_to_all | solution.py:1041
  (117 other events, 948.1 us)
